TPU v7x, 128 devices: a whole 4x4x4 slice. The times are simulated.
128 devices in a mesh: rep: 16 (over y, x), exp: 8 (over z, core).
Axes of the slice: x: 4, y: 4, z: 4, core: 2. Of those that a mesh axis runs over, the one named last changes fastest.
Arguments:
- grad_parts: float32 [16, 128, 1024, 384], P('rep', 'exp'), may hold values from -6 to 6
- momentum: bfloat16 [128, 1024, 384], P('exp', 'rep'), may hold values from -24 to 24
Outputs:
- update: bfloat16 [128, 1024, 384], P('exp', 'rep')
All inputs are finite; a program needn't handle non-finite values.
Results may differ from a plain program's by a relative error of at most 0.0013.
Values may be sent and summed in bfloat16 or wider, within the bound.
No kernel may reach another device: no remote copies, remote signals or barrier semaphores. Data moves between devices by JAX's collectives and lax.ppermute only.
A program may use at most 128 MiB of HBM per device.

v0:
```python
import functools

import jax
import jax.numpy as jnp
import numpy as np
from jax import lax
from jax.experimental import pallas as pl
from jax.experimental.pallas import tpu as pltpu
from jax.sharding import PartitionSpec as P

D = 1024
FF = 384
NS_ITERS = 5
QUARTER = D // 4
STRIP = 32
BAND = 64
GAIN = 1.0 + 0.95
BLEND = 0.95 * 0.95 / GAIN

ORDERS = ((0, 2, 1, 3), (2, 1, 3, 0), (1, 3, 0, 2), (3, 0, 2, 1))
SHIFTS = (11, 11, 10, 9)


def bits_of(rep):
    y, x = divmod(rep, 4)
    return (int(x in (1, 2)), int(x >= 2), int(y in (1, 2)), int(y >= 2))


def rep_of(bits):
    x = 2 * bits[1] + (bits[0] ^ bits[1])
    y = 2 * bits[3] + (bits[2] ^ bits[3])
    return 4 * y + x


def partners(bit):
    pairs = []
    for rep in range(16):
        bits = list(bits_of(rep))
        bits[bit] ^= 1
        pairs.append((rep, rep_of(bits)))
    return pairs


def expert_table():
    table = np.zeros((16, 4, 16), np.int32)
    for rep in range(16):
        for quarter, order in enumerate(ORDERS):
            for relative in range(16):
                bits = list(bits_of(rep))
                for place, bit in enumerate(order):
                    bits[bit] ^= (relative >> (3 - place)) & 1
                table[rep, quarter, relative] = rep_of(bits)
    return table


def encode(value, shift):
    scaled = value * float(2**shift)
    second = scaled * scaled
    fourth = second * second
    eighth = fourth * fourth
    return jnp.where(value < 0, -eighth, eighth).astype(jnp.bfloat16)


def decode(code, shift):
    code = code.astype(jnp.float32)
    size = jnp.maximum(jnp.abs(code), float(2.0**-126))
    return code * jnp.exp2(jnp.log2(size) * -0.875 - float(shift))


def step_kernel(quarter, step, info, parts_ref, momentum_ref, *refs):
    received, out_ref = refs[:-1], refs[-1]

    def total(rows):
        value = parts_ref[0, rows]
        for turn, ref in enumerate(received):
            value = value + decode(ref[0, rows], SHIFTS[turn])
        return value

    def strip(index, carry):
        rows = pl.ds(pl.multiple_of(index * STRIP, STRIP), STRIP)
        out_ref[0, rows] = encode(total(rows), SHIFTS[step])
        return carry

    lax.fori_loop(0, QUARTER // STRIP, strip, 0)

    @pl.when(info[16] == quarter)
    def _():
        def band(index, carry):
            start = pl.multiple_of(info[17] + index * STRIP, STRIP)
            rows = pl.ds(start, STRIP)
            held = momentum_ref[0, pl.ds(pl.multiple_of(index * STRIP, STRIP), STRIP)].astype(jnp.float32)
            out_ref[0, rows] = encode(total(rows) + BLEND * held, SHIFTS[step])
            return carry

        lax.fori_loop(0, BAND // STRIP, band, 0)


def step_call(quarter, step, info, parts, momentum, received):
    count = 8 >> step
    base = count

    def expert(index, info):
        return info[base + index]

    in_specs = [
        pl.BlockSpec((1, QUARTER, FF), lambda i, info: (expert(i, info), quarter, 0)),
        pl.BlockSpec((1, BAND, FF), lambda i, info: (expert(i, info), 0, 0)),
    ] + [pl.BlockSpec((1, QUARTER, FF), lambda i, info: (base + i, 0, 0)) for _ in received]
    size = count * QUARTER * FF
    return pl.pallas_call(
        functools.partial(step_kernel, quarter, step),
        grid_spec=pltpu.PrefetchScalarGridSpec(
            num_scalar_prefetch=1,
            grid=(count,),
            in_specs=in_specs,
            out_specs=pl.BlockSpec((1, QUARTER, FF), lambda i, info: (i, 0, 0)),
        ),
        out_shape=jax.ShapeDtypeStruct((count, QUARTER, FF), jnp.bfloat16),
        cost_estimate=pl.CostEstimate(
            flops=size * 16, bytes_accessed=size * (6 + 2 * step), transcendentals=2 * size * step
        ),
        name=f"codes_q{quarter}_s{step}",
    )(info, parts, momentum, *received)


def halves(value):
    high = value.astype(jnp.bfloat16)
    return high, (value - high.astype(jnp.float32)).astype(jnp.bfloat16)


def dot(left, right):
    return jnp.dot(left, right, preferred_element_type=jnp.float32)


def product(left, right):
    return dot(left[0], right[0]) + (dot(left[0], right[1]) + dot(left[1], right[0]))


def iterate_kernel(info, parts_ref, momentum_ref, *refs):
    received, out_ref, high_ref, low_ref, sum_ref = refs[:16], refs[16], refs[17], refs[18], refs[19]

    for quarter in range(4):
        mine = received[4 * quarter : 4 * quarter + 4]

        def strip(index, carry, quarter=quarter, mine=mine):
            inner = pl.ds(pl.multiple_of(index * STRIP, STRIP), STRIP)
            outer = pl.ds(pl.multiple_of(quarter * QUARTER + index * STRIP, STRIP), STRIP)
            value = parts_ref[0, outer]
            for turn, ref in enumerate(mine):
                value = value + decode(ref[0, inner], SHIFTS[turn])
            sum_ref[outer] = value
            return carry

        lax.fori_loop(0, QUARTER // STRIP, strip, 0)

    start = pl.multiple_of(info[16] * QUARTER + info[17], BAND)
    sum_ref[pl.ds(start, BAND)] += BLEND * momentum_ref[0].astype(jnp.float32)

    gram = jnp.zeros((FF, FF), jnp.float32)
    cross = jnp.zeros((FF, FF), jnp.float32)
    rows_in = (((0,), (0,)), ((), ()))
    for quarter in range(4):
        rows = pl.ds(quarter * QUARTER, QUARTER)
        high, low = halves(sum_ref[rows])
        high_ref[rows] = high
        low_ref[rows] = low
        gram += lax.dot_general(high, high, rows_in, preferred_element_type=jnp.float32)
        cross += lax.dot_general(high, low, rows_in, preferred_element_type=jnp.float32)
    gram += cross + cross.T

    row = lax.broadcasted_iota(jnp.int32, (FF, FF), 0)
    column = lax.broadcasted_iota(jnp.int32, (FF, FF), 1)
    on_diagonal = row == column
    squares = jnp.sum(jnp.where(on_diagonal, gram, 0.0))
    scale = 1.0 / (jnp.sqrt(jnp.full((1, 1), squares)) + 1e-07 / GAIN)
    a = gram * scale * scale
    power = None
    for turn in range(NS_ITERS):
        a_split = halves(a)
        b = -4.775 * a + 2.0315 * product(a_split, a_split)
        b_split = halves(b)
        if power is None:
            power = jnp.where(on_diagonal, 3.4445, 0.0) + b
        else:
            power = 3.4445 * power + product(halves(power), b_split)
        if turn < NS_ITERS - 1:
            once = 3.4445 * a + product(a_split, b_split)
            a = 3.4445 * once + product(halves(once), b_split)
    power_split = halves(power * (scale * float(max(D, FF)) ** 0.5))
    for quarter in range(4):
        rows = pl.ds(quarter * QUARTER, QUARTER)
        out_ref[rows] = product((high_ref[rows], low_ref[rows]), power_split).astype(jnp.bfloat16)


def iterate_call(info, parts, momentum, received):
    def own(i, info):
        return (info[0], 0, 0)

    in_specs = [
        pl.BlockSpec((1, D, FF), own),
        pl.BlockSpec((1, BAND, FF), own),
    ] + [pl.BlockSpec((1, QUARTER, FF), lambda i, info: (0, 0, 0)) for _ in received]
    return pl.pallas_call(
        iterate_kernel,
        grid_spec=pltpu.PrefetchScalarGridSpec(
            num_scalar_prefetch=1,
            grid=(1,),
            in_specs=in_specs,
            out_specs=pl.BlockSpec((D, FF), lambda i, info: (0, 0)),
            scratch_shapes=[
                pltpu.VMEM((D, FF), jnp.bfloat16),
                pltpu.VMEM((D, FF), jnp.bfloat16),
                pltpu.VMEM((D, FF), jnp.float32),
            ],
        ),
        out_shape=jax.ShapeDtypeStruct((D, FF), jnp.bfloat16),
        compiler_params=pltpu.CompilerParams(vmem_limit_bytes=40 * 1024 * 1024),
        cost_estimate=pl.CostEstimate(
            flops=3 * 2 * FF * FF * (17 * FF + 2 * D), bytes_accessed=6 * 1024 * 1024, transcendentals=0
        ),
        name="newton_schulz",
    )(info, parts, momentum, *received)


def local(grad_parts, momentum):
    parts = grad_parts[0]
    rep = lax.axis_index("rep")
    table = jnp.asarray(expert_table())[rep]
    place = jnp.stack([rep // 4, (rep % 4) * BAND]).astype(jnp.int32)
    infos = [jnp.concatenate([table[quarter], place]) for quarter in range(4)]
    received = [[] for _ in range(4)]
    for step in range(4):
        for quarter in range(4):
            codes = step_call(quarter, step, infos[quarter], parts, momentum, received[quarter])
            received[quarter].append(lax.ppermute(codes, "rep", partners(ORDERS[quarter][step])))
    update = iterate_call(infos[0], parts, momentum, sum(received, []))
    return lax.all_to_all(update.reshape(16, BAND, FF), "rep", split_axis=0, concat_axis=0, tiled=True)


def solution(mesh):
    return jax.shard_map(
        local,
        mesh=mesh,
        in_specs=(P("rep", "exp", None, None), P("exp", "rep", None)),
        out_specs=P("exp", "rep", None),
        check_vma=False,
    )
```

profile of v0, /device:TPU:0, one launch (start us, length us, event | category | flops | bytes accessed | tf_op | source)
XLA Modules:
  0.0 175.3 jit_solution(7988827881768496137)
XLA Ops:
  0.0 0.7 constant_dynamic-slice_fusion
  0.7 0.6 add_add_fusion.3.info
  1.3 6.9 %codes_q3_s0.1 = bf16[8,256,384]{2,1,0:T(8,128)(2,1)} custom-call(s32[18]{0:T(128)} %add_add_fusion.3.info, f32[16,1024,384]{2,1,0:T(8,128)} %bitcast.13, bf16[16,64,384]{2,1,0:T(8,128)(2,1)} %momentum_ref.33), custom_call_target="tpu_custom_call" | custom-call | flops 12582912 | bytes 4718592 | tf_op jit(solution)/shard_map/codes_q3_s0/pallas_call | solution.py:110
  8.2 3.3 %collective-permute-start.12 = (bf16[8,256,384]{2,1,0:T(8,128)(2,1)}, bf16[8,256,384]{2,1,0:T(8,128)(2,1)S(1)}, u32[]{:S(2)}, u32[]{:S(2)}) collective-permute-start(bf16[8,256,384]{2,1,0:T(8,128)(2,1)} %codes_q3_s0.1), channel_id=1, source_target_pairs={{0,96},{8,104},{16,112},{24,120},{32,64},{40,72},{48,80},{56,88},{... | collective-permute-start | bytes 4718600 | tf_op jit(solution)/shard_map/ppermute | solution.py:235
  11.5 0.6 add_add_fusion.info
  12.1 7.1 %codes_q0_s0.1 = bf16[8,256,384]{2,1,0:T(8,128)(2,1)} custom-call(s32[18]{0:T(128)} %add_add_fusion.info, f32[16,1024,384]{2,1,0:T(8,128)} %bitcast.14, bf16[16,64,384]{2,1,0:T(8,128)(2,1)} %momentum_ref.33), custom_call_target="tpu_custom_call" | custom-call | flops 12582912 | bytes 4718592 | tf_op jit(solution)/shard_map/codes_q0_s0/pallas_call | solution.py:110
  19.2 1.5 collective-permute-start
  20.7 0.6 add_add_fusion.2.info
  21.2 6.9 %codes_q2_s0.1 = bf16[8,256,384]{2,1,0:T(8,128)(2,1)} custom-call(s32[18]{0:T(128)} %add_add_fusion.2.info, f32[16,1024,384]{2,1,0:T(8,128)} %bitcast.15, bf16[16,64,384]{2,1,0:T(8,128)(2,1)} %momentum_ref.33), custom_call_target="tpu_custom_call" | custom-call | flops 12582912 | bytes 4718592 | tf_op jit(solution)/shard_map/codes_q2_s0/pallas_call | solution.py:110
  28.2 2.1 %collective-permute-start.8 = (bf16[8,256,384]{2,1,0:T(8,128)(2,1)}, bf16[8,256,384]{2,1,0:T(8,128)(2,1)}, u32[]{:S(2)}, u32[]{:S(2)}) collective-permute-start(bf16[8,256,384]{2,1,0:T(8,128)(2,1)} %codes_q2_s0.1), channel_id=1, source_target_pairs={{0,24},{8,16},{16,8},{24,0},{32,56},{40,48},{48,40},{56,32},{64,88... | collective-permute-start | bytes 4718600 | tf_op jit(solution)/shard_map/ppermute | solution.py:235
  30.2 0.7 add_add_fusion.1.info
  30.9 6.9 %codes_q1_s0.1 = bf16[8,256,384]{2,1,0:T(8,128)(2,1)} custom-call(s32[18]{0:T(128)} %add_add_fusion.1.info, f32[16,1024,384]{2,1,0:T(8,128)} %bitcast.16, bf16[16,64,384]{2,1,0:T(8,128)(2,1)} %momentum_ref.33), custom_call_target="tpu_custom_call" | custom-call | flops 12582912 | bytes 4718592 | tf_op jit(solution)/shard_map/codes_q1_s0/pallas_call | solution.py:110
  37.8 0.0 collective-permute-start.4
  37.8 8.3 %collective-permute-done.12.refs_0_.refs_12_ = bf16[8,256,384]{2,1,0:T(8,128)(2,1)S(1)} collective-permute-done((bf16[8,256,384]{2,1,0:T(8,128)(2,1)}, bf16[8,256,384]{2,1,0:T(8,128)(2,1)S(1)}, u32[]{:S(2)}, u32[]{:S(2)}) %collective-permute-start.12) | collective-permute-done | bytes 1572896 | tf_op jit(solution)/shard_map/ppermute | solution.py:235
  46.1 1.2 copy-done.1
  47.3 4.9 %codes_q3_s1.1 = bf16[4,256,384]{2,1,0:T(8,128)(2,1)} custom-call(s32[18]{0:T(128)} %add_add_fusion.3.info, f32[16,1024,384]{2,1,0:T(8,128)} %bitcast.17, bf16[16,64,384]{2,1,0:T(8,128)(2,1)} %momentum_ref.33, bf16[8,256,384]{2,1,0:T(8,128)(2,1)} %copy-done.1), custom_call_target="tpu_custom_call" | custom-call | flops 6291456 | bytes 3145728 | tf_op jit(solution)/shard_map/codes_q3_s1/pallas_call | solution.py:110
  52.2 1.5 collective-permute-start.13
  53.7 2.5 %collective-permute-done.refs_0_ = bf16[8,256,384]{2,1,0:T(8,128)(2,1)} collective-permute-done((bf16[8,256,384]{2,1,0:T(8,128)(2,1)}, bf16[8,256,384]{2,1,0:T(8,128)(2,1)}, u32[]{:S(2)}, u32[]{:S(2)}) %collective-permute-start) | collective-permute-done | bytes 1572896 | tf_op jit(solution)/shard_map/ppermute | solution.py:235
  56.2 5.1 %codes_q0_s1.1 = bf16[4,256,384]{2,1,0:T(8,128)(2,1)} custom-call(s32[18]{0:T(128)} %add_add_fusion.info, f32[16,1024,384]{2,1,0:T(8,128)} %bitcast.18, bf16[16,64,384]{2,1,0:T(8,128)(2,1)} %momentum_ref.33, bf16[8,256,384]{2,1,0:T(8,128)(2,1)} %collective-permute-done.refs_0_), custom_call_target="tpu_custom_call" | custom-call | flops 6291456 | bytes 3145728 | tf_op jit(solution)/shard_map/codes_q0_s1/pallas_call | solution.py:110
  61.2 0.0 collective-permute-start.1
  61.2 4.0 %collective-permute-done.8.refs_0_.refs_8_ = bf16[8,256,384]{2,1,0:T(8,128)(2,1)} collective-permute-done((bf16[8,256,384]{2,1,0:T(8,128)(2,1)}, bf16[8,256,384]{2,1,0:T(8,128)(2,1)}, u32[]{:S(2)}, u32[]{:S(2)}) %collective-permute-start.8) | collective-permute-done | bytes 1572896 | tf_op jit(solution)/shard_map/ppermute | solution.py:235
  65.3 4.9 %codes_q2_s1.1 = bf16[4,256,384]{2,1,0:T(8,128)(2,1)} custom-call(s32[18]{0:T(128)} %add_add_fusion.2.info, f32[16,1024,384]{2,1,0:T(8,128)} %bitcast.19, bf16[16,64,384]{2,1,0:T(8,128)(2,1)} %momentum_ref.33, bf16[8,256,384]{2,1,0:T(8,128)(2,1)} %collective-permute-done.8.refs_0_.refs_8_), custom_call_target="tpu_custom_call" | custom-call | flops 6291456 | bytes 3145728 | tf_op jit(solution)/shard_map/codes_q2_s1/pallas_call | solution.py:110
  70.2 0.1 collective-permute-start.9
  70.3 5.2 %collective-permute-done.4.refs_0_.refs_4_ = bf16[8,256,384]{2,1,0:T(8,128)(2,1)} collective-permute-done((bf16[8,256,384]{2,1,0:T(8,128)(2,1)}, bf16[8,256,384]{2,1,0:T(8,128)(2,1)}, u32[]{:S(2)}, u32[]{:S(2)}) %collective-permute-start.4) | collective-permute-done | bytes 1572896 | tf_op jit(solution)/shard_map/ppermute | solution.py:235
  75.4 4.9 %codes_q1_s1.1 = bf16[4,256,384]{2,1,0:T(8,128)(2,1)} custom-call(s32[18]{0:T(128)} %add_add_fusion.1.info, f32[16,1024,384]{2,1,0:T(8,128)} %bitcast.20, bf16[16,64,384]{2,1,0:T(8,128)(2,1)} %momentum_ref.33, bf16[8,256,384]{2,1,0:T(8,128)(2,1)} %collective-permute-done.4.refs_0_.refs_4_), custom_call_target="tpu_custom_call" | custom-call | flops 6291456 | bytes 3145728 | tf_op jit(solution)/shard_map/codes_q1_s1/pallas_call | solution.py:110
  80.4 1.1 collective-permute-start.5
  81.5 0.0 collective-permute-done.13.refs_1_.refs_13_
  81.5 0.9 copy-done.3
  82.4 3.6 %codes_q3_s2.1 = bf16[2,256,384]{2,1,0:T(8,128)(2,1)} custom-call(s32[18]{0:T(128)} %add_add_fusion.3.info, f32[16,1024,384]{2,1,0:T(8,128)} %bitcast.21, bf16[16,64,384]{2,1,0:T(8,128)(2,1)} %momentum_ref.33, bf16[8,256,384]{2,1,0:T(8,128)(2,1)} %copy-done.1, bf16[4,256,384]{2,1,0:T(8,128)(2,1)} %copy-done.3), custom_call_target="tpu_custom_call" | custom-call | flops 3145728 | bytes 1966080 | tf_op jit(solution)/shard_map/codes_q3_s2/pallas_call | solution.py:110
  86.0 0.2 collective-permute-start.14
  86.1 6.1 %collective-permute-done.1.refs_1_ = bf16[4,256,384]{2,1,0:T(8,128)(2,1)S(1)} collective-permute-done((bf16[4,256,384]{2,1,0:T(8,128)(2,1)}, bf16[4,256,384]{2,1,0:T(8,128)(2,1)S(1)}, u32[]{:S(2)}, u32[]{:S(2)}) %collective-permute-start.1) | collective-permute-done | bytes 786464 | tf_op jit(solution)/shard_map/ppermute | solution.py:235
  92.2 0.9 copy-done.5
  93.1 3.8 %codes_q0_s2.1 = bf16[2,256,384]{2,1,0:T(8,128)(2,1)} custom-call(s32[18]{0:T(128)} %add_add_fusion.info, f32[16,1024,384]{2,1,0:T(8,128)} %bitcast.22, bf16[16,64,384]{2,1,0:T(8,128)(2,1)} %momentum_ref.33, bf16[8,256,384]{2,1,0:T(8,128)(2,1)} %collective-permute-done.refs_0_, bf16[4,256,384]{2,1,0:T(8,128)(2,1)} %copy-done.5), custom_call_target="tpu_custom_call" | custom-call | flops 3145728 | bytes 1966080 | tf_op jit(solution)/shard_map/codes_q0_s2/pallas_call | solution.py:110
  96.9 1.1 collective-permute-start.2
  98.0 0.0 collective-permute-done.9.refs_1_.refs_9_
  98.0 0.9 copy-done.7
  98.9 3.6 %codes_q2_s2.1 = bf16[2,256,384]{2,1,0:T(8,128)(2,1)} custom-call(s32[18]{0:T(128)} %add_add_fusion.2.info, f32[16,1024,384]{2,1,0:T(8,128)} %bitcast.23, bf16[16,64,384]{2,1,0:T(8,128)(2,1)} %momentum_ref.33, bf16[8,256,384]{2,1,0:T(8,128)(2,1)} %collective-permute-done.8.refs_0_.refs_8_, bf16[4,256,384]{2,1,0:T(8,128)(2,1)} %copy-done.7), custom_call_target="tpu_custom_call" | custom-call | flops 3145728 | bytes 1966080 | tf_op jit(solution)/shard_map/codes_q2_s2/pallas_call | solution.py:110
  102.5 0.9 copy-done.9
  103.4 3.6 %codes_q1_s2.1 = bf16[2,256,384]{2,1,0:T(8,128)(2,1)} custom-call(s32[18]{0:T(128)} %add_add_fusion.1.info, f32[16,1024,384]{2,1,0:T(8,128)} %bitcast.24, bf16[16,64,384]{2,1,0:T(8,128)(2,1)} %momentum_ref.33, bf16[8,256,384]{2,1,0:T(8,128)(2,1)} %collective-permute-done.4.refs_0_.refs_4_, bf16[4,256,384]{2,1,0:T(8,128)(2,1)} %copy-done.9), custom_call_target="tpu_custom_call" | custom-call | flops 3145728 | bytes 1966080 | tf_op jit(solution)/shard_map/codes_q1_s2/pallas_call | solution.py:110
  107.0 0.7 copy-done.11
  107.7 3.2 %codes_q3_s3.1 = bf16[1,256,384]{2,1,0:T(8,128)(2,1)} custom-call(s32[18]{0:T(128)} %add_add_fusion.3.info, f32[16,1024,384]{2,1,0:T(8,128)} %bitcast.25, bf16[16,64,384]{2,1,0:T(8,128)(2,1)} %momentum_ref.33, bf16[8,256,384]{2,1,0:T(8,128)(2,1)} %copy-done.1, bf16[4,256,384]{2,1,0:T(8,128)(2,1)} %copy-done.3, bf16[2,256,384]{2,1,0:T(8,128)(2,1)} %copy-done.11), custom_call_target="tpu_custom_call" | custom-call | flops 1572864 | bytes 1179648 | tf_op jit(solution)/shard_map/codes_q3_s3/pallas_call | solution.py:110
  110.9 2.1 %collective-permute-start.15 = (bf16[1,256,384]{2,1,0:T(8,128)(2,1)}, bf16[1,256,384]{2,1,0:T(8,128)(2,1)}, u32[]{:S(2)}, u32[]{:S(2)}) collective-permute-start(bf16[1,256,384]{2,1,0:T(8,128)(2,1)} %codes_q3_s3.1), channel_id=1, source_target_pairs={{0,24},{8,16},{16,8},{24,0},{32,56},{40,48},{48,40},{56,32},{64,88... | collective-permute-start | bytes 589832 | tf_op jit(solution)/shard_map/ppermute | solution.py:235
  113.0 0.0 collective-permute-done.2.refs_2_
  113.0 0.7 copy-done.13
  113.7 3.3 %codes_q0_s3.1 = bf16[1,256,384]{2,1,0:T(8,128)(2,1)} custom-call(s32[18]{0:T(128)} %add_add_fusion.info, f32[16,1024,384]{2,1,0:T(8,128)} %bitcast.26, bf16[16,64,384]{2,1,0:T(8,128)(2,1)} %momentum_ref.33, bf16[8,256,384]{2,1,0:T(8,128)(2,1)} %collective-permute-done.refs_0_, bf16[4,256,384]{2,1,0:T(8,128)(2,1)} %copy-done.5, bf16[2,256,384]{2,1,0:T(8,128)(2,1)} %copy-done.13), custom_call_target="tpu_custom_call" | custom-call | flops 1572864 | bytes 1179648 | tf_op jit(solution)/shard_map/codes_q0_s3/pallas_call | solution.py:110
  117.0 3.2 %collective-permute-start.3 = (bf16[1,256,384]{2,1,0:T(8,128)(2,1)}, bf16[1,256,384]{2,1,0:T(8,128)(2,1)}, u32[]{:S(2)}, u32[]{:S(2)}) collective-permute-start(bf16[1,256,384]{2,1,0:T(8,128)(2,1)} %codes_q0_s3.1), channel_id=1, source_target_pairs={{0,96},{8,104},{16,112},{24,120},{32,64},{40,72},{48,80},{56,88},{... | collective-permute-start | bytes 589832 | tf_op jit(solution)/shard_map/ppermute | solution.py:235
  120.3 0.8 copy-done.15
  121.1 3.2 %codes_q2_s3.1 = bf16[1,256,384]{2,1,0:T(8,128)(2,1)} custom-call(s32[18]{0:T(128)} %add_add_fusion.2.info, f32[16,1024,384]{2,1,0:T(8,128)} %bitcast.27, bf16[16,64,384]{2,1,0:T(8,128)(2,1)} %momentum_ref.33, bf16[8,256,384]{2,1,0:T(8,128)(2,1)} %collective-permute-done.8.refs_0_.refs_8_, bf16[4,256,384]{2,1,0:T(8,128)(2,1)} %copy-done.7, ...), custom_call_target="tpu_custom_call" | custom-call | flops 1572864 | bytes 1179648 | tf_op jit(solution)/shard_map/codes_q2_s3/pallas_call | solution.py:110
  124.2 0.1 collective-permute-start.11
  124.3 3.4 %codes_q1_s3.1 = bf16[1,256,384]{2,1,0:T(8,128)(2,1)} custom-call(s32[18]{0:T(128)} %add_add_fusion.1.info, f32[16,1024,384]{2,1,0:T(8,128)} %bitcast.28, bf16[16,64,384]{2,1,0:T(8,128)(2,1)} %momentum_ref.33, bf16[8,256,384]{2,1,0:T(8,128)(2,1)} %collective-permute-done.4.refs_0_.refs_4_, bf16[4,256,384]{2,1,0:T(8,128)(2,1)} %copy-done.9, ...), custom_call_target="tpu_custom_call" | custom-call | flops 1572864 | bytes 1179648 | tf_op jit(solution)/shard_map/codes_q1_s3/pallas_call | solution.py:110
  127.8 1.4 collective-permute-start.7
  129.2 0.0 collective-permute-done.15.refs_15_
  129.2 0.0 collective-permute-done.3.refs_3_
  129.2 1.1 collective-permute-done.11.refs_11_
  130.3 3.4 %collective-permute-done.7.refs_7_ = bf16[1,256,384]{2,1,0:T(8,128)(2,1)S(1)} collective-permute-done((bf16[1,256,384]{2,1,0:T(8,128)(2,1)}, bf16[1,256,384]{2,1,0:T(8,128)(2,1)S(1)}, u32[]{:S(2)}, u32[]{:S(2)}) %collective-permute-start.7) | collective-permute-done | bytes 196640 | tf_op jit(solution)/shard_map/ppermute | solution.py:235
  133.7 0.0 copy-start.6
  133.7 1.1 copy-done.6
  134.8 1.1 copy-done.8
  136.0 1.1 copy-done.10
  137.1 1.0 copy-done.14
  138.1 1.0 copy-done.16
  139.1 19.3 %newton_schulz.1 = bf16[1024,384]{1,0:T(8,128)(2,1)S(1)} custom-call(s32[18]{0:T(128)S(1)} %copy-done.17, f32[16,1024,384]{2,1,0:T(8,128)} %bitcast.29, bf16[16,64,384]{2,1,0:T(8,128)(2,1)S(1)} %copy-done, bf16[8,256,384]{2,1,0:T(8,128)(2,1)} %collective-permute-done.refs_0_, bf16[4,256,384]{2,1,0:T(8,128)(2,1)S(1)} %copy-done.6, ...), custom_call_target="tpu_custom_call" | custom-call | flops 7587495936 | bytes 6291456 | tf_op jit(solution)/shard_map/newton_schulz/pallas_call | solution.py:203
  158.4 16.1 %all_to_all.5 = bf16[16,64,384]{2,1,0:T(8,128)(2,1)S(1)} all-to-all(bf16[16,64,384]{2,1,0:T(8,128)(2,1)S(1)} %bitcast.12), channel_id=1, replica_groups=mesh['rep'=16,'exp'=8] {'rep'}, dimensions={0} | all-to-all | bytes 1572864 | tf_op jit(solution)/shard_map/all_to_all | solution.py:237
  174.4 0.9 copy.5
  (29 shorter events, 0.1 us)
Async XLA Ops:
  8.2 37.9 %collective-permute-start.12 = (bf16[8,256,384]{2,1,0:T(8,128)(2,1)}, bf16[8,256,384]{2,1,0:T(8,128)(2,1)S(1)}, u32[]{:S(2)}, u32[]{:S(2)}) collective-permute-start(bf16[8,256,384]{2,1,0:T(8,128)(2,1)} %codes_q3_s0.1), channel_id=1, source_target_pairs={{0,96},{8,104},{16,112},{24,120},{32,64},{40,72},{48,80},{56,88},{... | collective-permute-start | bytes 4718600 | tf_op jit(solution)/shard_map/ppermute | solution.py:235
  19.2 37.0 %collective-permute-start = (bf16[8,256,384]{2,1,0:T(8,128)(2,1)}, bf16[8,256,384]{2,1,0:T(8,128)(2,1)}, u32[]{:S(2)}, u32[]{:S(2)}) collective-permute-start(bf16[8,256,384]{2,1,0:T(8,128)(2,1)} %codes_q0_s0.1), channel_id=1, source_target_pairs={{0,8},{8,0},{16,24},{24,16},{32,40},{40,32},{48,56},{56,48},{64,72... | collective-permute-start | bytes 4718600 | tf_op jit(solution)/shard_map/ppermute | solution.py:235
  28.2 37.1 %collective-permute-start.8 = (bf16[8,256,384]{2,1,0:T(8,128)(2,1)}, bf16[8,256,384]{2,1,0:T(8,128)(2,1)}, u32[]{:S(2)}, u32[]{:S(2)}) collective-permute-start(bf16[8,256,384]{2,1,0:T(8,128)(2,1)} %codes_q2_s0.1), channel_id=1, source_target_pairs={{0,24},{8,16},{16,8},{24,0},{32,56},{40,48},{48,40},{56,32},{64,88... | collective-permute-start | bytes 4718600 | tf_op jit(solution)/shard_map/ppermute | solution.py:235
  37.8 37.7 %collective-permute-start.4 = (bf16[8,256,384]{2,1,0:T(8,128)(2,1)}, bf16[8,256,384]{2,1,0:T(8,128)(2,1)}, u32[]{:S(2)}, u32[]{:S(2)}) collective-permute-start(bf16[8,256,384]{2,1,0:T(8,128)(2,1)} %codes_q1_s0.1), channel_id=1, source_target_pairs={{0,32},{8,40},{16,48},{24,56},{32,0},{40,8},{48,16},{56,24},{64,96... | collective-permute-start | bytes 4718600 | tf_op jit(solution)/shard_map/ppermute | solution.py:235
  46.1 1.2 copy-start.1
  52.2 29.3 %collective-permute-start.13 = (bf16[4,256,384]{2,1,0:T(8,128)(2,1)}, bf16[4,256,384]{2,1,0:T(8,128)(2,1)S(1)}, u32[]{:S(2)}, u32[]{:S(2)}) collective-permute-start(bf16[4,256,384]{2,1,0:T(8,128)(2,1)} %codes_q3_s1.1), channel_id=1, source_target_pairs={{0,8},{8,0},{16,24},{24,16},{32,40},{40,32},{48,56},{56,48},{64,72... | collective-permute-start | bytes 2359304 | tf_op jit(solution)/shard_map/ppermute | solution.py:235
  61.2 31.0 %collective-permute-start.1 = (bf16[4,256,384]{2,1,0:T(8,128)(2,1)}, bf16[4,256,384]{2,1,0:T(8,128)(2,1)S(1)}, u32[]{:S(2)}, u32[]{:S(2)}) collective-permute-start(bf16[4,256,384]{2,1,0:T(8,128)(2,1)} %codes_q0_s1.1), channel_id=1, source_target_pairs={{0,32},{8,40},{16,48},{24,56},{32,0},{40,8},{48,16},{56,24},{64,96... | collective-permute-start | bytes 2359304 | tf_op jit(solution)/shard_map/ppermute | solution.py:235
  70.2 27.8 %collective-permute-start.9 = (bf16[4,256,384]{2,1,0:T(8,128)(2,1)}, bf16[4,256,384]{2,1,0:T(8,128)(2,1)S(1)}, u32[]{:S(2)}, u32[]{:S(2)}) collective-permute-start(bf16[4,256,384]{2,1,0:T(8,128)(2,1)} %codes_q2_s1.1), channel_id=1, source_target_pairs={{0,96},{8,104},{16,112},{24,120},{32,64},{40,72},{48,80},{56,88},{... | collective-permute-start | bytes 2359304 | tf_op jit(solution)/shard_map/ppermute | solution.py:235
  80.4 22.1 %collective-permute-start.5 = (bf16[4,256,384]{2,1,0:T(8,128)(2,1)}, bf16[4,256,384]{2,1,0:T(8,128)(2,1)S(1)}, u32[]{:S(2)}, u32[]{:S(2)}) collective-permute-start(bf16[4,256,384]{2,1,0:T(8,128)(2,1)} %codes_q1_s1.1), channel_id=1, source_target_pairs={{0,24},{8,16},{16,8},{24,0},{32,56},{40,48},{48,40},{56,32},{64,88... | collective-permute-start | bytes 2359304 | tf_op jit(solution)/shard_map/ppermute | solution.py:235
  81.5 0.9 copy-start.3
  86.0 21.0 %collective-permute-start.14 = (bf16[2,256,384]{2,1,0:T(8,128)(2,1)}, bf16[2,256,384]{2,1,0:T(8,128)(2,1)S(1)}, u32[]{:S(2)}, u32[]{:S(2)}) collective-permute-start(bf16[2,256,384]{2,1,0:T(8,128)(2,1)} %codes_q3_s2.1), channel_id=1, source_target_pairs={{0,32},{8,40},{16,48},{24,56},{32,0},{40,8},{48,16},{56,24},{64,96... | collective-permute-start | bytes 1179656 | tf_op jit(solution)/shard_map/ppermute | solution.py:235
  92.2 0.9 copy-start.5
  96.9 16.1 %collective-permute-start.2 = (bf16[2,256,384]{2,1,0:T(8,128)(2,1)}, bf16[2,256,384]{2,1,0:T(8,128)(2,1)S(1)}, u32[]{:S(2)}, u32[]{:S(2)}) collective-permute-start(bf16[2,256,384]{2,1,0:T(8,128)(2,1)} %codes_q0_s2.1), channel_id=1, source_target_pairs={{0,24},{8,16},{16,8},{24,0},{32,56},{40,48},{48,40},{56,32},{64,88... | collective-permute-start | bytes 1179656 | tf_op jit(solution)/shard_map/ppermute | solution.py:235
  98.0 0.9 copy-start.7
  102.5 17.8 %collective-permute-start.10 = (bf16[2,256,384]{2,1,0:T(8,128)(2,1)}, bf16[2,256,384]{2,1,0:T(8,128)(2,1)S(1)}, u32[]{:S(2)}, u32[]{:S(2)}) collective-permute-start(bf16[2,256,384]{2,1,0:T(8,128)(2,1)} %codes_q2_s2.1), channel_id=1, source_target_pairs={{0,8},{8,0},{16,24},{24,16},{32,40},{40,32},{48,56},{56,48},{64,72... | collective-permute-start | bytes 1179656 | tf_op jit(solution)/shard_map/ppermute | solution.py:235
  102.5 0.9 copy-start.9
  107.0 17.4 %collective-permute-start.6 = (bf16[2,256,384]{2,1,0:T(8,128)(2,1)}, bf16[2,256,384]{2,1,0:T(8,128)(2,1)}, u32[]{:S(2)}, u32[]{:S(2)}) collective-permute-start(bf16[2,256,384]{2,1,0:T(8,128)(2,1)} %codes_q1_s2.1), channel_id=1, source_target_pairs={{0,96},{8,104},{16,112},{24,120},{32,64},{40,72},{48,80},{56,88},{... | collective-permute-start | bytes 1179656 | tf_op jit(solution)/shard_map/ppermute | solution.py:235
  107.0 0.7 copy-start.11
  110.9 18.3 %collective-permute-start.15 = (bf16[1,256,384]{2,1,0:T(8,128)(2,1)}, bf16[1,256,384]{2,1,0:T(8,128)(2,1)}, u32[]{:S(2)}, u32[]{:S(2)}) collective-permute-start(bf16[1,256,384]{2,1,0:T(8,128)(2,1)} %codes_q3_s3.1), channel_id=1, source_target_pairs={{0,24},{8,16},{16,8},{24,0},{32,56},{40,48},{48,40},{56,32},{64,88... | collective-permute-start | bytes 589832 | tf_op jit(solution)/shard_map/ppermute | solution.py:235
  113.0 0.8 copy-start.13
  117.0 12.2 %collective-permute-start.3 = (bf16[1,256,384]{2,1,0:T(8,128)(2,1)}, bf16[1,256,384]{2,1,0:T(8,128)(2,1)}, u32[]{:S(2)}, u32[]{:S(2)}) collective-permute-start(bf16[1,256,384]{2,1,0:T(8,128)(2,1)} %codes_q0_s3.1), channel_id=1, source_target_pairs={{0,96},{8,104},{16,112},{24,120},{32,64},{40,72},{48,80},{56,88},{... | collective-permute-start | bytes 589832 | tf_op jit(solution)/shard_map/ppermute | solution.py:235
  120.3 0.8 copy-start.15
  124.2 9.4 %copy-start = (bf16[16,64,384]{2,1,0:T(8,128)(2,1)S(1)}, bf16[16,64,384]{2,1,0:T(8,128)(2,1)}, u32[]{:S(2)}) copy-start(bf16[16,64,384]{2,1,0:T(8,128)(2,1)} %momentum_ref.33) | copy-start | bytes 2359300
  124.2 9.4 %copy-start.2 = (bf16[8,256,384]{2,1,0:T(8,128)(2,1)S(1)}, bf16[8,256,384]{2,1,0:T(8,128)(2,1)}, u32[]{:S(2)}) copy-start(bf16[8,256,384]{2,1,0:T(8,128)(2,1)} %copy-done.1) | copy-start | bytes 4718596
  124.2 9.4 %copy-start.4 = (bf16[4,256,384]{2,1,0:T(8,128)(2,1)S(1)}, bf16[4,256,384]{2,1,0:T(8,128)(2,1)}, u32[]{:S(2)}) copy-start(bf16[4,256,384]{2,1,0:T(8,128)(2,1)} %copy-done.3) | copy-start | bytes 2359300
  124.2 9.4 %copy-start.12 = (bf16[2,256,384]{2,1,0:T(8,128)(2,1)S(1)}, bf16[2,256,384]{2,1,0:T(8,128)(2,1)}, u32[]{:S(2)}) copy-start(bf16[2,256,384]{2,1,0:T(8,128)(2,1)} %copy-done.11) | copy-start | bytes 1179652
  124.2 9.5 %copy-start.17 = (s32[18]{0:T(128)S(1)}, s32[18]{0:T(128)}, u32[]{:S(2)}) copy-start(s32[18]{0:T(128)} %add_add_fusion.info) | copy-start | bytes 220
  124.2 6.1 %collective-permute-start.11 = (bf16[1,256,384]{2,1,0:T(8,128)(2,1)}, bf16[1,256,384]{2,1,0:T(8,128)(2,1)}, u32[]{:S(2)}, u32[]{:S(2)}) collective-permute-start(bf16[1,256,384]{2,1,0:T(8,128)(2,1)} %codes_q2_s3.1), channel_id=1, source_target_pairs={{0,32},{8,40},{16,48},{24,56},{32,0},{40,8},{48,16},{56,24},{64,96... | collective-permute-start | bytes 589832 | tf_op jit(solution)/shard_map/ppermute | solution.py:235
  127.8 5.9 %collective-permute-start.7 = (bf16[1,256,384]{2,1,0:T(8,128)(2,1)}, bf16[1,256,384]{2,1,0:T(8,128)(2,1)S(1)}, u32[]{:S(2)}, u32[]{:S(2)}) collective-permute-start(bf16[1,256,384]{2,1,0:T(8,128)(2,1)} %codes_q1_s3.1), channel_id=1, source_target_pairs={{0,8},{8,0},{16,24},{24,16},{32,40},{40,32},{48,56},{56,48},{64,72... | collective-permute-start | bytes 589832 | tf_op jit(solution)/shard_map/ppermute | solution.py:235
  133.7 1.1 copy-start.6
  134.8 1.1 copy-start.8
  136.0 1.1 copy-start.10
  137.1 1.0 copy-start.14
  138.1 1.0 copy-start.16
where the time goes:
time: 177 us; the launch traced here: 175 us
  Pallas kernels  94.4 us (53%)
  waiting for transfers between devices  30.5 us (17%)
  starting transfers between devices  17.8 us (10%)
  blocking collectives  16.1 us (9%)
  local copies, waits for them, and re-layouts  14 us (8%)
  other arithmetic  2.4 us (1%)
    pallas_call x16, Pallas kernels, step_call(): pl.pallas_call(functools.partial(step_kernel, quarter, step), grid_spec=p...  75.2 us
    ppermute x16, waiting for transfers between devices, local(): lax.ppermute(codes, 'rep', partners(ORDERS[quarter][step]))  30.5 us
    pallas_call x1, Pallas kernels, iterate_call(): pl.pallas_call(iterate_kernel, grid_spec=pltpu.PrefetchScalarGridSpec(num...  19.3 us
    ppermute x16, starting transfers between devices, local(): lax.ppermute(codes, 'rep', partners(ORDERS[quarter][step]))  17.8 us
    all_to_all x1, blocking collectives, local(): lax.all_to_all(update.reshape(16, BAND, FF), 'rep', split_axis=0, concat_...  16.1 us
    unnamed x37, local copies, waits for them, and re-layouts  13.4 us
  transfers between devices with their start and end apart: 16, of which 7 were waited for; matrix products, arithmetic and copies ran while one was open for 1% of the time, Pallas kernels for 39%

commit v1 on v0

v1 whole, which is shorter than its diff:
```python
import functools
import math

import jax
import jax.numpy as jnp
import numpy as np
from jax import lax
from jax.experimental import pallas as pl
from jax.experimental.pallas import tpu as pltpu
from jax.sharding import PartitionSpec as P

D = 1024
FF = 384
NS_ITERS = 5
QUARTER = D // 4
STRIP = 64
BAND = 64
GAIN = 1.0 + 0.95
BLEND = 0.95 * 0.95 / GAIN

ORDERS = ((3, 0, 2, 1), (1, 3, 0, 2), (2, 1, 3, 0), (0, 2, 1, 3))
SHIFTS = (11, 11, 10, 9)


def bits_of(rep):
    y, x = divmod(rep, 4)
    return (int(x in (1, 2)), int(x >= 2), int(y in (1, 2)), int(y >= 2))


def rep_of(bits):
    x = 2 * bits[1] + (bits[0] ^ bits[1])
    y = 2 * bits[3] + (bits[2] ^ bits[3])
    return 4 * y + x


def partners(bit):
    pairs = []
    for rep in range(16):
        bits = list(bits_of(rep))
        bits[bit] ^= 1
        pairs.append((rep, rep_of(bits)))
    return pairs


def expert_table():
    table = np.zeros((16, 128), np.int32)
    for rep in range(16):
        for quarter, order in enumerate(ORDERS):
            for relative in range(16):
                bits = list(bits_of(rep))
                for place, bit in enumerate(order):
                    bits[bit] ^= (relative >> (3 - place)) & 1
                table[rep, 16 * quarter + relative] = rep_of(bits)
        table[rep, 64:66] = rep // 4, rep % 4 * BAND
    return table


def encode(value, shift):
    scaled = value * float(2**shift)
    second = scaled * scaled
    fourth = second * second
    eighth = fourth * fourth
    return jnp.where(value < 0, -eighth, eighth).astype(jnp.bfloat16)


def decode(code, shift):
    code = code.astype(jnp.float32)
    size = jnp.maximum(jnp.abs(code), float(2.0**-126))
    return code * jnp.exp2(jnp.log(size) * (-0.875 / math.log(2.0)) - float(shift))


def fetches(quarter, entries, info, parts_ref, momentum_ref, held_ref, band_ref, sems, band_sems):
    rows = pl.ds(quarter * QUARTER, QUARTER)

    def raw(index):
        expert = info[16 * quarter + entries + index]
        return pltpu.make_async_copy(parts_ref.at[expert, rows], held_ref.at[index], sems.at[index])

    def band(index):
        expert = info[16 * quarter + entries + index]
        return pltpu.make_async_copy(momentum_ref.at[expert], band_ref.at[index], band_sems.at[index])

    def start():
        for index in range(8):
            raw(index).start()

        @pl.when(info[64] == quarter)
        def _():
            for index in range(8):
                band(index).start()

    def finish(index):
        raw(index).wait()

        @pl.when(info[64] == quarter)
        def _():
            band(index).wait()
            rows = pl.ds(pl.multiple_of(info[65], BAND), BAND)
            held_ref[index, rows] += BLEND * band_ref[index].astype(jnp.float32)

    return start, finish


FETCH_SCRATCH = (
    pltpu.VMEM((8, BAND, FF), jnp.bfloat16),
    pltpu.SemaphoreType.DMA((8,)),
    pltpu.SemaphoreType.DMA((8,)),
)


def encode_expert(held_ref, out_ref, index):
    for start in range(0, QUARTER, STRIP):
        rows = pl.ds(start, STRIP)
        out_ref[index, rows] = encode(held_ref[index, rows], SHIFTS[0])


def first_kernel(info, parts_ref, momentum_ref, out_ref, next_ref, held_ref, *scratch):
    start_now, finish_now = fetches(3, 8, info, parts_ref, momentum_ref, held_ref, *scratch[:3])
    start_next, finish_next = fetches(2, 8, info, parts_ref, momentum_ref, next_ref, *scratch[3:])
    start_now()
    start_next()

    def expert(index, carry):
        finish_now(index)
        encode_expert(held_ref, out_ref, index)
        return carry

    lax.fori_loop(0, 8, expert, 0)
    lax.fori_loop(0, 8, lambda index, carry: (finish_next(index), carry)[1], 0)


def later_kernel(quarter, info, parts_ref, momentum_ref, held_ref, out_ref, *rest):
    last = quarter == 0
    if not last:
        start_next, finish_next = fetches(quarter - 1, 8, info, parts_ref, momentum_ref, *rest)
        start_next()

    def expert(index, carry):
        encode_expert(held_ref, out_ref, index)
        return carry

    lax.fori_loop(0, 8, expert, 0)
    if not last:
        lax.fori_loop(0, 8, lambda index, carry: (finish_next(index), carry)[1], 0)


def first_calls(info, parts, momentum):
    size = 8 * QUARTER * FF
    whole = pl.BlockSpec(memory_space=pltpu.VMEM)
    raw = jax.ShapeDtypeStruct((8, QUARTER, FF), jnp.float32)
    codes = [None] * 4
    held = None
    for quarter in (3, 2, 1, 0):
        last = quarter == 0
        results = pl.pallas_call(
            first_kernel if held is None else functools.partial(later_kernel, quarter),
            in_specs=[
                pl.BlockSpec(memory_space=pltpu.SMEM),
                pl.BlockSpec(memory_space=pltpu.HBM),
                pl.BlockSpec(memory_space=pltpu.HBM),
            ]
            + [whole] * (held is not None),
            out_specs=[whole] * (1 if last else 2),
            scratch_shapes=[pltpu.VMEM((8, QUARTER, FF), jnp.float32)] * (held is None)
            + [*FETCH_SCRATCH] * ((held is None) + (not last)),
            out_shape=[jax.ShapeDtypeStruct((8, QUARTER, FF), jnp.bfloat16)] + [raw] * (not last),
            compiler_params=pltpu.CompilerParams(vmem_limit_bytes=40 * 1024 * 1024),
            cost_estimate=pl.CostEstimate(flops=size * 10, bytes_accessed=size * 6, transcendentals=0),
            name=f"first_q{quarter}",
        )(info, parts, momentum, *([] if held is None else [held]))
        codes[quarter] = results[0]
        held = results[-1]
    return codes


def keep_kernel(info, parts_ref, momentum_ref, *refs):
    held_refs, band_refs, sems, band_sems = refs[4:8], *refs[8:]
    pending = []
    for quarter, held_ref in enumerate(held_refs):
        start, finish = fetches(
            quarter, 0, info, parts_ref, momentum_ref, held_ref, band_refs, sems.at[quarter], band_sems
        )
        start()
        pending.append(finish)
    for finish in pending:
        lax.fori_loop(0, 8, lambda index, carry: (finish(index), carry)[1], 0)


def keep_call(info, parts, momentum, codes):
    size = 8 * QUARTER * FF
    whole = pl.BlockSpec(memory_space=pltpu.VMEM)
    return pl.pallas_call(
        keep_kernel,
        in_specs=[
            pl.BlockSpec(memory_space=pltpu.SMEM),
            pl.BlockSpec(memory_space=pltpu.HBM),
            pl.BlockSpec(memory_space=pltpu.HBM),
        ]
        + [pl.BlockSpec(memory_space=pl.ANY)] * 4,
        out_specs=[whole] * 4,
        scratch_shapes=[
            pltpu.VMEM((8, BAND, FF), jnp.bfloat16),
            pltpu.SemaphoreType.DMA((4, 8)),
            pltpu.SemaphoreType.DMA((8,)),
        ],
        out_shape=[jax.ShapeDtypeStruct((8, QUARTER, FF), jnp.float32)] * 4,
        compiler_params=pltpu.CompilerParams(vmem_limit_bytes=32 * 1024 * 1024),
        cost_estimate=pl.CostEstimate(flops=size, bytes_accessed=size * 16, transcendentals=0),
        name="keep",
    )(info, parts, momentum, *codes)


def step_kernel(step, kept_ref, *refs):
    received, out_ref = refs[:step], refs[step]
    count = out_ref.shape[0]

    def expert(index, carry):
        for start in range(0, QUARTER, STRIP):
            rows = pl.ds(start, STRIP)
            value = kept_ref[count + index, rows]
            for turn, ref in enumerate(received):
                value = value + decode(ref[count + index, rows], SHIFTS[turn])
            out_ref[index, rows] = encode(value, SHIFTS[step])
        return carry

    lax.fori_loop(0, count, expert, 0)


def step_call(quarter, step, kept, received):
    count = 8 >> step
    size = count * QUARTER * FF
    whole = pl.BlockSpec(memory_space=pltpu.VMEM)
    return pl.pallas_call(
        functools.partial(step_kernel, step),
        in_specs=[whole] * (1 + step),
        out_specs=whole,
        out_shape=jax.ShapeDtypeStruct((count, QUARTER, FF), jnp.bfloat16),
        compiler_params=pltpu.CompilerParams(vmem_limit_bytes=8 * 1024 * 1024),
        cost_estimate=pl.CostEstimate(
            flops=size * 16, bytes_accessed=size * (6 + 2 * step), transcendentals=2 * size * step
        ),
        name=f"codes_q{quarter}_s{step}",
    )(kept, *received)


def halves(value):
    high = value.astype(jnp.bfloat16)
    return high, (value - high.astype(jnp.float32)).astype(jnp.bfloat16)


def dot(left, right):
    return jnp.dot(left, right, preferred_element_type=jnp.float32)


def product(left, right):
    return dot(left[0], right[0]) + (dot(left[0], right[1]) + dot(left[1], right[0]))


def iterate_kernel(*refs):
    kept_refs, received, out_ref, high_ref, low_ref, sum_ref = refs[:4], refs[4:20], *refs[20:]
    for quarter, kept_ref in enumerate(kept_refs):
        mine = received[4 * quarter : 4 * quarter + 4]
        for start in range(0, QUARTER, STRIP):
            value = kept_ref[0, pl.ds(start, STRIP)]
            for turn, ref in enumerate(mine):
                value = value + decode(ref[0, pl.ds(start, STRIP)], SHIFTS[turn])
            sum_ref[pl.ds(quarter * QUARTER + start, STRIP)] = value

    gram = jnp.zeros((FF, FF), jnp.float32)
    cross = jnp.zeros((FF, FF), jnp.float32)
    rows_in = (((0,), (0,)), ((), ()))
    for quarter in range(4):
        rows = pl.ds(quarter * QUARTER, QUARTER)
        high, low = halves(sum_ref[rows])
        high_ref[rows] = high
        low_ref[rows] = low
        gram += lax.dot_general(high, high, rows_in, preferred_element_type=jnp.float32)
        cross += lax.dot_general(high, low, rows_in, preferred_element_type=jnp.float32)
    gram += cross + cross.T

    row = lax.broadcasted_iota(jnp.int32, (FF, FF), 0)
    column = lax.broadcasted_iota(jnp.int32, (FF, FF), 1)
    on_diagonal = row == column
    squares = jnp.sum(jnp.where(on_diagonal, gram, 0.0))
    scale = 1.0 / (jnp.sqrt(jnp.full((1, 1), squares)) + 1e-07 / GAIN)
    a = gram * scale * scale
    power = None
    for turn in range(NS_ITERS):
        a_split = halves(a)
        b = -4.775 * a + 2.0315 * product(a_split, a_split)
        b_split = halves(b)
        if power is None:
            power = jnp.where(on_diagonal, 3.4445, 0.0) + b
        else:
            power = 3.4445 * power + product(halves(power), b_split)
        if turn < NS_ITERS - 1:
            once = 3.4445 * a + product(a_split, b_split)
            a = 3.4445 * once + product(halves(once), b_split)
    power_split = halves(power * (scale * float(max(D, FF)) ** 0.5))
    for quarter in range(4):
        rows = pl.ds(quarter * QUARTER, QUARTER)
        out_ref[rows] = product((high_ref[rows], low_ref[rows]), power_split).astype(jnp.bfloat16)


def iterate_call(kept, received):
    whole = pl.BlockSpec(memory_space=pltpu.VMEM)
    return pl.pallas_call(
        iterate_kernel,
        in_specs=[whole] * (len(kept) + len(received)),
        out_specs=whole,
        scratch_shapes=[
            pltpu.VMEM((D, FF), jnp.bfloat16),
            pltpu.VMEM((D, FF), jnp.bfloat16),
            pltpu.VMEM((D, FF), jnp.float32),
        ],
        out_shape=jax.ShapeDtypeStruct((D, FF), jnp.bfloat16),
        compiler_params=pltpu.CompilerParams(vmem_limit_bytes=16 * 1024 * 1024),
        cost_estimate=pl.CostEstimate(
            flops=3 * 2 * FF * FF * (17 * FF + 2 * D), bytes_accessed=6 * 1024 * 1024, transcendentals=0
        ),
        name="newton_schulz",
    )(*kept, *received)


def local(grad_parts, momentum):
    parts = grad_parts[0]
    info = jnp.asarray(expert_table())[lax.axis_index("rep")]
    codes = first_calls(info, parts, momentum)
    kept = keep_call(info, parts, momentum, codes)
    received = [[] for _ in range(4)]
    for step in range(4):
        for quarter in range(4):
            if step:
                codes[quarter] = step_call(quarter, step, kept[quarter], received[quarter])
            received[quarter].append(
                lax.ppermute(codes[quarter], "rep", partners(ORDERS[quarter][step]))
            )
    update = iterate_call(kept, sum(received, []))
    return lax.all_to_all(update.reshape(16, BAND, FF), "rep", split_axis=0, concat_axis=0, tiled=True)


def solution(mesh):
    return jax.shard_map(
        local,
        mesh=mesh,
        in_specs=(P("rep", "exp", None, None), P("exp", "rep", None)),
        out_specs=P("exp", "rep", None),
        check_vma=False,
    )
```

time: 177 us -> 127 us (0.72)
  Pallas kernels: 94.4 us -> 43.1 us
  local copies, waits for them, and re-layouts: 14 us -> 2.71 us
  waiting for transfers between devices: 30.5 us -> 39.4 us
  starting transfers between devices: 17.8 us -> 25.3 us
  other arithmetic: 2.4 us -> 0 us
    pallas_call x17 -> x18, Pallas kernels: 94.4 us -> 43.1 us  [the longest x1 16.5 us: iterate_call(): pl.pallas_call(iterate_kernel, in_specs=[whole] * (len(kept) + len(receiv...]
    unnamed x37 -> x5, local copies, waits for them, and re-layouts: 13.4 us -> 2.02 us
    ppermute x16, waiting for transfers between devices: 30.5 us -> 39.4 us  [local(): lax.ppermute(codes[quarter], 'rep', partners(ORDERS[quarter][step]))]
    ppermute x16, starting transfers between devices: 17.8 us -> 25.3 us  [local(): lax.ppermute(codes[quarter], 'rep', partners(ORDERS[quarter][step]))]
    concatenate x4 -> x0, other arithmetic: 2.4 us -> none  [local(): infos = [jnp.concatenate([table[quarter], place]) for quarter in range(4)]]
  transfers between devices with their start and end apart: 16 -> 16, of which waited for: 7 -> 10; matrix products, arithmetic and copies ran while one was open for 1% -> 0% of each run, Pallas kernels for 39% -> 17%
where the time goes in v1:
time: 127 us
  Pallas kernels  43.1 us (34%)
  waiting for transfers between devices  39.4 us (31%)
  starting transfers between devices  25.3 us (20%)
  blocking collectives  16.4 us (13%)
  local copies, waits for them, and re-layouts  2.71 us (2%)
    ppermute x16, waiting for transfers between devices, local(): lax.ppermute(codes[quarter], 'rep', partners(ORDERS[quarter][step]))  39.4 us
    ppermute x16, starting transfers between devices, local(): lax.ppermute(codes[quarter], 'rep', partners(ORDERS[quarter][step]))  25.3 us
    pallas_call x1, Pallas kernels, iterate_call(): pl.pallas_call(iterate_kernel, in_specs=[whole] * (len(kept) + len(receiv...  16.5 us
    all_to_all x1, blocking collectives, local(): lax.all_to_all(update.reshape(16, BAND, FF), 'rep', split_axis=0, concat_...  16.4 us
    pallas_call x4, Pallas kernels, first_calls(): pl.pallas_call(first_kernel if held is None else functools.partial(later_...  12.3 us
    pallas_call x12, Pallas kernels, step_call(): pl.pallas_call(functools.partial(step_kernel, step), in_specs=[whole] * (...  8.7 us
    pallas_call x1, Pallas kernels, keep_call(): pl.pallas_call(keep_kernel, in_specs=[pl.BlockSpec(memory_space=pltpu.SME...  5.6 us
  transfers between devices with their start and end apart: 16, of which 10 were waited for; matrix products, arithmetic and copies ran while one was open for 0% of the time, Pallas kernels for 17%

profile of v1, /device:TPU:0, one launch (start us, length us, event | category | flops | bytes accessed | tf_op | source)
XLA Modules:
  0.0 127.0 jit_solution(7893231720471035222)
XLA Ops:
  0.0 0.7 dynamic-slice_bitcast_fusion.info
  0.7 0.0 copy-start
  0.7 1.1 copy-done
  1.8 4.8 %first_q3.1 = (bf16[8,256,384]{2,1,0:T(8,128)(2,1)}, f32[8,256,384]{2,1,0:T(8,128)S(1)}) custom-call(s32[128]{0:T(128)S(1)} %dynamic-slice_bitcast_fusion.info, f32[16,1024,384]{2,1,0:T(8,128)} %bitcast.5, bf16[16,64,384]{2,1,0:T(8,128)(2,1)S(1)} %copy-done), custom_call_target="tpu_custom_call" | custom-call | flops 7864320 | bytes 4718592 | tf_op jit(solution)/shard_map/first_q3/pallas_call | solution.py:155
  6.6 1.7 %collective-permute-start.12 = (bf16[8,256,384]{2,1,0:T(8,128)(2,1)}, bf16[8,256,384]{2,1,0:T(8,128)(2,1)S(1)}, u32[]{:S(2)}, u32[]{:S(2)}) collective-permute-start(bf16[8,256,384]{2,1,0:T(8,128)(2,1)} %get-tuple-element.20.refs_3_), channel_id=1, source_target_pairs={{0,8},{8,0},{16,24},{24,16},{32,40},{40,32},{48,56},{56,48},{64,72... | collective-permute-start | bytes 4718600 | tf_op jit(solution)/shard_map/ppermute | solution.py:336
  8.3 2.5 %first_q2.1 = (bf16[8,256,384]{2,1,0:T(8,128)(2,1)S(1)}, f32[8,256,384]{2,1,0:T(8,128)S(1)}) custom-call(s32[128]{0:T(128)S(1)} %dynamic-slice_bitcast_fusion.info, f32[16,1024,384]{2,1,0:T(8,128)} %bitcast.6, bf16[16,64,384]{2,1,0:T(8,128)(2,1)S(1)} %copy-done, f32[8,256,384]{2,1,0:T(8,128)S(1)} %get-tuple-element.15.held_ref), custom_call_target="tpu_custom_call" | custom-call | flops 7864320 | bytes 4718592 | tf_op jit(solution)/shard_map/first_q2/pallas_call | solution.py:155
  10.8 1.7 %collective-permute-start.8 = (bf16[8,256,384]{2,1,0:T(8,128)(2,1)S(1)}, bf16[8,256,384]{2,1,0:T(8,128)(2,1)S(1)}, u32[]{:S(2)}, u32[]{:S(2)}) collective-permute-start(bf16[8,256,384]{2,1,0:T(8,128)(2,1)S(1)} %get-tuple-element.19.refs_2_), channel_id=1, source_target_pairs={{0,32},{8,40},{16,48},{24,56},{32,0},{40,8},{48,16},{56,24},{64,96... | collective-permute-start | bytes 4718600 | tf_op jit(solution)/shard_map/ppermute | solution.py:336
  12.5 3.7 %first_q1.1 = (bf16[8,256,384]{2,1,0:T(8,128)(2,1)}, f32[8,256,384]{2,1,0:T(8,128)S(1)}) custom-call(s32[128]{0:T(128)S(1)} %dynamic-slice_bitcast_fusion.info, f32[16,1024,384]{2,1,0:T(8,128)} %bitcast.7, bf16[16,64,384]{2,1,0:T(8,128)(2,1)S(1)} %copy-done, f32[8,256,384]{2,1,0:T(8,128)S(1)} %get-tuple-element.16.held_ref), custom_call_target="tpu_custom_call" | custom-call | flops 7864320 | bytes 4718592 | tf_op jit(solution)/shard_map/first_q1/pallas_call | solution.py:155
  16.1 2.2 %collective-permute-start.4 = (bf16[8,256,384]{2,1,0:T(8,128)(2,1)}, bf16[8,256,384]{2,1,0:T(8,128)(2,1)S(1)}, u32[]{:S(2)}, u32[]{:S(2)}) collective-permute-start(bf16[8,256,384]{2,1,0:T(8,128)(2,1)} %get-tuple-element.18.refs_1_), channel_id=1, source_target_pairs={{0,24},{8,16},{16,8},{24,0},{32,56},{40,48},{48,40},{56,32},{64,88... | collective-permute-start | bytes 4718600 | tf_op jit(solution)/shard_map/ppermute | solution.py:336
  18.3 0.0 copy-start.1
  18.3 1.4 %first_q0.1.refs_0_ = bf16[8,256,384]{2,1,0:T(8,128)(2,1)S(1)} custom-call(s32[128]{0:T(128)S(1)} %dynamic-slice_bitcast_fusion.info, f32[16,1024,384]{2,1,0:T(8,128)} %bitcast.8, bf16[16,64,384]{2,1,0:T(8,128)(2,1)S(1)} %copy-done, f32[8,256,384]{2,1,0:T(8,128)S(1)} %get-tuple-element.17.held_ref), custom_call_target="tpu_custom_call" | custom-call | flops 7864320 | bytes 4718592 | tf_op jit(solution)/shard_map/first_q0/pallas_call | solution.py:155
  19.7 2.2 %collective-permute-start = (bf16[8,256,384]{2,1,0:T(8,128)(2,1)S(1)}, bf16[8,256,384]{2,1,0:T(8,128)(2,1)S(1)}, u32[]{:S(2)}, u32[]{:S(2)}) collective-permute-start(bf16[8,256,384]{2,1,0:T(8,128)(2,1)S(1)} %first_q0.1.refs_0_), channel_id=1, source_target_pairs={{0,96},{8,104},{16,112},{24,120},{32,64},{40,72},{48,80},{56,88},{... | collective-permute-start | bytes 4718600 | tf_op jit(solution)/shard_map/ppermute | solution.py:336
  21.9 0.0 copy-done.1
  21.9 5.6 %keep.1 = (f32[8,256,384]{2,1,0:T(8,128)S(1)}, f32[8,256,384]{2,1,0:T(8,128)S(1)}, f32[8,256,384]{2,1,0:T(8,128)S(1)}, f32[8,256,384]{2,1,0:T(8,128)S(1)}) custom-call(s32[128]{0:T(128)S(1)} %dynamic-slice_bitcast_fusion.info, f32[16,1024,384]{2,1,0:T(8,128)} %bitcast.9, bf16[16,64,384]{2,1,0:T(8,128)(2,1)S(1)} %copy-done.1, ...), custom_call_target="tpu_custom_call" | custom-call | flops 786432 | bytes 12582912 | tf_op jit(solution)/shard_map/keep/pallas_call | solution.py:192
  27.5 15.3 %collective-permute-done.12.refs_0_.refs_16_ = bf16[8,256,384]{2,1,0:T(8,128)(2,1)S(1)} collective-permute-done((bf16[8,256,384]{2,1,0:T(8,128)(2,1)}, bf16[8,256,384]{2,1,0:T(8,128)(2,1)S(1)}, u32[]{:S(2)}, u32[]{:S(2)}) %collective-permute-start.12) | collective-permute-done | bytes 1572896 | tf_op jit(solution)/shard_map/ppermute | solution.py:336
  42.9 1.0 codes_q3_s1.1
  43.8 2.0 %collective-permute-start.13 = (bf16[4,256,384]{2,1,0:T(8,128)(2,1)S(1)}, bf16[4,256,384]{2,1,0:T(8,128)(2,1)S(1)}, u32[]{:S(2)}, u32[]{:S(2)}) collective-permute-start(bf16[4,256,384]{2,1,0:T(8,128)(2,1)S(1)} %codes_q3_s1.1), channel_id=1, source_target_pairs={{0,32},{8,40},{16,48},{24,56},{32,0},{40,8},{48,16},{56,24},{64,96... | collective-permute-start | bytes 2359304 | tf_op jit(solution)/shard_map/ppermute | solution.py:336
  45.8 1.9 %collective-permute-done.8.refs_0_.refs_12_ = bf16[8,256,384]{2,1,0:T(8,128)(2,1)S(1)} collective-permute-done((bf16[8,256,384]{2,1,0:T(8,128)(2,1)S(1)}, bf16[8,256,384]{2,1,0:T(8,128)(2,1)S(1)}, u32[]{:S(2)}, u32[]{:S(2)}) %collective-permute-start.8) | collective-permute-done | bytes 1572896 | tf_op jit(solution)/shard_map/ppermute | solution.py:336
  47.7 1.0 codes_q2_s1.1
  48.7 1.4 %collective-permute-start.9 = (bf16[4,256,384]{2,1,0:T(8,128)(2,1)S(1)}, bf16[4,256,384]{2,1,0:T(8,128)(2,1)S(1)}, u32[]{:S(2)}, u32[]{:S(2)}) collective-permute-start(bf16[4,256,384]{2,1,0:T(8,128)(2,1)S(1)} %codes_q2_s1.1), channel_id=1, source_target_pairs={{0,24},{8,16},{16,8},{24,0},{32,56},{40,48},{48,40},{56,32},{64,88... | collective-permute-start | bytes 2359304 | tf_op jit(solution)/shard_map/ppermute | solution.py:336
  50.1 4.9 %collective-permute-done.4.refs_0_.refs_8_ = bf16[8,256,384]{2,1,0:T(8,128)(2,1)S(1)} collective-permute-done((bf16[8,256,384]{2,1,0:T(8,128)(2,1)}, bf16[8,256,384]{2,1,0:T(8,128)(2,1)S(1)}, u32[]{:S(2)}, u32[]{:S(2)}) %collective-permute-start.4) | collective-permute-done | bytes 1572896 | tf_op jit(solution)/shard_map/ppermute | solution.py:336
  55.0 1.0 codes_q1_s1.1
  55.9 2.2 %collective-permute-start.5 = (bf16[4,256,384]{2,1,0:T(8,128)(2,1)S(1)}, bf16[4,256,384]{2,1,0:T(8,128)(2,1)S(1)}, u32[]{:S(2)}, u32[]{:S(2)}) collective-permute-start(bf16[4,256,384]{2,1,0:T(8,128)(2,1)S(1)} %codes_q1_s1.1), channel_id=1, source_target_pairs={{0,96},{8,104},{16,112},{24,120},{32,64},{40,72},{48,80},{56,88},{... | collective-permute-start | bytes 2359304 | tf_op jit(solution)/shard_map/ppermute | solution.py:336
  58.2 0.0 collective-permute-done.refs_0_.refs_4_
  58.2 0.9 codes_q0_s1.1
  59.1 0.1 collective-permute-start.1
  59.2 4.3 %collective-permute-done.13.refs_1_.refs_17_ = bf16[4,256,384]{2,1,0:T(8,128)(2,1)S(1)} collective-permute-done((bf16[4,256,384]{2,1,0:T(8,128)(2,1)S(1)}, bf16[4,256,384]{2,1,0:T(8,128)(2,1)S(1)}, u32[]{:S(2)}, u32[]{:S(2)}) %collective-permute-start.13) | collective-permute-done | bytes 786464 | tf_op jit(solution)/shard_map/ppermute | solution.py:336
  63.6 0.7 codes_q3_s2.1
  64.3 2.2 %collective-permute-start.14 = (bf16[2,256,384]{2,1,0:T(8,128)(2,1)S(1)}, bf16[2,256,384]{2,1,0:T(8,128)(2,1)S(1)}, u32[]{:S(2)}, u32[]{:S(2)}) collective-permute-start(bf16[2,256,384]{2,1,0:T(8,128)(2,1)S(1)} %codes_q3_s2.1), channel_id=1, source_target_pairs={{0,24},{8,16},{16,8},{24,0},{32,56},{40,48},{48,40},{56,32},{64,88... | collective-permute-start | bytes 1179656 | tf_op jit(solution)/shard_map/ppermute | solution.py:336
  66.5 5.4 %collective-permute-done.9.refs_1_.refs_13_ = bf16[4,256,384]{2,1,0:T(8,128)(2,1)S(1)} collective-permute-done((bf16[4,256,384]{2,1,0:T(8,128)(2,1)S(1)}, bf16[4,256,384]{2,1,0:T(8,128)(2,1)S(1)}, u32[]{:S(2)}, u32[]{:S(2)}) %collective-permute-start.9) | collective-permute-done | bytes 786464 | tf_op jit(solution)/shard_map/ppermute | solution.py:336
  71.8 0.7 codes_q2_s2.1
  72.6 2.2 %collective-permute-start.10 = (bf16[2,256,384]{2,1,0:T(8,128)(2,1)S(1)}, bf16[2,256,384]{2,1,0:T(8,128)(2,1)S(1)}, u32[]{:S(2)}, u32[]{:S(2)}) collective-permute-start(bf16[2,256,384]{2,1,0:T(8,128)(2,1)S(1)} %codes_q2_s2.1), channel_id=1, source_target_pairs={{0,96},{8,104},{16,112},{24,120},{32,64},{40,72},{48,80},{56,88},{... | collective-permute-start | bytes 1179656 | tf_op jit(solution)/shard_map/ppermute | solution.py:336
  74.8 0.0 collective-permute-done.5.refs_1_.refs_9_
  74.8 0.7 codes_q1_s2.1
  75.5 0.1 collective-permute-start.6
  75.6 0.0 collective-permute-done.1.refs_1_.refs_5_
  75.6 0.7 codes_q0_s2.1
  76.4 0.8 collective-permute-start.2
  77.2 1.3 collective-permute-done.14.refs_2_.refs_18_
  78.5 0.5 codes_q3_s3.1
  79.0 2.2 %collective-permute-start.15 = (bf16[1,256,384]{2,1,0:T(8,128)(2,1)S(1)}, bf16[1,256,384]{2,1,0:T(8,128)(2,1)S(1)}, u32[]{:S(2)}, u32[]{:S(2)}) collective-permute-start(bf16[1,256,384]{2,1,0:T(8,128)(2,1)S(1)} %codes_q3_s3.1), channel_id=1, source_target_pairs={{0,96},{8,104},{16,112},{24,120},{32,64},{40,72},{48,80},{56,88},{... | collective-permute-start | bytes 589832 | tf_op jit(solution)/shard_map/ppermute | solution.py:336
  81.2 0.9 collective-permute-done.10.refs_2_.refs_14_
  82.1 0.5 codes_q2_s3.1
  82.6 1.0 collective-permute-start.11
  83.6 0.7 collective-permute-done.6.refs_2_.refs_10_
  84.3 0.5 codes_q1_s3.1
  84.8 0.8 collective-permute-start.7
  85.6 0.0 collective-permute-done.2.refs_2_.refs_6_
  85.6 0.5 codes_q0_s3.1
  86.1 2.4 %collective-permute-start.3 = (bf16[1,256,384]{2,1,0:T(8,128)(2,1)S(1)}, bf16[1,256,384]{2,1,0:T(8,128)(2,1)S(1)}, u32[]{:S(2)}, u32[]{:S(2)}) collective-permute-start(bf16[1,256,384]{2,1,0:T(8,128)(2,1)S(1)} %codes_q0_s3.1), channel_id=1, source_target_pairs={{0,24},{8,16},{16,8},{24,0},{32,56},{40,48},{48,40},{56,32},{64,88... | collective-permute-start | bytes 589832 | tf_op jit(solution)/shard_map/ppermute | solution.py:336
  88.5 0.0 collective-permute-done.15.refs_19_
  88.5 0.0 collective-permute-done.11.refs_15_
  88.5 2.0 %collective-permute-done.7.refs_11_ = bf16[1,256,384]{2,1,0:T(8,128)(2,1)S(1)} collective-permute-done((bf16[1,256,384]{2,1,0:T(8,128)(2,1)S(1)}, bf16[1,256,384]{2,1,0:T(8,128)(2,1)S(1)}, u32[]{:S(2)}, u32[]{:S(2)}) %collective-permute-start.7) | collective-permute-done | bytes 196640 | tf_op jit(solution)/shard_map/ppermute | solution.py:336
  90.5 2.7 %collective-permute-done.3.refs_7_ = bf16[1,256,384]{2,1,0:T(8,128)(2,1)S(1)} collective-permute-done((bf16[1,256,384]{2,1,0:T(8,128)(2,1)S(1)}, bf16[1,256,384]{2,1,0:T(8,128)(2,1)S(1)}, u32[]{:S(2)}, u32[]{:S(2)}) %collective-permute-start.3) | collective-permute-done | bytes 196640 | tf_op jit(solution)/shard_map/ppermute | solution.py:336
  93.2 16.5 %newton_schulz.1 = bf16[1024,384]{1,0:T(8,128)(2,1)S(1)} custom-call(f32[8,256,384]{2,1,0:T(8,128)S(1)} %get-tuple-element.21.kept_ref.refs_0_, f32[8,256,384]{2,1,0:T(8,128)S(1)} %get-tuple-element.22.kept_ref.refs_1_, f32[8,256,384]{2,1,0:T(8,128)S(1)} %get-tuple-element.23.kept_ref.refs_2_, f32[8,256,384]{2,1,0:T(8,128)S(1)} %get-tuple-element.24.kept_ref.refs_3_, ...), custom_call_target="tpu_custom_call" | custom-call | flops 7587495936 | bytes 6291456 | tf_op jit(solution)/shard_map/newton_schulz/pallas_call | solution.py:307
  109.7 16.4 %all_to_all.5 = bf16[16,64,384]{2,1,0:T(8,128)(2,1)S(1)} all-to-all(bf16[16,64,384]{2,1,0:T(8,128)(2,1)S(1)} %bitcast.4), channel_id=1, replica_groups=mesh['rep'=16,'exp'=8] {'rep'}, dimensions={0} | all-to-all | bytes 1572864 | tf_op jit(solution)/shard_map/all_to_all | solution.py:339
  126.1 0.9 copy.5
Async XLA Ops:
  0.7 1.1 copy-start
  6.6 36.3 %collective-permute-start.12 = (bf16[8,256,384]{2,1,0:T(8,128)(2,1)}, bf16[8,256,384]{2,1,0:T(8,128)(2,1)S(1)}, u32[]{:S(2)}, u32[]{:S(2)}) collective-permute-start(bf16[8,256,384]{2,1,0:T(8,128)(2,1)} %get-tuple-element.20.refs_3_), channel_id=1, source_target_pairs={{0,8},{8,0},{16,24},{24,16},{32,40},{40,32},{48,56},{56,48},{64,72... | collective-permute-start | bytes 4718600 | tf_op jit(solution)/shard_map/ppermute | solution.py:336
  10.8 37.0 %collective-permute-start.8 = (bf16[8,256,384]{2,1,0:T(8,128)(2,1)S(1)}, bf16[8,256,384]{2,1,0:T(8,128)(2,1)S(1)}, u32[]{:S(2)}, u32[]{:S(2)}) collective-permute-start(bf16[8,256,384]{2,1,0:T(8,128)(2,1)S(1)} %get-tuple-element.19.refs_2_), channel_id=1, source_target_pairs={{0,32},{8,40},{16,48},{24,56},{32,0},{40,8},{48,16},{56,24},{64,96... | collective-permute-start | bytes 4718600 | tf_op jit(solution)/shard_map/ppermute | solution.py:336
  16.1 38.8 %collective-permute-start.4 = (bf16[8,256,384]{2,1,0:T(8,128)(2,1)}, bf16[8,256,384]{2,1,0:T(8,128)(2,1)S(1)}, u32[]{:S(2)}, u32[]{:S(2)}) collective-permute-start(bf16[8,256,384]{2,1,0:T(8,128)(2,1)} %get-tuple-element.18.refs_1_), channel_id=1, source_target_pairs={{0,24},{8,16},{16,8},{24,0},{32,56},{40,48},{48,40},{56,32},{64,88... | collective-permute-start | bytes 4718600 | tf_op jit(solution)/shard_map/ppermute | solution.py:336
  18.3 3.6 %copy-start.1 = (bf16[16,64,384]{2,1,0:T(8,128)(2,1)S(1)}, bf16[16,64,384]{2,1,0:T(8,128)(2,1)}, u32[]{:S(2)}) copy-start(bf16[16,64,384]{2,1,0:T(8,128)(2,1)} %momentum_ref.9) | copy-start | bytes 2359300
  19.7 38.5 %collective-permute-start = (bf16[8,256,384]{2,1,0:T(8,128)(2,1)S(1)}, bf16[8,256,384]{2,1,0:T(8,128)(2,1)S(1)}, u32[]{:S(2)}, u32[]{:S(2)}) collective-permute-start(bf16[8,256,384]{2,1,0:T(8,128)(2,1)S(1)} %first_q0.1.refs_0_), channel_id=1, source_target_pairs={{0,96},{8,104},{16,112},{24,120},{32,64},{40,72},{48,80},{56,88},{... | collective-permute-start | bytes 4718600 | tf_op jit(solution)/shard_map/ppermute | solution.py:336
  43.8 19.7 %collective-permute-start.13 = (bf16[4,256,384]{2,1,0:T(8,128)(2,1)S(1)}, bf16[4,256,384]{2,1,0:T(8,128)(2,1)S(1)}, u32[]{:S(2)}, u32[]{:S(2)}) collective-permute-start(bf16[4,256,384]{2,1,0:T(8,128)(2,1)S(1)} %codes_q3_s1.1), channel_id=1, source_target_pairs={{0,32},{8,40},{16,48},{24,56},{32,0},{40,8},{48,16},{56,24},{64,96... | collective-permute-start | bytes 2359304 | tf_op jit(solution)/shard_map/ppermute | solution.py:336
  48.7 23.1 %collective-permute-start.9 = (bf16[4,256,384]{2,1,0:T(8,128)(2,1)S(1)}, bf16[4,256,384]{2,1,0:T(8,128)(2,1)S(1)}, u32[]{:S(2)}, u32[]{:S(2)}) collective-permute-start(bf16[4,256,384]{2,1,0:T(8,128)(2,1)S(1)} %codes_q2_s1.1), channel_id=1, source_target_pairs={{0,24},{8,16},{16,8},{24,0},{32,56},{40,48},{48,40},{56,32},{64,88... | collective-permute-start | bytes 2359304 | tf_op jit(solution)/shard_map/ppermute | solution.py:336
  55.9 18.9 %collective-permute-start.5 = (bf16[4,256,384]{2,1,0:T(8,128)(2,1)S(1)}, bf16[4,256,384]{2,1,0:T(8,128)(2,1)S(1)}, u32[]{:S(2)}, u32[]{:S(2)}) collective-permute-start(bf16[4,256,384]{2,1,0:T(8,128)(2,1)S(1)} %codes_q1_s1.1), channel_id=1, source_target_pairs={{0,96},{8,104},{16,112},{24,120},{32,64},{40,72},{48,80},{56,88},{... | collective-permute-start | bytes 2359304 | tf_op jit(solution)/shard_map/ppermute | solution.py:336
  59.1 16.5 %collective-permute-start.1 = (bf16[4,256,384]{2,1,0:T(8,128)(2,1)S(1)}, bf16[4,256,384]{2,1,0:T(8,128)(2,1)S(1)}, u32[]{:S(2)}, u32[]{:S(2)}) collective-permute-start(bf16[4,256,384]{2,1,0:T(8,128)(2,1)S(1)} %codes_q0_s1.1), channel_id=1, source_target_pairs={{0,8},{8,0},{16,24},{24,16},{32,40},{40,32},{48,56},{56,48},{64,72... | collective-permute-start | bytes 2359304 | tf_op jit(solution)/shard_map/ppermute | solution.py:336
  64.3 14.2 %collective-permute-start.14 = (bf16[2,256,384]{2,1,0:T(8,128)(2,1)S(1)}, bf16[2,256,384]{2,1,0:T(8,128)(2,1)S(1)}, u32[]{:S(2)}, u32[]{:S(2)}) collective-permute-start(bf16[2,256,384]{2,1,0:T(8,128)(2,1)S(1)} %codes_q3_s2.1), channel_id=1, source_target_pairs={{0,24},{8,16},{16,8},{24,0},{32,56},{40,48},{48,40},{56,32},{64,88... | collective-permute-start | bytes 1179656 | tf_op jit(solution)/shard_map/ppermute | solution.py:336
  72.6 9.5 %collective-permute-start.10 = (bf16[2,256,384]{2,1,0:T(8,128)(2,1)S(1)}, bf16[2,256,384]{2,1,0:T(8,128)(2,1)S(1)}, u32[]{:S(2)}, u32[]{:S(2)}) collective-permute-start(bf16[2,256,384]{2,1,0:T(8,128)(2,1)S(1)} %codes_q2_s2.1), channel_id=1, source_target_pairs={{0,96},{8,104},{16,112},{24,120},{32,64},{40,72},{48,80},{56,88},{... | collective-permute-start | bytes 1179656 | tf_op jit(solution)/shard_map/ppermute | solution.py:336
  75.5 8.7 %collective-permute-start.6 = (bf16[2,256,384]{2,1,0:T(8,128)(2,1)S(1)}, bf16[2,256,384]{2,1,0:T(8,128)(2,1)S(1)}, u32[]{:S(2)}, u32[]{:S(2)}) collective-permute-start(bf16[2,256,384]{2,1,0:T(8,128)(2,1)S(1)} %codes_q1_s2.1), channel_id=1, source_target_pairs={{0,8},{8,0},{16,24},{24,16},{32,40},{40,32},{48,56},{56,48},{64,72... | collective-permute-start | bytes 1179656 | tf_op jit(solution)/shard_map/ppermute | solution.py:336
  76.4 9.2 %collective-permute-start.2 = (bf16[2,256,384]{2,1,0:T(8,128)(2,1)S(1)}, bf16[2,256,384]{2,1,0:T(8,128)(2,1)S(1)}, u32[]{:S(2)}, u32[]{:S(2)}) collective-permute-start(bf16[2,256,384]{2,1,0:T(8,128)(2,1)S(1)} %codes_q0_s2.1), channel_id=1, source_target_pairs={{0,32},{8,40},{16,48},{24,56},{32,0},{40,8},{48,16},{56,24},{64,96... | collective-permute-start | bytes 1179656 | tf_op jit(solution)/shard_map/ppermute | solution.py:336
  79.0 9.5 %collective-permute-start.15 = (bf16[1,256,384]{2,1,0:T(8,128)(2,1)S(1)}, bf16[1,256,384]{2,1,0:T(8,128)(2,1)S(1)}, u32[]{:S(2)}, u32[]{:S(2)}) collective-permute-start(bf16[1,256,384]{2,1,0:T(8,128)(2,1)S(1)} %codes_q3_s3.1), channel_id=1, source_target_pairs={{0,96},{8,104},{16,112},{24,120},{32,64},{40,72},{48,80},{56,88},{... | collective-permute-start | bytes 589832 | tf_op jit(solution)/shard_map/ppermute | solution.py:336
  82.6 5.9 %collective-permute-start.11 = (bf16[1,256,384]{2,1,0:T(8,128)(2,1)S(1)}, bf16[1,256,384]{2,1,0:T(8,128)(2,1)S(1)}, u32[]{:S(2)}, u32[]{:S(2)}) collective-permute-start(bf16[1,256,384]{2,1,0:T(8,128)(2,1)S(1)} %codes_q2_s3.1), channel_id=1, source_target_pairs={{0,8},{8,0},{16,24},{24,16},{32,40},{40,32},{48,56},{56,48},{64,72... | collective-permute-start | bytes 589832 | tf_op jit(solution)/shard_map/ppermute | solution.py:336
  84.8 5.7 %collective-permute-start.7 = (bf16[1,256,384]{2,1,0:T(8,128)(2,1)S(1)}, bf16[1,256,384]{2,1,0:T(8,128)(2,1)S(1)}, u32[]{:S(2)}, u32[]{:S(2)}) collective-permute-start(bf16[1,256,384]{2,1,0:T(8,128)(2,1)S(1)} %codes_q1_s3.1), channel_id=1, source_target_pairs={{0,32},{8,40},{16,48},{24,56},{32,0},{40,8},{48,16},{56,24},{64,96... | collective-permute-start | bytes 589832 | tf_op jit(solution)/shard_map/ppermute | solution.py:336
  86.1 7.1 %collective-permute-start.3 = (bf16[1,256,384]{2,1,0:T(8,128)(2,1)S(1)}, bf16[1,256,384]{2,1,0:T(8,128)(2,1)S(1)}, u32[]{:S(2)}, u32[]{:S(2)}) collective-permute-start(bf16[1,256,384]{2,1,0:T(8,128)(2,1)S(1)} %codes_q0_s3.1), channel_id=1, source_target_pairs={{0,24},{8,16},{16,8},{24,0},{32,56},{40,48},{48,40},{56,32},{64,88... | collective-permute-start | bytes 589832 | tf_op jit(solution)/shard_map/ppermute | solution.py:336

commit v2 on v1

v2 whole, which is shorter than its diff:
```python
import functools
import math

import jax
import jax.numpy as jnp
from jax import lax
from jax.experimental import pallas as pl
from jax.experimental.pallas import tpu as pltpu
from jax.sharding import PartitionSpec as P

D = 1024
FF = 384
NS_ITERS = 5
QUARTER = D // 4
STRIP = 64
BAND = 64
SPLIT = 256
GAIN = 1.0 + 0.95
BLEND = 0.95 * 0.95 / GAIN

ORDERS = ((3, 0, 2, 1), (1, 3, 0, 2), (2, 1, 3, 0), (0, 2, 1, 3))
FLIPS = (1, 3, 4, 12)
SHIFTS = (3, 3, 2, 2)
BEND = 2


def partners(bit):
    return [(rep, rep ^ FLIPS[bit]) for rep in range(16)]


def expert_of(quarter, sent, index):
    first, *others = [FLIPS[bit] for bit in ORDERS[quarter]]
    expert = lax.axis_index("rep") ^ (first if sent else 0)
    for place, flip in enumerate(others):
        expert = expert ^ (((index >> (2 - place)) & 1) * flip)
    return expert


def encode(value, shift):
    scaled = value * float(2**shift)
    second = scaled * scaled
    fourth = second * second
    eighth = fourth * fourth
    size = eighth * jnp.maximum(eighth, float(2 ** (8 * BEND)))
    return jnp.where(value < 0, -size, size).astype(jnp.bfloat16)


def decode(code, shift):
    code = code.astype(jnp.float32)
    level = jnp.log(jnp.maximum(jnp.abs(code), float(2.0**-126)))
    steep = level * (-15 / 16 / math.log(2.0)) - float(shift)
    flat = level * (-7 / 8 / math.log(2.0)) - float(shift + BEND)
    return code * jnp.exp2(jnp.minimum(steep, flat))


def fetches(quarter, sent, parts_ref, momentum_ref, held_ref, band_ref, sems, band_sems):
    rows = pl.ds(quarter * QUARTER, QUARTER)
    rep = lax.axis_index("rep")
    has_band = (rep >> 2) == quarter

    def raw(index):
        expert = expert_of(quarter, sent, index)
        return pltpu.make_async_copy(parts_ref.at[expert, rows], held_ref.at[index], sems.at[index])

    def band(index):
        expert = expert_of(quarter, sent, index)
        return pltpu.make_async_copy(momentum_ref.at[expert], band_ref.at[index], band_sems.at[index])

    def start(index):
        @pl.when(has_band)
        def _():
            band(index).start()

        raw(index).start()

    def finish(index):
        raw(index).wait()

        @pl.when(has_band)
        def _():
            band(index).wait()
            rows = pl.ds(pl.multiple_of((rep & 3) * BAND, BAND), BAND)
            held_ref[index, rows] += BLEND * band_ref[index].astype(jnp.float32)

    return start, finish


FETCH_SCRATCH = (
    pltpu.VMEM((8, BAND, FF), jnp.bfloat16),
    pltpu.SemaphoreType.DMA((8,)),
    pltpu.SemaphoreType.DMA((8,)),
)


def encode_expert(held_ref, out_ref, index):
    for start in range(0, QUARTER, STRIP):
        rows = pl.ds(start, STRIP)
        out_ref[index, rows] = encode(held_ref[index, rows], SHIFTS[0])


def loop(body):
    def step(index, carry):
        body(index)
        return carry

    lax.fori_loop(0, 8, step, 0)


def first_kernel(parts_ref, momentum_ref, out_ref, next_ref, held_ref, *scratch):
    start_now, finish_now = fetches(3, True, parts_ref, momentum_ref, held_ref, *scratch[:3])
    start_next, finish_next = fetches(2, True, parts_ref, momentum_ref, next_ref, *scratch[3:])
    loop(start_now)

    def expert(index):
        finish_now(index)
        start_next(index)
        encode_expert(held_ref, out_ref, index)

    loop(expert)
    loop(finish_next)


def later_kernel(quarter, parts_ref, momentum_ref, held_ref, out_ref, *rest):
    last = quarter == 0
    if not last:
        start_next, finish_next = fetches(quarter - 1, True, parts_ref, momentum_ref, *rest)
        loop(start_next)
    loop(functools.partial(encode_expert, held_ref, out_ref))
    if not last:
        loop(finish_next)


def first_calls(parts, momentum):
    size = 8 * QUARTER * FF
    whole = pl.BlockSpec(memory_space=pltpu.VMEM)
    raw = jax.ShapeDtypeStruct((8, QUARTER, FF), jnp.float32)
    codes = [None] * 4
    held = None
    for quarter in (3, 2, 1, 0):
        last = quarter == 0
        results = pl.pallas_call(
            first_kernel if held is None else functools.partial(later_kernel, quarter),
            in_specs=[pl.BlockSpec(memory_space=pltpu.HBM)] * 2 + [whole] * (held is not None),
            out_specs=[whole] * (1 if last else 2),
            scratch_shapes=[pltpu.VMEM((8, QUARTER, FF), jnp.float32)] * (held is None)
            + [*FETCH_SCRATCH] * ((held is None) + (not last)),
            out_shape=[jax.ShapeDtypeStruct((8, QUARTER, FF), jnp.bfloat16)] + [raw] * (not last),
            compiler_params=pltpu.CompilerParams(vmem_limit_bytes=40 * 1024 * 1024),
            cost_estimate=pl.CostEstimate(flops=size * 10, bytes_accessed=size * 6, transcendentals=0),
            name=f"first_q{quarter}",
        )(parts, momentum, *([] if held is None else [held]))
        codes[quarter] = results[0]
        held = results[-1]
    return codes


def keep_kernel(parts_ref, momentum_ref, *refs):
    held_refs, band_refs, sems, band_sems = refs[4:8], *refs[8:]
    pending = []
    for quarter, held_ref in enumerate(held_refs):
        start, finish = fetches(
            quarter, False, parts_ref, momentum_ref, held_ref, band_refs, sems.at[quarter], band_sems
        )
        loop(start)
        pending.append(finish)
    for finish in pending:
        loop(finish)


def keep_call(parts, momentum, codes):
    size = 8 * QUARTER * FF
    whole = pl.BlockSpec(memory_space=pltpu.VMEM)
    return pl.pallas_call(
        keep_kernel,
        in_specs=[pl.BlockSpec(memory_space=pltpu.HBM)] * 2 + [pl.BlockSpec(memory_space=pl.ANY)] * 4,
        out_specs=[whole] * 4,
        scratch_shapes=[
            pltpu.VMEM((8, BAND, FF), jnp.bfloat16),
            pltpu.SemaphoreType.DMA((4, 8)),
            pltpu.SemaphoreType.DMA((8,)),
        ],
        out_shape=[jax.ShapeDtypeStruct((8, QUARTER, FF), jnp.float32)] * 4,
        compiler_params=pltpu.CompilerParams(vmem_limit_bytes=32 * 1024 * 1024),
        cost_estimate=pl.CostEstimate(flops=size, bytes_accessed=size * 16, transcendentals=0),
        name="keep",
    )(parts, momentum, *codes)


def step_kernel(step, kept_ref, *refs):
    received, out_ref = refs[:step], refs[step]
    count = out_ref.shape[0]

    def expert(index, carry):
        for start in range(0, QUARTER, STRIP):
            rows = pl.ds(start, STRIP)
            value = kept_ref[count + index, rows]
            for turn, ref in enumerate(received):
                value = value + decode(ref[count + index, rows], SHIFTS[turn])
            out_ref[index, rows] = encode(value, SHIFTS[step])
        return carry

    lax.fori_loop(0, count, expert, 0)


def step_call(quarter, step, kept, received):
    count = 8 >> step
    size = count * QUARTER * FF
    whole = pl.BlockSpec(memory_space=pltpu.VMEM)
    return pl.pallas_call(
        functools.partial(step_kernel, step),
        in_specs=[whole] * (1 + step),
        out_specs=whole,
        out_shape=jax.ShapeDtypeStruct((count, QUARTER, FF), jnp.bfloat16),
        compiler_params=pltpu.CompilerParams(vmem_limit_bytes=8 * 1024 * 1024),
        cost_estimate=pl.CostEstimate(
            flops=size * 16, bytes_accessed=size * (6 + 2 * step), transcendentals=2 * size * step
        ),
        name=f"codes_q{quarter}_s{step}",
    )(kept, *received)


def halves(value):
    high = value.astype(jnp.bfloat16)
    return high, (value - high.astype(jnp.float32)).astype(jnp.bfloat16)


def dot(left, right):
    return jnp.dot(left, right, preferred_element_type=jnp.float32)


def wide(left):
    return jnp.concatenate([left[0], left[1], left[0]], axis=1)


def tall(right):
    return jnp.concatenate([right[0], right[0], right[1]], axis=0)


def symmetric(left, right):
    left, right = wide(left), tall(right)
    most = dot(left, right[:, :SPLIT])
    corner = dot(left[SPLIT:], right[:, SPLIT:])
    return jnp.concatenate([most, jnp.concatenate([most[SPLIT:].T, corner], axis=0)], axis=1)


def gram_part(kept_refs, received, high_ref, low_ref):
    part = None
    for quarter, kept_ref in enumerate(kept_refs):
        mine = received[4 * quarter : 4 * quarter + 4]
        for start in range(0, QUARTER, STRIP):
            value = kept_ref[0, pl.ds(start, STRIP)]
            for turn, ref in enumerate(mine):
                value = value + decode(ref[0, pl.ds(start, STRIP)], SHIFTS[turn])
            rows = pl.ds(quarter * QUARTER + start, STRIP)
            high_ref[rows], low_ref[rows] = halves(value)
        rows = pl.ds(quarter * QUARTER, QUARTER)
        high = high_ref[rows]
        more = dot(high.T, jnp.concatenate([high, low_ref[rows]], axis=1))
        part = more if part is None else part + more
    return part


def gather_kernel(*refs):
    kept_refs, received, high_ref, low_ref, part_ref = refs[:3], refs[3:15], *refs[15:]
    part_ref[...] = gram_part(kept_refs, received, high_ref, low_ref)


def gather_call(kept, received):
    whole = pl.BlockSpec(memory_space=pltpu.VMEM)
    rows = QUARTER * len(kept)
    split = jax.ShapeDtypeStruct((rows, FF), jnp.bfloat16)
    return pl.pallas_call(
        gather_kernel,
        in_specs=[whole] * (len(kept) + len(received)),
        out_specs=[whole] * 3,
        out_shape=[split, split, jax.ShapeDtypeStruct((FF, 2 * FF), jnp.float32)],
        compiler_params=pltpu.CompilerParams(vmem_limit_bytes=16 * 1024 * 1024),
        cost_estimate=pl.CostEstimate(
            flops=4 * rows * FF * FF, bytes_accessed=16 * rows * FF, transcendentals=8 * rows * FF
        ),
        name="gather",
    )(*kept, *received)


def iterate_kernel(kept_ref, *refs):
    received, early_high, early_low, part_ref, out_ref, high_ref, low_ref = refs[:4], *refs[4:]
    part = part_ref[...] + gram_part([kept_ref], received, high_ref, low_ref)
    gram = part[:, :FF] + (part[:, FF:] + part[:, FF:].T)

    row = lax.broadcasted_iota(jnp.int32, (FF, FF), 0)
    column = lax.broadcasted_iota(jnp.int32, (FF, FF), 1)
    on_diagonal = row == column
    squares = jnp.sum(jnp.where(on_diagonal, gram, 0.0))
    scale = 1.0 / (jnp.sqrt(jnp.full((1, 1), squares)) + 1e-07 / GAIN)
    a = gram * scale * scale
    power = None
    for turn in range(NS_ITERS):
        a_split = halves(a)
        b = -4.775 * a + 2.0315 * symmetric(a_split, a_split)
        b_split = halves(b)
        if power is None:
            power = jnp.where(on_diagonal, 3.4445, 0.0) + b
        else:
            power = 3.4445 * power + symmetric(halves(power), b_split)
        if turn < NS_ITERS - 1:
            once = 3.4445 * a + symmetric(a_split, b_split)
            a = 3.4445 * once + symmetric(halves(once), b_split)
    power_split = tall(halves(power * (scale * float(max(D, FF)) ** 0.5)))
    for quarter in range(4):
        rows = pl.ds(quarter * QUARTER, QUARTER)
        if quarter:
            early = pl.ds((quarter - 1) * QUARTER, QUARTER)
            left = (early_high[early], early_low[early])
        else:
            left = (high_ref[...], low_ref[...])
        out_ref[rows] = dot(wide(left), power_split).astype(jnp.bfloat16)


def iterate_call(kept, received, early):
    whole = pl.BlockSpec(memory_space=pltpu.VMEM)
    return pl.pallas_call(
        iterate_kernel,
        in_specs=[whole] * (1 + len(received) + len(early)),
        out_specs=whole,
        scratch_shapes=[pltpu.VMEM((QUARTER, FF), jnp.bfloat16)] * 2,
        out_shape=jax.ShapeDtypeStruct((D, FF), jnp.bfloat16),
        compiler_params=pltpu.CompilerParams(vmem_limit_bytes=16 * 1024 * 1024),
        cost_estimate=pl.CostEstimate(
            flops=3 * 2 * FF * FF * (17 * FF + D), bytes_accessed=6 * 1024 * 1024, transcendentals=0
        ),
        name="newton_schulz",
    )(kept, *received, *early)


def local(grad_parts, momentum):
    parts = grad_parts[0]
    codes = first_calls(parts, momentum)
    kept = keep_call(parts, momentum, codes)
    received = [[] for _ in range(4)]
    for step in range(4):
        for quarter in range(4):
            if step:
                codes[quarter] = step_call(quarter, step, kept[quarter], received[quarter])
            received[quarter].append(
                lax.ppermute(codes[quarter], "rep", partners(ORDERS[quarter][step]))
            )
    early = gather_call(kept[1:], sum(received[1:], []))
    update = iterate_call(kept[0], received[0], early)
    return lax.all_to_all(update.reshape(16, BAND, FF), "rep", split_axis=0, concat_axis=0, tiled=True)


def solution(mesh):
    return jax.shard_map(
        local,
        mesh=mesh,
        in_specs=(P("rep", "exp", None, None), P("exp", "rep", None)),
        out_specs=P("exp", "rep", None),
        check_vma=False,
    )
```

time: 127 us -> 120 us (0.945)
  Pallas kernels: 43.1 us -> 39.6 us
  waiting for transfers between devices: 39.4 us -> 37.6 us
  starting transfers between devices: 25.3 us -> 24 us
    pallas_call x4, Pallas kernels: 12.3 us -> 8.55 us  [first_calls(): pl.pallas_call(first_kernel if held is None else functools.partial(later_...]
    pallas_call x12, Pallas kernels: 8.7 us -> 11.2 us  [step_call(): pl.pallas_call(functools.partial(step_kernel, step), in_specs=[whole] * (...]
    pallas_call x2 -> x3, Pallas kernels: 22.1 us -> 19.9 us  [the longest x1 12 us: iterate_call(): pl.pallas_call(iterate_kernel, in_specs=[whole] * (1 + len(received) + le...]
    ppermute x16, waiting for transfers between devices: 39.4 us -> 37.6 us  [local(): lax.ppermute(codes[quarter], 'rep', partners(ORDERS[quarter][step]))]
    ppermute x16, starting transfers between devices: 25.3 us -> 24 us  [local(): lax.ppermute(codes[quarter], 'rep', partners(ORDERS[quarter][step]))]
  transfers between devices with their start and end apart: 16 -> 16, of which waited for: 10 -> 12; matrix products, arithmetic and copies ran while one was open for 0% -> 0% of each run, Pallas kernels for 17% -> 20%
where the time goes in v2:
time: 120 us; the launch traced here: 119 us
  Pallas kernels  39.6 us (33%)
  waiting for transfers between devices  37.6 us (31%)
  starting transfers between devices  24 us (20%)
  blocking collectives  16 us (13%)
  local copies, waits for them, and re-layouts  2.02 us (2%)
    ppermute x16, waiting for transfers between devices, local(): lax.ppermute(codes[quarter], 'rep', partners(ORDERS[quarter][step]))  37.6 us
    ppermute x16, starting transfers between devices, local(): lax.ppermute(codes[quarter], 'rep', partners(ORDERS[quarter][step]))  24 us
    all_to_all x1, blocking collectives, local(): lax.all_to_all(update.reshape(16, BAND, FF), 'rep', split_axis=0, concat_...  16 us
    pallas_call x1, Pallas kernels, iterate_call(): pl.pallas_call(iterate_kernel, in_specs=[whole] * (1 + len(received) + le...  12 us
    pallas_call x12, Pallas kernels, step_call(): pl.pallas_call(functools.partial(step_kernel, step), in_specs=[whole] * (...  11.2 us
    pallas_call x4, Pallas kernels, first_calls(): pl.pallas_call(first_kernel if held is None else functools.partial(later_...  8.55 us
    pallas_call x1, Pallas kernels, keep_call(): pl.pallas_call(keep_kernel, in_specs=[pl.BlockSpec(memory_space=pltpu.HBM...  5.14 us
    pallas_call x1, Pallas kernels, gather_call(): pl.pallas_call(gather_kernel, in_specs=[whole] * (len(kept) + len(receive...  2.72 us
  transfers between devices with their start and end apart: 16, of which 12 were waited for; matrix products, arithmetic and copies ran while one was open for 0% of the time, Pallas kernels for 20%

profile of v2, /device:TPU:0, one launch (start us, length us, event | category | flops | bytes accessed | tf_op | source)
XLA Modules:
  0.0 119.4 jit_solution(14076137167968778572)
XLA Ops:
  0.0 0.0 copy-start
  0.0 1.1 copy-done
  1.1 3.4 %first_q3.1 = (bf16[8,256,384]{2,1,0:T(8,128)(2,1)S(1)}, f32[8,256,384]{2,1,0:T(8,128)S(1)}) custom-call(f32[16,1024,384]{2,1,0:T(8,128)} %bitcast.3, bf16[16,64,384]{2,1,0:T(8,128)(2,1)S(1)} %copy-done), custom_call_target="tpu_custom_call" | custom-call | flops 7864320 | bytes 4718592 | tf_op jit(solution)/shard_map/first_q3/pallas_call | solution.py:141
  4.6 1.7 %collective-permute-start.12 = (bf16[8,256,384]{2,1,0:T(8,128)(2,1)S(1)}, bf16[8,256,384]{2,1,0:T(8,128)(2,1)S(1)}, u32[]{:S(2)}, u32[]{:S(2)}) collective-permute-start(bf16[8,256,384]{2,1,0:T(8,128)(2,1)S(1)} %get-tuple-element.23.refs_3_), channel_id=1, source_target_pairs={{0,8},{8,0},{16,24},{24,16},{32,40},{40,32},{48,56},{56,48},{64,72... | collective-permute-start | bytes 4718600 | tf_op jit(solution)/shard_map/ppermute | solution.py:345
  6.2 2.0 %first_q2.1 = (bf16[8,256,384]{2,1,0:T(8,128)(2,1)S(1)}, f32[8,256,384]{2,1,0:T(8,128)S(1)}) custom-call(f32[16,1024,384]{2,1,0:T(8,128)} %bitcast.4, bf16[16,64,384]{2,1,0:T(8,128)(2,1)S(1)} %copy-done, f32[8,256,384]{2,1,0:T(8,128)S(1)} %get-tuple-element.18.held_ref), custom_call_target="tpu_custom_call" | custom-call | flops 7864320 | bytes 4718592 | tf_op jit(solution)/shard_map/first_q2/pallas_call | solution.py:141
  8.2 1.8 %collective-permute-start.8 = (bf16[8,256,384]{2,1,0:T(8,128)(2,1)S(1)}, bf16[8,256,384]{2,1,0:T(8,128)(2,1)S(1)}, u32[]{:S(2)}, u32[]{:S(2)}) collective-permute-start(bf16[8,256,384]{2,1,0:T(8,128)(2,1)S(1)} %get-tuple-element.22.refs_2_), channel_id=1, source_target_pairs={{0,32},{8,40},{16,48},{24,56},{32,0},{40,8},{48,16},{56,24},{64,96... | collective-permute-start | bytes 4718600 | tf_op jit(solution)/shard_map/ppermute | solution.py:345
  10.0 2.1 %first_q1.1 = (bf16[8,256,384]{2,1,0:T(8,128)(2,1)S(1)}, f32[8,256,384]{2,1,0:T(8,128)S(1)}) custom-call(f32[16,1024,384]{2,1,0:T(8,128)} %bitcast.5, bf16[16,64,384]{2,1,0:T(8,128)(2,1)S(1)} %copy-done, f32[8,256,384]{2,1,0:T(8,128)S(1)} %get-tuple-element.19.held_ref), custom_call_target="tpu_custom_call" | custom-call | flops 7864320 | bytes 4718592 | tf_op jit(solution)/shard_map/first_q1/pallas_call | solution.py:141
  12.2 2.2 %collective-permute-start.4 = (bf16[8,256,384]{2,1,0:T(8,128)(2,1)S(1)}, bf16[8,256,384]{2,1,0:T(8,128)(2,1)S(1)}, u32[]{:S(2)}, u32[]{:S(2)}) collective-permute-start(bf16[8,256,384]{2,1,0:T(8,128)(2,1)S(1)} %get-tuple-element.21.refs_1_), channel_id=1, source_target_pairs={{0,24},{8,16},{16,8},{24,0},{32,56},{40,48},{48,40},{56,32},{64,88... | collective-permute-start | bytes 4718600 | tf_op jit(solution)/shard_map/ppermute | solution.py:345
  14.3 0.0 copy-start.1
  14.3 1.0 first_q0.1.refs_0_
  15.4 2.4 %collective-permute-start = (bf16[8,256,384]{2,1,0:T(8,128)(2,1)S(1)}, bf16[8,256,384]{2,1,0:T(8,128)(2,1)S(1)}, u32[]{:S(2)}, u32[]{:S(2)}) collective-permute-start(bf16[8,256,384]{2,1,0:T(8,128)(2,1)S(1)} %first_q0.1.refs_0_), channel_id=1, source_target_pairs={{0,96},{8,104},{16,112},{24,120},{32,64},{40,72},{48,80},{56,88},{... | collective-permute-start | bytes 4718600 | tf_op jit(solution)/shard_map/ppermute | solution.py:345
  17.7 0.0 copy-done.1
  17.7 5.1 %keep.1 = (f32[8,256,384]{2,1,0:T(8,128)S(1)}, f32[8,256,384]{2,1,0:T(8,128)S(1)}, f32[8,256,384]{2,1,0:T(8,128)S(1)}, f32[8,256,384]{2,1,0:T(8,128)S(1)}) custom-call(f32[16,1024,384]{2,1,0:T(8,128)} %bitcast.7, bf16[16,64,384]{2,1,0:T(8,128)(2,1)S(1)} %copy-done.1, bf16[8,256,384]{2,1,0:T(8,128)(2,1)S(1)} %first_q0.1.refs_0_, ...), custom_call_target="tpu_custom_call" | custom-call | flops 786432 | bytes 12582912 | tf_op jit(solution)/shard_map/keep/pallas_call | solution.py:173
  22.9 17.7 %collective-permute-done.12.refs_0_.refs_11_ = bf16[8,256,384]{2,1,0:T(8,128)(2,1)S(1)} collective-permute-done((bf16[8,256,384]{2,1,0:T(8,128)(2,1)S(1)}, bf16[8,256,384]{2,1,0:T(8,128)(2,1)S(1)}, u32[]{:S(2)}, u32[]{:S(2)}) %collective-permute-start.12) | collective-permute-done | bytes 1572896 | tf_op jit(solution)/shard_map/ppermute | solution.py:345
  40.6 1.2 %codes_q3_s1.1 = bf16[4,256,384]{2,1,0:T(8,128)(2,1)S(1)} custom-call(f32[8,256,384]{2,1,0:T(8,128)S(1)} %get-tuple-element.27.kept_ref.refs_2_, bf16[8,256,384]{2,1,0:T(8,128)(2,1)S(1)} %collective-permute-done.12.refs_0_.refs_11_), custom_call_target="tpu_custom_call" | custom-call | flops 6291456 | bytes 3145728 | tf_op jit(solution)/shard_map/codes_q3_s1/pallas_call | solution.py:209
  41.9 1.9 %collective-permute-start.13 = (bf16[4,256,384]{2,1,0:T(8,128)(2,1)S(1)}, bf16[4,256,384]{2,1,0:T(8,128)(2,1)S(1)}, u32[]{:S(2)}, u32[]{:S(2)}) collective-permute-start(bf16[4,256,384]{2,1,0:T(8,128)(2,1)S(1)} %codes_q3_s1.1), channel_id=1, source_target_pairs={{0,32},{8,40},{16,48},{24,56},{32,0},{40,8},{48,16},{56,24},{64,96... | collective-permute-start | bytes 2359304 | tf_op jit(solution)/shard_map/ppermute | solution.py:345
  43.8 0.9 collective-permute-done.8.refs_0_.refs_7_
  44.6 1.2 %codes_q2_s1.1 = bf16[4,256,384]{2,1,0:T(8,128)(2,1)S(1)} custom-call(f32[8,256,384]{2,1,0:T(8,128)S(1)} %get-tuple-element.26.kept_ref.refs_1_, bf16[8,256,384]{2,1,0:T(8,128)(2,1)S(1)} %collective-permute-done.8.refs_0_.refs_7_), custom_call_target="tpu_custom_call" | custom-call | flops 6291456 | bytes 3145728 | tf_op jit(solution)/shard_map/codes_q2_s1/pallas_call | solution.py:209
  45.9 2.0 %collective-permute-start.9 = (bf16[4,256,384]{2,1,0:T(8,128)(2,1)S(1)}, bf16[4,256,384]{2,1,0:T(8,128)(2,1)S(1)}, u32[]{:S(2)}, u32[]{:S(2)}) collective-permute-start(bf16[4,256,384]{2,1,0:T(8,128)(2,1)S(1)} %codes_q2_s1.1), channel_id=1, source_target_pairs={{0,24},{8,16},{16,8},{24,0},{32,56},{40,48},{48,40},{56,32},{64,88... | collective-permute-start | bytes 2359304 | tf_op jit(solution)/shard_map/ppermute | solution.py:345
  47.8 2.2 %collective-permute-done.4.refs_0_.refs_3_ = bf16[8,256,384]{2,1,0:T(8,128)(2,1)S(1)} collective-permute-done((bf16[8,256,384]{2,1,0:T(8,128)(2,1)S(1)}, bf16[8,256,384]{2,1,0:T(8,128)(2,1)S(1)}, u32[]{:S(2)}, u32[]{:S(2)}) %collective-permute-start.4) | collective-permute-done | bytes 1572896 | tf_op jit(solution)/shard_map/ppermute | solution.py:345
  50.1 1.2 %codes_q1_s1.1 = bf16[4,256,384]{2,1,0:T(8,128)(2,1)S(1)} custom-call(f32[8,256,384]{2,1,0:T(8,128)S(1)} %get-tuple-element.25.kept_ref.refs_0_, bf16[8,256,384]{2,1,0:T(8,128)(2,1)S(1)} %collective-permute-done.4.refs_0_.refs_3_), custom_call_target="tpu_custom_call" | custom-call | flops 6291456 | bytes 3145728 | tf_op jit(solution)/shard_map/codes_q1_s1/pallas_call | solution.py:209
  51.3 1.5 %collective-permute-start.5 = (bf16[4,256,384]{2,1,0:T(8,128)(2,1)S(1)}, bf16[4,256,384]{2,1,0:T(8,128)(2,1)S(1)}, u32[]{:S(2)}, u32[]{:S(2)}) collective-permute-start(bf16[4,256,384]{2,1,0:T(8,128)(2,1)S(1)} %codes_q1_s1.1), channel_id=1, source_target_pairs={{0,96},{8,104},{16,112},{24,120},{32,64},{40,72},{48,80},{56,88},{... | collective-permute-start | bytes 2359304 | tf_op jit(solution)/shard_map/ppermute | solution.py:345
  52.8 0.0 collective-permute-done.refs_0_
  52.8 1.2 %codes_q0_s1.1 = bf16[4,256,384]{2,1,0:T(8,128)(2,1)S(1)} custom-call(f32[8,256,384]{2,1,0:T(8,128)S(1)} %get-tuple-element.24.kept_ref, bf16[8,256,384]{2,1,0:T(8,128)(2,1)S(1)} %collective-permute-done.refs_0_), custom_call_target="tpu_custom_call" | custom-call | flops 6291456 | bytes 3145728 | tf_op jit(solution)/shard_map/codes_q0_s1/pallas_call | solution.py:209
  54.1 0.1 collective-permute-start.1
  54.2 6.8 %collective-permute-done.13.refs_1_.refs_12_ = bf16[4,256,384]{2,1,0:T(8,128)(2,1)S(1)} collective-permute-done((bf16[4,256,384]{2,1,0:T(8,128)(2,1)S(1)}, bf16[4,256,384]{2,1,0:T(8,128)(2,1)S(1)}, u32[]{:S(2)}, u32[]{:S(2)}) %collective-permute-start.13) | collective-permute-done | bytes 786464 | tf_op jit(solution)/shard_map/ppermute | solution.py:345
  61.0 0.9 codes_q3_s2.1
  61.9 2.4 %collective-permute-start.14 = (bf16[2,256,384]{2,1,0:T(8,128)(2,1)S(1)}, bf16[2,256,384]{2,1,0:T(8,128)(2,1)S(1)}, u32[]{:S(2)}, u32[]{:S(2)}) collective-permute-start(bf16[2,256,384]{2,1,0:T(8,128)(2,1)S(1)} %codes_q3_s2.1), channel_id=1, source_target_pairs={{0,24},{8,16},{16,8},{24,0},{32,56},{40,48},{48,40},{56,32},{64,88... | collective-permute-start | bytes 1179656 | tf_op jit(solution)/shard_map/ppermute | solution.py:345
  64.4 2.8 %collective-permute-done.9.refs_1_.refs_8_ = bf16[4,256,384]{2,1,0:T(8,128)(2,1)S(1)} collective-permute-done((bf16[4,256,384]{2,1,0:T(8,128)(2,1)S(1)}, bf16[4,256,384]{2,1,0:T(8,128)(2,1)S(1)}, u32[]{:S(2)}, u32[]{:S(2)}) %collective-permute-start.9) | collective-permute-done | bytes 786464 | tf_op jit(solution)/shard_map/ppermute | solution.py:345
  67.2 0.9 codes_q2_s2.1
  68.1 1.8 %collective-permute-start.10 = (bf16[2,256,384]{2,1,0:T(8,128)(2,1)S(1)}, bf16[2,256,384]{2,1,0:T(8,128)(2,1)S(1)}, u32[]{:S(2)}, u32[]{:S(2)}) collective-permute-start(bf16[2,256,384]{2,1,0:T(8,128)(2,1)S(1)} %codes_q2_s2.1), channel_id=1, source_target_pairs={{0,96},{8,104},{16,112},{24,120},{32,64},{40,72},{48,80},{56,88},{... | collective-permute-start | bytes 1179656 | tf_op jit(solution)/shard_map/ppermute | solution.py:345
  69.9 0.0 collective-permute-done.5.refs_1_.refs_4_
  69.9 0.9 codes_q1_s2.1
  70.8 0.1 collective-permute-start.6
  70.9 1.7 %collective-permute-done.1.refs_1_ = bf16[4,256,384]{2,1,0:T(8,128)(2,1)S(1)} collective-permute-done((bf16[4,256,384]{2,1,0:T(8,128)(2,1)S(1)}, bf16[4,256,384]{2,1,0:T(8,128)(2,1)S(1)}, u32[]{:S(2)}, u32[]{:S(2)}) %collective-permute-start.1) | collective-permute-done | bytes 786464 | tf_op jit(solution)/shard_map/ppermute | solution.py:345
  72.7 0.9 codes_q0_s2.1
  73.6 0.5 collective-permute-start.2
  74.1 0.2 collective-permute-done.14.refs_2_.refs_13_
  74.3 0.6 codes_q3_s3.1
  74.9 2.4 %collective-permute-start.15 = (bf16[1,256,384]{2,1,0:T(8,128)(2,1)S(1)}, bf16[1,256,384]{2,1,0:T(8,128)(2,1)S(1)}, u32[]{:S(2)}, u32[]{:S(2)}) collective-permute-start(bf16[1,256,384]{2,1,0:T(8,128)(2,1)S(1)} %codes_q3_s3.1), channel_id=1, source_target_pairs={{0,96},{8,104},{16,112},{24,120},{32,64},{40,72},{48,80},{56,88},{... | collective-permute-start | bytes 589832 | tf_op jit(solution)/shard_map/ppermute | solution.py:345
  77.3 0.5 collective-permute-done.10.refs_2_.refs_9_
  77.9 0.6 codes_q2_s3.1
  78.5 0.6 collective-permute-start.11
  79.1 2.0 %collective-permute-done.6.refs_2_.refs_5_ = bf16[2,256,384]{2,1,0:T(8,128)(2,1)S(1)} collective-permute-done((bf16[2,256,384]{2,1,0:T(8,128)(2,1)S(1)}, bf16[2,256,384]{2,1,0:T(8,128)(2,1)S(1)}, u32[]{:S(2)}, u32[]{:S(2)}) %collective-permute-start.6) | collective-permute-done | bytes 393248 | tf_op jit(solution)/shard_map/ppermute | solution.py:345
  81.1 0.6 codes_q1_s3.1
  81.7 0.5 collective-permute-start.7
  82.2 0.4 collective-permute-done.2.refs_2_
  82.6 0.6 codes_q0_s3.1
  83.3 2.2 %collective-permute-start.3 = (bf16[1,256,384]{2,1,0:T(8,128)(2,1)S(1)}, bf16[1,256,384]{2,1,0:T(8,128)(2,1)S(1)}, u32[]{:S(2)}, u32[]{:S(2)}) collective-permute-start(bf16[1,256,384]{2,1,0:T(8,128)(2,1)S(1)} %codes_q0_s3.1), channel_id=1, source_target_pairs={{0,24},{8,16},{16,8},{24,0},{32,56},{40,48},{48,40},{56,32},{64,88... | collective-permute-start | bytes 589832 | tf_op jit(solution)/shard_map/ppermute | solution.py:345
  85.5 0.0 collective-permute-done.15.refs_14_
  85.5 0.0 collective-permute-done.11.refs_10_
  85.5 2.0 %collective-permute-done.7.refs_6_ = bf16[1,256,384]{2,1,0:T(8,128)(2,1)S(1)} collective-permute-done((bf16[1,256,384]{2,1,0:T(8,128)(2,1)S(1)}, bf16[1,256,384]{2,1,0:T(8,128)(2,1)S(1)}, u32[]{:S(2)}, u32[]{:S(2)}) %collective-permute-start.7) | collective-permute-done | bytes 196640 | tf_op jit(solution)/shard_map/ppermute | solution.py:345
  87.5 2.7 %gather.1 = (bf16[768,384]{1,0:T(8,128)(2,1)S(1)}, bf16[768,384]{1,0:T(8,128)(2,1)S(1)}, f32[384,768]{1,0:T(8,128)S(1)}) custom-call(f32[8,256,384]{2,1,0:T(8,128)S(1)} %get-tuple-element.25.kept_ref.refs_0_, f32[8,256,384]{2,1,0:T(8,128)S(1)} %get-tuple-element.26.kept_ref.refs_1_, f32[8,256,384]{2,1,0:T(8,128)S(1)} %get-tuple-element.27.kept_ref.refs_2_, ...), custom_call_target="tpu_custom_call" | custom-call | flops 452984832 | bytes 4718592 | tf_op jit(solution)/shard_map/gather/pallas_call | solution.py:272
  90.2 0.2 collective-permute-done.3.refs_3_
  90.4 12.0 %newton_schulz.1 = bf16[1024,384]{1,0:T(8,128)(2,1)S(1)} custom-call(f32[8,256,384]{2,1,0:T(8,128)S(1)} %get-tuple-element.24.kept_ref, bf16[8,256,384]{2,1,0:T(8,128)(2,1)S(1)} %collective-permute-done.refs_0_, bf16[4,256,384]{2,1,0:T(8,128)(2,1)S(1)} %collective-permute-done.1.refs_1_, bf16[2,256,384]{2,1,0:T(8,128)(2,1)S(1)} %collective-permute-done.2.refs_2_, ...), custom_call_target="tpu_custom_call" | custom-call | flops 6681526272 | bytes 6291456 | tf_op jit(solution)/shard_map/newton_schulz/pallas_call | solution.py:321
  102.5 16.0 %all_to_all.5 = bf16[16,64,384]{2,1,0:T(8,128)(2,1)S(1)} all-to-all(bf16[16,64,384]{2,1,0:T(8,128)(2,1)S(1)} %bitcast.2), channel_id=1, replica_groups=mesh['rep'=16,'exp'=8] {'rep'}, dimensions={0} | all-to-all | bytes 1572864 | tf_op jit(solution)/shard_map/all_to_all | solution.py:349
  118.5 0.9 copy.4
Async XLA Ops:
  0.0 1.1 copy-start
  4.6 36.0 %collective-permute-start.12 = (bf16[8,256,384]{2,1,0:T(8,128)(2,1)S(1)}, bf16[8,256,384]{2,1,0:T(8,128)(2,1)S(1)}, u32[]{:S(2)}, u32[]{:S(2)}) collective-permute-start(bf16[8,256,384]{2,1,0:T(8,128)(2,1)S(1)} %get-tuple-element.23.refs_3_), channel_id=1, source_target_pairs={{0,8},{8,0},{16,24},{24,16},{32,40},{40,32},{48,56},{56,48},{64,72... | collective-permute-start | bytes 4718600 | tf_op jit(solution)/shard_map/ppermute | solution.py:345
  8.2 36.4 %collective-permute-start.8 = (bf16[8,256,384]{2,1,0:T(8,128)(2,1)S(1)}, bf16[8,256,384]{2,1,0:T(8,128)(2,1)S(1)}, u32[]{:S(2)}, u32[]{:S(2)}) collective-permute-start(bf16[8,256,384]{2,1,0:T(8,128)(2,1)S(1)} %get-tuple-element.22.refs_2_), channel_id=1, source_target_pairs={{0,32},{8,40},{16,48},{24,56},{32,0},{40,8},{48,16},{56,24},{64,96... | collective-permute-start | bytes 4718600 | tf_op jit(solution)/shard_map/ppermute | solution.py:345
  12.2 37.9 %collective-permute-start.4 = (bf16[8,256,384]{2,1,0:T(8,128)(2,1)S(1)}, bf16[8,256,384]{2,1,0:T(8,128)(2,1)S(1)}, u32[]{:S(2)}, u32[]{:S(2)}) collective-permute-start(bf16[8,256,384]{2,1,0:T(8,128)(2,1)S(1)} %get-tuple-element.21.refs_1_), channel_id=1, source_target_pairs={{0,24},{8,16},{16,8},{24,0},{32,56},{40,48},{48,40},{56,32},{64,88... | collective-permute-start | bytes 4718600 | tf_op jit(solution)/shard_map/ppermute | solution.py:345
  14.3 3.4 %copy-start.1 = (bf16[16,64,384]{2,1,0:T(8,128)(2,1)S(1)}, bf16[16,64,384]{2,1,0:T(8,128)(2,1)}, u32[]{:S(2)}) copy-start(bf16[16,64,384]{2,1,0:T(8,128)(2,1)} %momentum_ref.9) | copy-start | bytes 2359300
  15.4 37.5 %collective-permute-start = (bf16[8,256,384]{2,1,0:T(8,128)(2,1)S(1)}, bf16[8,256,384]{2,1,0:T(8,128)(2,1)S(1)}, u32[]{:S(2)}, u32[]{:S(2)}) collective-permute-start(bf16[8,256,384]{2,1,0:T(8,128)(2,1)S(1)} %first_q0.1.refs_0_), channel_id=1, source_target_pairs={{0,96},{8,104},{16,112},{24,120},{32,64},{40,72},{48,80},{56,88},{... | collective-permute-start | bytes 4718600 | tf_op jit(solution)/shard_map/ppermute | solution.py:345
  41.9 19.1 %collective-permute-start.13 = (bf16[4,256,384]{2,1,0:T(8,128)(2,1)S(1)}, bf16[4,256,384]{2,1,0:T(8,128)(2,1)S(1)}, u32[]{:S(2)}, u32[]{:S(2)}) collective-permute-start(bf16[4,256,384]{2,1,0:T(8,128)(2,1)S(1)} %codes_q3_s1.1), channel_id=1, source_target_pairs={{0,32},{8,40},{16,48},{24,56},{32,0},{40,8},{48,16},{56,24},{64,96... | collective-permute-start | bytes 2359304 | tf_op jit(solution)/shard_map/ppermute | solution.py:345
  45.9 21.3 %collective-permute-start.9 = (bf16[4,256,384]{2,1,0:T(8,128)(2,1)S(1)}, bf16[4,256,384]{2,1,0:T(8,128)(2,1)S(1)}, u32[]{:S(2)}, u32[]{:S(2)}) collective-permute-start(bf16[4,256,384]{2,1,0:T(8,128)(2,1)S(1)} %codes_q2_s1.1), channel_id=1, source_target_pairs={{0,24},{8,16},{16,8},{24,0},{32,56},{40,48},{48,40},{56,32},{64,88... | collective-permute-start | bytes 2359304 | tf_op jit(solution)/shard_map/ppermute | solution.py:345
  51.3 18.6 %collective-permute-start.5 = (bf16[4,256,384]{2,1,0:T(8,128)(2,1)S(1)}, bf16[4,256,384]{2,1,0:T(8,128)(2,1)S(1)}, u32[]{:S(2)}, u32[]{:S(2)}) collective-permute-start(bf16[4,256,384]{2,1,0:T(8,128)(2,1)S(1)} %codes_q1_s1.1), channel_id=1, source_target_pairs={{0,96},{8,104},{16,112},{24,120},{32,64},{40,72},{48,80},{56,88},{... | collective-permute-start | bytes 2359304 | tf_op jit(solution)/shard_map/ppermute | solution.py:345
  54.1 18.6 %collective-permute-start.1 = (bf16[4,256,384]{2,1,0:T(8,128)(2,1)S(1)}, bf16[4,256,384]{2,1,0:T(8,128)(2,1)S(1)}, u32[]{:S(2)}, u32[]{:S(2)}) collective-permute-start(bf16[4,256,384]{2,1,0:T(8,128)(2,1)S(1)} %codes_q0_s1.1), channel_id=1, source_target_pairs={{0,8},{8,0},{16,24},{24,16},{32,40},{40,32},{48,56},{56,48},{64,72... | collective-permute-start | bytes 2359304 | tf_op jit(solution)/shard_map/ppermute | solution.py:345
  61.9 12.4 %collective-permute-start.14 = (bf16[2,256,384]{2,1,0:T(8,128)(2,1)S(1)}, bf16[2,256,384]{2,1,0:T(8,128)(2,1)S(1)}, u32[]{:S(2)}, u32[]{:S(2)}) collective-permute-start(bf16[2,256,384]{2,1,0:T(8,128)(2,1)S(1)} %codes_q3_s2.1), channel_id=1, source_target_pairs={{0,24},{8,16},{16,8},{24,0},{32,56},{40,48},{48,40},{56,32},{64,88... | collective-permute-start | bytes 1179656 | tf_op jit(solution)/shard_map/ppermute | solution.py:345
  68.1 9.7 %collective-permute-start.10 = (bf16[2,256,384]{2,1,0:T(8,128)(2,1)S(1)}, bf16[2,256,384]{2,1,0:T(8,128)(2,1)S(1)}, u32[]{:S(2)}, u32[]{:S(2)}) collective-permute-start(bf16[2,256,384]{2,1,0:T(8,128)(2,1)S(1)} %codes_q2_s2.1), channel_id=1, source_target_pairs={{0,96},{8,104},{16,112},{24,120},{32,64},{40,72},{48,80},{56,88},{... | collective-permute-start | bytes 1179656 | tf_op jit(solution)/shard_map/ppermute | solution.py:345
  70.8 10.2 %collective-permute-start.6 = (bf16[2,256,384]{2,1,0:T(8,128)(2,1)S(1)}, bf16[2,256,384]{2,1,0:T(8,128)(2,1)S(1)}, u32[]{:S(2)}, u32[]{:S(2)}) collective-permute-start(bf16[2,256,384]{2,1,0:T(8,128)(2,1)S(1)} %codes_q1_s2.1), channel_id=1, source_target_pairs={{0,8},{8,0},{16,24},{24,16},{32,40},{40,32},{48,56},{56,48},{64,72... | collective-permute-start | bytes 1179656 | tf_op jit(solution)/shard_map/ppermute | solution.py:345
  73.6 9.0 %collective-permute-start.2 = (bf16[2,256,384]{2,1,0:T(8,128)(2,1)S(1)}, bf16[2,256,384]{2,1,0:T(8,128)(2,1)S(1)}, u32[]{:S(2)}, u32[]{:S(2)}) collective-permute-start(bf16[2,256,384]{2,1,0:T(8,128)(2,1)S(1)} %codes_q0_s2.1), channel_id=1, source_target_pairs={{0,32},{8,40},{16,48},{24,56},{32,0},{40,8},{48,16},{56,24},{64,96... | collective-permute-start | bytes 1179656 | tf_op jit(solution)/shard_map/ppermute | solution.py:345
  74.9 10.6 %collective-permute-start.15 = (bf16[1,256,384]{2,1,0:T(8,128)(2,1)S(1)}, bf16[1,256,384]{2,1,0:T(8,128)(2,1)S(1)}, u32[]{:S(2)}, u32[]{:S(2)}) collective-permute-start(bf16[1,256,384]{2,1,0:T(8,128)(2,1)S(1)} %codes_q3_s3.1), channel_id=1, source_target_pairs={{0,96},{8,104},{16,112},{24,120},{32,64},{40,72},{48,80},{56,88},{... | collective-permute-start | bytes 589832 | tf_op jit(solution)/shard_map/ppermute | solution.py:345
  78.5 7.0 %collective-permute-start.11 = (bf16[1,256,384]{2,1,0:T(8,128)(2,1)S(1)}, bf16[1,256,384]{2,1,0:T(8,128)(2,1)S(1)}, u32[]{:S(2)}, u32[]{:S(2)}) collective-permute-start(bf16[1,256,384]{2,1,0:T(8,128)(2,1)S(1)} %codes_q2_s3.1), channel_id=1, source_target_pairs={{0,8},{8,0},{16,24},{24,16},{32,40},{40,32},{48,56},{56,48},{64,72... | collective-permute-start | bytes 589832 | tf_op jit(solution)/shard_map/ppermute | solution.py:345
  81.7 5.7 %collective-permute-start.7 = (bf16[1,256,384]{2,1,0:T(8,128)(2,1)S(1)}, bf16[1,256,384]{2,1,0:T(8,128)(2,1)S(1)}, u32[]{:S(2)}, u32[]{:S(2)}) collective-permute-start(bf16[1,256,384]{2,1,0:T(8,128)(2,1)S(1)} %codes_q1_s3.1), channel_id=1, source_target_pairs={{0,32},{8,40},{16,48},{24,56},{32,0},{40,8},{48,16},{56,24},{64,96... | collective-permute-start | bytes 589832 | tf_op jit(solution)/shard_map/ppermute | solution.py:345
  83.3 7.1 %collective-permute-start.3 = (bf16[1,256,384]{2,1,0:T(8,128)(2,1)S(1)}, bf16[1,256,384]{2,1,0:T(8,128)(2,1)S(1)}, u32[]{:S(2)}, u32[]{:S(2)}) collective-permute-start(bf16[1,256,384]{2,1,0:T(8,128)(2,1)S(1)} %codes_q0_s3.1), channel_id=1, source_target_pairs={{0,24},{8,16},{16,8},{24,0},{32,56},{40,48},{48,40},{56,32},{64,88... | collective-permute-start | bytes 589832 | tf_op jit(solution)/shard_map/ppermute | solution.py:345

commit v3 on v2

v3 whole, which is shorter than its diff:
```python
import functools
import math

import jax
import jax.numpy as jnp
from jax import lax
from jax.experimental import pallas as pl
from jax.experimental.pallas import tpu as pltpu
from jax.sharding import PartitionSpec as P

D = 1024
FF = 384
NS_ITERS = 5
ROWS = (240, 256, 256, 272)
FIRST = (784, 528, 272, 0)
PIECE = 16
STRIP = 64
BAND = 64
SPLIT = 256
BLOCK = 256
GAIN = 1.0 + 0.95
BLEND = 0.95 * 0.95 / GAIN

ORDERS = ((3, 0, 2, 1), (1, 3, 0, 2), (2, 1, 3, 0), (0, 2, 1, 3))
FLIPS = (1, 3, 4, 12)
SHIFT = 8
POWER = 9


def partners(bit):
    return [(rep, rep ^ FLIPS[bit]) for rep in range(16)]


def expert_of(quarter, sent, index):
    first, *others = [FLIPS[bit] for bit in ORDERS[quarter]]
    expert = lax.axis_index("rep") ^ (first if sent else 0)
    for place, flip in enumerate(others):
        expert = expert ^ (((index >> (2 - place)) & 1) * flip)
    return expert


def encode(value):
    second = value * value
    fourth = second * second
    return (fourth * fourth * value).astype(jnp.bfloat16)


def decode(code):
    code = code.astype(jnp.float32)
    level = jnp.log(jnp.maximum(jnp.abs(code), float(2.0**-126)))
    return code * jnp.exp2(level * ((1 / POWER - 1) / math.log(2.0)))


def raw_copy(quarter, sent, parts_ref, held_ref, sems, index):
    rows = pl.ds(FIRST[quarter], ROWS[quarter])
    expert = expert_of(quarter, sent, index)
    return pltpu.make_async_copy(parts_ref.at[expert, rows], held_ref.at[index], sems.at[index])


def on_band(quarter, body):
    low, count = FIRST[quarter], ROWS[quarter]
    band_low = lax.axis_index("rep") * BAND

    @pl.when((band_low < low + count) & (band_low + BAND > low))
    def _():
        for start in range(0, BAND, PIECE):
            row = band_low + start - low

            @pl.when((row >= 0) & (row < count))
            def _(start=start, row=row):
                body(pl.ds(pl.multiple_of(row, PIECE), PIECE), pl.ds(start, PIECE))


def strips(count):
    return [pl.ds(start, min(STRIP, count - start)) for start in range(0, count, STRIP)]


def loop(count, body):
    def step(index, carry):
        body(index)
        return carry

    lax.fori_loop(0, count, step, 0)


def fetch_kernel(parts_ref, held_ref, sems):
    loop(8, lambda index: raw_copy(3, True, parts_ref, held_ref, sems, index).start())
    loop(8, lambda index: raw_copy(3, True, parts_ref, held_ref, sems, index).wait())


def first_kernel(quarter, parts_ref, momentum_ref, held_ref, out_ref, *rest):
    if rest:
        loop(8, lambda index: raw_copy(quarter - 1, True, parts_ref, *rest, index).start())

    def expert(index):
        for rows in strips(ROWS[quarter]):
            out_ref[index, rows] = encode(held_ref[index, rows] * float(2**SHIFT))

        def blend(rows, band):
            held = momentum_ref[expert_of(quarter, True, index), band].astype(jnp.float32)
            out_ref[index, rows] = encode((held_ref[index, rows] + BLEND * held) * float(2**SHIFT))

        on_band(quarter, blend)

    loop(8, expert)
    if rest:
        loop(8, lambda index: raw_copy(quarter - 1, True, parts_ref, *rest, index).wait())


def first_calls(parts, momentum):
    hbm = pl.BlockSpec(memory_space=pltpu.HBM)
    whole = pl.BlockSpec(memory_space=pltpu.VMEM)
    params = pltpu.CompilerParams(vmem_limit_bytes=40 * 1024 * 1024)

    def raw(quarter):
        return jax.ShapeDtypeStruct((8, ROWS[quarter], FF), jnp.float32)

    held = pl.pallas_call(
        fetch_kernel,
        in_specs=[hbm],
        out_specs=whole,
        scratch_shapes=[pltpu.SemaphoreType.DMA((8,))],
        out_shape=raw(3),
        compiler_params=params,
        cost_estimate=pl.CostEstimate(flops=0, bytes_accessed=64 * ROWS[3] * FF, transcendentals=0),
        name="fetch",
    )(parts)
    codes = [None] * 4
    for quarter in (3, 2, 1, 0):
        more = quarter > 0
        size = 8 * ROWS[quarter] * FF
        results = pl.pallas_call(
            functools.partial(first_kernel, quarter),
            in_specs=[hbm, whole, whole],
            out_specs=[whole] * (1 + more),
            scratch_shapes=[pltpu.SemaphoreType.DMA((8,))] * more,
            out_shape=[jax.ShapeDtypeStruct((8, ROWS[quarter], FF), jnp.bfloat16)] + [raw(quarter - 1)] * more,
            compiler_params=params,
            cost_estimate=pl.CostEstimate(flops=size * 10, bytes_accessed=size * 6, transcendentals=0),
            name=f"first_q{quarter}",
        )(parts, momentum, held)
        codes[quarter] = results[0]
        held = results[-1]
    return codes


def keep_kernel(parts_ref, momentum_ref, *refs):
    held_refs, sems = refs[4:8], refs[8]

    def copy(quarter, index):
        return raw_copy(quarter, False, parts_ref, held_refs[quarter], sems.at[quarter], index)

    for quarter in range(4):
        loop(8, lambda index, quarter=quarter: copy(quarter, index).start())
    for quarter, held_ref in enumerate(held_refs):

        def expert(index, quarter=quarter, held_ref=held_ref):
            copy(quarter, index).wait()
            for rows in strips(ROWS[quarter]):
                held_ref[index, rows] = held_ref[index, rows] * float(2**SHIFT)

            def blend(rows, band):
                held = momentum_ref[expert_of(quarter, False, index), band].astype(jnp.float32)
                held_ref[index, rows] += BLEND * float(2**SHIFT) * held

            on_band(quarter, blend)

        loop(8, expert)


def keep_call(parts, momentum, codes):
    whole = pl.BlockSpec(memory_space=pltpu.VMEM)
    return pl.pallas_call(
        keep_kernel,
        in_specs=[pl.BlockSpec(memory_space=pltpu.HBM), whole] + [pl.BlockSpec(memory_space=pl.ANY)] * 4,
        out_specs=[whole] * 4,
        scratch_shapes=[pltpu.SemaphoreType.DMA((4, 8))],
        out_shape=[jax.ShapeDtypeStruct((8, rows, FF), jnp.float32) for rows in ROWS],
        compiler_params=pltpu.CompilerParams(vmem_limit_bytes=32 * 1024 * 1024),
        cost_estimate=pl.CostEstimate(flops=8 * D * FF, bytes_accessed=64 * D * FF, transcendentals=0),
        name="keep",
    )(parts, momentum, *codes)


def fold_kernel(*refs):
    kept_refs, received, out_refs = refs[:4], refs[4:8], refs[9:]
    for kept_ref, ref, out_ref in zip(kept_refs, received, out_refs):

        def expert(index, kept_ref=kept_ref, ref=ref, out_ref=out_ref):
            for rows in strips(out_ref.shape[1]):
                out_ref[index, rows] = kept_ref[index, rows] + decode(ref[index, rows])

        loop(4, expert)


def fold_call(kept, received, after):
    whole = pl.BlockSpec(memory_space=pltpu.VMEM)
    return pl.pallas_call(
        fold_kernel,
        in_specs=[whole] * 8 + [pl.BlockSpec(memory_space=pl.ANY)],
        out_specs=[whole] * 4,
        out_shape=[jax.ShapeDtypeStruct((4, rows, FF), jnp.float32) for rows in ROWS],
        compiler_params=pltpu.CompilerParams(vmem_limit_bytes=8 * 1024 * 1024),
        cost_estimate=pl.CostEstimate(flops=32 * D * FF, bytes_accessed=40 * D * FF, transcendentals=8 * D * FF),
        name="fold",
    )(*kept, *received, after)


def step_kernel(place, base_ref, *refs):
    received, out_ref = refs[:-1], refs[-1]

    def expert(index):
        for rows in strips(out_ref.shape[1]):
            value = base_ref[place + index, rows]
            for ref in received:
                value = value + decode(ref[place + index, rows])
            out_ref[index, rows] = encode(value)

    loop(out_ref.shape[0], expert)


def step_call(quarter, step, base, received):
    count = 8 >> step
    size = count * ROWS[quarter] * FF
    whole = pl.BlockSpec(memory_space=pltpu.VMEM)
    return pl.pallas_call(
        functools.partial(step_kernel, count),
        in_specs=[whole] * (1 + len(received)),
        out_specs=whole,
        out_shape=jax.ShapeDtypeStruct((count, ROWS[quarter], FF), jnp.bfloat16),
        compiler_params=pltpu.CompilerParams(vmem_limit_bytes=8 * 1024 * 1024),
        cost_estimate=pl.CostEstimate(
            flops=size * 16, bytes_accessed=size * (6 + 2 * step), transcendentals=2 * size * step
        ),
        name=f"codes_q{quarter}_s{step}",
    )(base, *received)


def halves(value):
    high = value.astype(jnp.bfloat16)
    return high, (value - high.astype(jnp.float32)).astype(jnp.bfloat16)


def dot(left, right):
    return jnp.dot(left, right, preferred_element_type=jnp.float32)


def wide(left):
    return jnp.concatenate([left[0], left[1], left[0]], axis=1)


def tall(right):
    return jnp.concatenate([right[0], right[0], right[1]], axis=0)


def symmetric(left, right):
    left, right = wide(left), tall(right)
    most = dot(left, right[:, :SPLIT])
    corner = dot(left[SPLIT:], right[:, SPLIT:])
    return jnp.concatenate([most, jnp.concatenate([most[SPLIT:].T, corner], axis=0)], axis=1)


def split_sums(kept_ref, received, high_ref, low_ref, first):
    for rows in strips(kept_ref.shape[1]):
        value = kept_ref[0, rows]
        for ref in received:
            value = value + decode(ref[0, rows])
        out = pl.ds(first + rows.start, rows.size)
        high_ref[out], low_ref[out] = halves(value)


def gram_part(high_ref, low_ref):
    part = None
    for start in range(0, high_ref.shape[0] - BLOCK + 1, BLOCK):
        rows = pl.ds(start, BLOCK)
        high = high_ref[rows]
        more = dot(high.T, jnp.concatenate([high, low_ref[rows]], axis=1))
        part = more if part is None else part + more
    return part


def gather_kernel(*refs):
    kept_refs, received, high_ref, low_ref, part_ref = refs[:3], refs[3:12], *refs[12:]
    for place, kept_ref in enumerate(kept_refs):
        split_sums(kept_ref, received[3 * place : 3 * place + 3], high_ref, low_ref, FIRST[1 + place])
    part_ref[...] = gram_part(high_ref, low_ref)


def gather_call(kept, received):
    whole = pl.BlockSpec(memory_space=pltpu.VMEM)
    rows = FIRST[0]
    split = jax.ShapeDtypeStruct((rows, FF), jnp.bfloat16)
    return pl.pallas_call(
        gather_kernel,
        in_specs=[whole] * (len(kept) + len(received)),
        out_specs=[whole] * 3,
        out_shape=[split, split, jax.ShapeDtypeStruct((FF, 2 * FF), jnp.float32)],
        compiler_params=pltpu.CompilerParams(vmem_limit_bytes=16 * 1024 * 1024),
        cost_estimate=pl.CostEstimate(
            flops=4 * rows * FF * FF, bytes_accessed=16 * rows * FF, transcendentals=8 * rows * FF
        ),
        name="gather",
    )(*kept, *received)


def iterate_kernel(kept_ref, *refs):
    received, early_high, early_low, part_ref, out_ref, high_ref, low_ref = refs[:3], *refs[3:]
    over = FIRST[0] % BLOCK
    high_ref[pl.ds(0, over)] = early_high[pl.ds(FIRST[0] - over, over)]
    low_ref[pl.ds(0, over)] = early_low[pl.ds(FIRST[0] - over, over)]
    split_sums(kept_ref, received, high_ref, low_ref, over)
    part = part_ref[...] + gram_part(high_ref, low_ref)
    gram = part[:, :FF] + (part[:, FF:] + part[:, FF:].T)

    row = lax.broadcasted_iota(jnp.int32, (FF, FF), 0)
    column = lax.broadcasted_iota(jnp.int32, (FF, FF), 1)
    on_diagonal = row == column
    squares = jnp.sum(jnp.where(on_diagonal, gram, 0.0))
    scale = 1.0 / (jnp.sqrt(jnp.full((1, 1), squares)) + 1e-07 / GAIN * 2**SHIFT)
    a = gram * scale * scale
    power = None
    for turn in range(NS_ITERS):
        a_split = halves(a)
        b = -4.775 * a + 2.0315 * symmetric(a_split, a_split)
        b_split = halves(b)
        if power is None:
            power = jnp.where(on_diagonal, 3.4445, 0.0) + b
        else:
            power = 3.4445 * power + symmetric(halves(power), b_split)
        if turn < NS_ITERS - 1:
            once = 3.4445 * a + symmetric(a_split, b_split)
            a = 3.4445 * once + symmetric(halves(once), b_split)
    power_split = tall(halves(power * (scale * float(max(D, FF)) ** 0.5)))
    for start in range(0, D, BLOCK):
        rows = pl.ds(start, BLOCK)
        if start + BLOCK <= FIRST[0]:
            left = (early_high[rows], early_low[rows])
        else:
            left = (high_ref[...], low_ref[...])
        out_ref[rows] = dot(wide(left), power_split).astype(jnp.bfloat16)


def iterate_call(kept, received, early):
    whole = pl.BlockSpec(memory_space=pltpu.VMEM)
    return pl.pallas_call(
        iterate_kernel,
        in_specs=[whole] * (1 + len(received) + len(early)),
        out_specs=whole,
        scratch_shapes=[pltpu.VMEM((BLOCK, FF), jnp.bfloat16)] * 2,
        out_shape=jax.ShapeDtypeStruct((D, FF), jnp.bfloat16),
        compiler_params=pltpu.CompilerParams(vmem_limit_bytes=16 * 1024 * 1024),
        cost_estimate=pl.CostEstimate(
            flops=3 * 2 * FF * FF * (17 * FF + D), bytes_accessed=6 * 1024 * 1024, transcendentals=0
        ),
        name="newton_schulz",
    )(kept, *received, *early)


def local(grad_parts, momentum):
    parts = grad_parts[0]

    def send(codes, step):
        return [lax.ppermute(codes[quarter], "rep", partners(ORDERS[quarter][step])) for quarter in range(4)]

    codes = first_calls(parts, momentum)
    kept = keep_call(parts, momentum, codes)
    first = send(codes, 0)
    codes = [step_call(quarter, 1, kept[quarter], [first[quarter]]) for quarter in range(4)]
    base = fold_call(kept, first, codes[0])
    second = send(codes, 1)
    codes = [step_call(quarter, 2, base[quarter], [second[quarter]]) for quarter in range(4)]
    third = send(codes, 2)
    codes = [step_call(quarter, 3, base[quarter], [second[quarter], third[quarter]]) for quarter in range(4)]
    received = list(zip(second, third, send(codes, 3)))
    early = gather_call(base[1:], sum(received[1:], ()))
    update = iterate_call(base[0], received[0], early)
    return lax.all_to_all(update.reshape(16, BAND, FF), "rep", split_axis=0, concat_axis=0, tiled=True)


def solution(mesh):
    return jax.shard_map(
        local,
        mesh=mesh,
        in_specs=(P("rep", "exp", None, None), P("exp", "rep", None)),
        out_specs=P("exp", "rep", None),
        check_vma=False,
    )
```

time: 120 us -> 116 us (0.967)
  Pallas kernels: 39.6 us -> 34.5 us
  starting transfers between devices: 24 us -> 27.1 us
    pallas_call x16 -> x18, Pallas kernels: 19.7 us -> 16.1 us  [the longest x4 6.25 us: first_calls(): pl.pallas_call(functools.partial(first_kernel, quarter), in_specs=[hbm, w...]
    ppermute x16, starting transfers between devices: 24 us -> 27.1 us  [send(): lax.ppermute(codes[quarter], 'rep', partners(ORDERS[quarter][step]))]
  transfers between devices with their start and end apart: 16 -> 16, of which waited for: 12 -> 7; matrix products, arithmetic and copies ran while one was open for 0% -> 0% of each run, Pallas kernels for 20% -> 16%
where the time goes in v3:
time: 116 us
  waiting for transfers between devices  37.3 us (32%)
  Pallas kernels  34.5 us (30%)
  starting transfers between devices  27.1 us (23%)
  blocking collectives  15.7 us (14%)
    ppermute x16, waiting for transfers between devices, send(): lax.ppermute(codes[quarter], 'rep', partners(ORDERS[quarter][step]))  37.3 us
    ppermute x16, starting transfers between devices, send(): lax.ppermute(codes[quarter], 'rep', partners(ORDERS[quarter][step]))  27.1 us
    all_to_all x1, blocking collectives, local(): lax.all_to_all(update.reshape(16, BAND, FF), 'rep', split_axis=0, concat_...  15.7 us
    pallas_call x1, Pallas kernels, iterate_call(): pl.pallas_call(iterate_kernel, in_specs=[whole] * (1 + len(received) + le...  11.7 us
    pallas_call x4, Pallas kernels, first_calls(): pl.pallas_call(functools.partial(first_kernel, quarter), in_specs=[hbm, w...  6.25 us
    pallas_call x12, Pallas kernels, step_call(): pl.pallas_call(functools.partial(step_kernel, count), in_specs=[whole] *...  5.76 us
    pallas_call x1, Pallas kernels, keep_call(): pl.pallas_call(keep_kernel, in_specs=[pl.BlockSpec(memory_space=pltpu.HBM...  4.95 us
  transfers between devices with their start and end apart: 16, of which 7 were waited for; matrix products, arithmetic and copies ran while one was open for 0% of the time, Pallas kernels for 16%

profile of v3, /device:TPU:0, one launch (start us, length us, event | category | flops | bytes accessed | tf_op | source)
XLA Modules:
  0.0 115.7 jit_solution(8734121356302773423)
XLA Ops:
  0.0 0.0 copy-start
  0.0 2.0 %fetch.1.held_ref = f32[8,272,384]{2,1,0:T(8,128)S(1)} custom-call(f32[16,1024,384]{2,1,0:T(8,128)} %bitcast.3), custom_call_target="tpu_custom_call" | custom-call | bytes 6684672 | tf_op jit(solution)/shard_map/fetch/pallas_call | solution.py:118
  2.0 0.1 copy-done
  2.1 1.9 %first_q3.1 = (bf16[8,272,384]{2,1,0:T(8,128)(2,1)S(1)}, f32[8,256,384]{2,1,0:T(8,128)S(1)}) custom-call(f32[16,1024,384]{2,1,0:T(8,128)} %bitcast.4, bf16[16,64,384]{2,1,0:T(8,128)(2,1)S(1)} %copy-done, f32[8,272,384]{2,1,0:T(8,128)S(1)} %fetch.1.held_ref), custom_call_target="tpu_custom_call" | custom-call | flops 8355840 | bytes 5013504 | tf_op jit(solution)/shard_map/first_q3/pallas_call | solution.py:132
  4.0 1.7 %collective-permute-start.3 = (bf16[8,272,384]{2,1,0:T(8,128)(2,1)S(1)}, bf16[8,272,384]{2,1,0:T(8,128)(2,1)S(1)}, u32[]{:S(2)}, u32[]{:S(2)}) collective-permute-start(bf16[8,272,384]{2,1,0:T(8,128)(2,1)S(1)} %get-tuple-element.27.refs_3_), channel_id=1, source_target_pairs={{0,8},{8,0},{16,24},{24,16},{32,40},{40,32},{48,56},{56,48},{64,72... | collective-permute-start | bytes 5013512 | tf_op jit(solution)/shard_map/ppermute | solution.py:363
  5.7 1.9 %first_q2.1 = (bf16[8,256,384]{2,1,0:T(8,128)(2,1)S(1)}, f32[8,256,384]{2,1,0:T(8,128)S(1)}) custom-call(f32[16,1024,384]{2,1,0:T(8,128)} %bitcast.5, bf16[16,64,384]{2,1,0:T(8,128)(2,1)S(1)} %copy-done, f32[8,256,384]{2,1,0:T(8,128)S(1)} %get-tuple-element.22.held_ref), custom_call_target="tpu_custom_call" | custom-call | flops 7864320 | bytes 4718592 | tf_op jit(solution)/shard_map/first_q2/pallas_call | solution.py:132
  7.6 1.7 %collective-permute-start.2 = (bf16[8,256,384]{2,1,0:T(8,128)(2,1)S(1)}, bf16[8,256,384]{2,1,0:T(8,128)(2,1)S(1)}, u32[]{:S(2)}, u32[]{:S(2)}) collective-permute-start(bf16[8,256,384]{2,1,0:T(8,128)(2,1)S(1)} %get-tuple-element.26.refs_2_), channel_id=1, source_target_pairs={{0,32},{8,40},{16,48},{24,56},{32,0},{40,8},{48,16},{56,24},{64,96... | collective-permute-start | bytes 4718600 | tf_op jit(solution)/shard_map/ppermute | solution.py:363
  9.3 1.8 %first_q1.1 = (bf16[8,256,384]{2,1,0:T(8,128)(2,1)S(1)}, f32[8,240,384]{2,1,0:T(8,128)S(1)}) custom-call(f32[16,1024,384]{2,1,0:T(8,128)} %bitcast.6, bf16[16,64,384]{2,1,0:T(8,128)(2,1)S(1)} %copy-done, f32[8,256,384]{2,1,0:T(8,128)S(1)} %get-tuple-element.23.held_ref), custom_call_target="tpu_custom_call" | custom-call | flops 7864320 | bytes 4718592 | tf_op jit(solution)/shard_map/first_q1/pallas_call | solution.py:132
  11.1 2.2 %collective-permute-start.1 = (bf16[8,256,384]{2,1,0:T(8,128)(2,1)S(1)}, bf16[8,256,384]{2,1,0:T(8,128)(2,1)S(1)}, u32[]{:S(2)}, u32[]{:S(2)}) collective-permute-start(bf16[8,256,384]{2,1,0:T(8,128)(2,1)S(1)} %get-tuple-element.25.refs_1_), channel_id=1, source_target_pairs={{0,24},{8,16},{16,8},{24,0},{32,56},{40,48},{48,40},{56,32},{64,88... | collective-permute-start | bytes 4718600 | tf_op jit(solution)/shard_map/ppermute | solution.py:363
  13.3 0.6 first_q0.1.refs_0_
  13.9 2.7 %collective-permute-start = (bf16[8,240,384]{2,1,0:T(8,128)(2,1)S(1)}, bf16[8,240,384]{2,1,0:T(8,128)(2,1)S(1)}, u32[]{:S(2)}, u32[]{:S(2)}) collective-permute-start(bf16[8,240,384]{2,1,0:T(8,128)(2,1)S(1)} %first_q0.1.refs_0_), channel_id=1, source_target_pairs={{0,96},{8,104},{16,112},{24,120},{32,64},{40,72},{48,80},{56,88},{... | collective-permute-start | bytes 4423688 | tf_op jit(solution)/shard_map/ppermute | solution.py:363
  16.6 5.0 %keep.1 = (f32[8,240,384]{2,1,0:T(8,128)S(1)}, f32[8,256,384]{2,1,0:T(8,128)S(1)}, f32[8,256,384]{2,1,0:T(8,128)S(1)}, f32[8,272,384]{2,1,0:T(8,128)S(1)}) custom-call(f32[16,1024,384]{2,1,0:T(8,128)} %bitcast.8, bf16[16,64,384]{2,1,0:T(8,128)(2,1)S(1)} %copy-done, bf16[8,240,384]{2,1,0:T(8,128)(2,1)S(1)} %first_q0.1.refs_0_, ...), custom_call_target="tpu_custom_call" | custom-call | flops 3145728 | bytes 25165824 | tf_op jit(solution)/shard_map/keep/pallas_call | solution.py:173
  21.6 20.6 %collective-permute-done.3.refs_7_.refs_0_ = bf16[8,272,384]{2,1,0:T(8,128)(2,1)S(1)} collective-permute-done((bf16[8,272,384]{2,1,0:T(8,128)(2,1)S(1)}, bf16[8,272,384]{2,1,0:T(8,128)(2,1)S(1)}, u32[]{:S(2)}, u32[]{:S(2)}) %collective-permute-start.3) | collective-permute-done | bytes 1671200 | tf_op jit(solution)/shard_map/ppermute | solution.py:363
  42.2 0.8 codes_q3_s1.1
  43.0 1.9 %collective-permute-start.13 = (bf16[4,272,384]{2,1,0:T(8,128)(2,1)S(1)}, bf16[4,272,384]{2,1,0:T(8,128)(2,1)S(1)}, u32[]{:S(2)}, u32[]{:S(2)}) collective-permute-start(bf16[4,272,384]{2,1,0:T(8,128)(2,1)S(1)} %codes_q3_s1.1), channel_id=1, source_target_pairs={{0,32},{8,40},{16,48},{24,56},{32,0},{40,8},{48,16},{56,24},{64,96... | collective-permute-start | bytes 2506760 | tf_op jit(solution)/shard_map/ppermute | solution.py:363
  44.9 0.0 collective-permute-done.2.refs_6_.refs_0_
  44.9 0.8 codes_q2_s1.1
  45.7 2.8 %collective-permute-start.10 = (bf16[4,256,384]{2,1,0:T(8,128)(2,1)S(1)}, bf16[4,256,384]{2,1,0:T(8,128)(2,1)S(1)}, u32[]{:S(2)}, u32[]{:S(2)}) collective-permute-start(bf16[4,256,384]{2,1,0:T(8,128)(2,1)S(1)} %codes_q2_s1.1), channel_id=1, source_target_pairs={{0,24},{8,16},{16,8},{24,0},{32,56},{40,48},{48,40},{56,32},{64,88... | collective-permute-start | bytes 2359304 | tf_op jit(solution)/shard_map/ppermute | solution.py:363
  48.5 0.0 collective-permute-done.1.refs_5_.refs_0_
  48.5 0.8 codes_q1_s1.1
  49.3 2.3 %collective-permute-start.7 = (bf16[4,256,384]{2,1,0:T(8,128)(2,1)S(1)}, bf16[4,256,384]{2,1,0:T(8,128)(2,1)S(1)}, u32[]{:S(2)}, u32[]{:S(2)}) collective-permute-start(bf16[4,256,384]{2,1,0:T(8,128)(2,1)S(1)} %codes_q1_s1.1), channel_id=1, source_target_pairs={{0,96},{8,104},{16,112},{24,120},{32,64},{40,72},{48,80},{56,88},{... | collective-permute-start | bytes 2359304 | tf_op jit(solution)/shard_map/ppermute | solution.py:363
  51.6 0.0 collective-permute-done.refs_0_.refs_4_
  51.6 0.7 codes_q0_s1.1.refs_8_
  52.3 0.3 collective-permute-start.4
  52.6 2.1 %fold.1 = (f32[4,240,384]{2,1,0:T(8,128)S(1)}, f32[4,256,384]{2,1,0:T(8,128)S(1)}, f32[4,256,384]{2,1,0:T(8,128)S(1)}, f32[4,272,384]{2,1,0:T(8,128)S(1)}) custom-call(f32[8,240,384]{2,1,0:T(8,128)S(1)} %get-tuple-element.28.base_ref.refs_0_, f32[8,256,384]{2,1,0:T(8,128)S(1)} %get-tuple-element.29.refs_1_.base_ref, ...), custom_call_target="tpu_custom_call" | custom-call | flops 12582912 | bytes 15728640 | tf_op jit(solution)/shard_map/fold/pallas_call | solution.py:198
  54.6 8.0 %collective-permute-done.13.refs_0_.refs_9_ = bf16[4,272,384]{2,1,0:T(8,128)(2,1)S(1)} collective-permute-done((bf16[4,272,384]{2,1,0:T(8,128)(2,1)S(1)}, bf16[4,272,384]{2,1,0:T(8,128)(2,1)S(1)}, u32[]{:S(2)}, u32[]{:S(2)}) %collective-permute-start.13) | collective-permute-done | bytes 835616 | tf_op jit(solution)/shard_map/ppermute | solution.py:363
  62.6 0.4 codes_q3_s2.1
  63.0 3.0 %collective-permute-start.14 = (bf16[2,272,384]{2,1,0:T(8,128)(2,1)S(1)}, bf16[2,272,384]{2,1,0:T(8,128)(2,1)S(1)}, u32[]{:S(2)}, u32[]{:S(2)}) collective-permute-start(bf16[2,272,384]{2,1,0:T(8,128)(2,1)S(1)} %codes_q3_s2.1), channel_id=1, source_target_pairs={{0,24},{8,16},{16,8},{24,0},{32,56},{40,48},{48,40},{56,32},{64,88... | collective-permute-start | bytes 1253384 | tf_op jit(solution)/shard_map/ppermute | solution.py:363
  66.0 0.0 collective-permute-done.10.refs_0_.refs_6_
  66.1 0.4 codes_q2_s2.1
  66.4 3.1 %collective-permute-start.11 = (bf16[2,256,384]{2,1,0:T(8,128)(2,1)S(1)}, bf16[2,256,384]{2,1,0:T(8,128)(2,1)S(1)}, u32[]{:S(2)}, u32[]{:S(2)}) collective-permute-start(bf16[2,256,384]{2,1,0:T(8,128)(2,1)S(1)} %codes_q2_s2.1), channel_id=1, source_target_pairs={{0,96},{8,104},{16,112},{24,120},{32,64},{40,72},{48,80},{56,88},{... | collective-permute-start | bytes 1179656 | tf_op jit(solution)/shard_map/ppermute | solution.py:363
  69.5 0.0 collective-permute-done.7.refs_0_.refs_3_
  69.5 0.4 codes_q1_s2.1
  69.9 0.3 collective-permute-start.8
  70.2 0.0 collective-permute-done.4.refs_0_
  70.2 0.4 codes_q0_s2.1
  70.6 0.2 collective-permute-start.5
  70.8 3.3 %collective-permute-done.14.refs_1_.refs_10_ = bf16[2,272,384]{2,1,0:T(8,128)(2,1)S(1)} collective-permute-done((bf16[2,272,384]{2,1,0:T(8,128)(2,1)S(1)}, bf16[2,272,384]{2,1,0:T(8,128)(2,1)S(1)}, u32[]{:S(2)}, u32[]{:S(2)}) %collective-permute-start.14) | collective-permute-done | bytes 417824 | tf_op jit(solution)/shard_map/ppermute | solution.py:363
  74.1 0.3 codes_q3_s3.1
  74.4 3.1 %collective-permute-start.15 = (bf16[1,272,384]{2,1,0:T(8,128)(2,1)S(1)}, bf16[1,272,384]{2,1,0:T(8,128)(2,1)S(1)}, u32[]{:S(2)}, u32[]{:S(2)}) collective-permute-start(bf16[1,272,384]{2,1,0:T(8,128)(2,1)S(1)} %codes_q3_s3.1), channel_id=1, source_target_pairs={{0,96},{8,104},{16,112},{24,120},{32,64},{40,72},{48,80},{56,88},{... | collective-permute-start | bytes 626696 | tf_op jit(solution)/shard_map/ppermute | solution.py:363
  77.5 0.6 collective-permute-done.11.refs_1_.refs_7_
  78.1 0.3 codes_q2_s3.1
  78.4 0.3 collective-permute-start.12
  78.7 0.9 collective-permute-done.8.refs_1_.refs_4_
  79.6 0.3 codes_q1_s3.1
  79.9 0.2 collective-permute-start.9
  80.1 0.0 collective-permute-done.5.refs_1_
  80.1 0.3 codes_q0_s3.1
  80.4 1.3 %collective-permute-start.6 = (bf16[1,240,384]{2,1,0:T(8,128)(2,1)S(1)}, bf16[1,240,384]{2,1,0:T(8,128)(2,1)S(1)}, u32[]{:S(2)}, u32[]{:S(2)}) collective-permute-start(bf16[1,240,384]{2,1,0:T(8,128)(2,1)S(1)} %codes_q0_s3.1), channel_id=1, source_target_pairs={{0,24},{8,16},{16,8},{24,0},{32,56},{40,48},{48,40},{56,32},{64,88... | collective-permute-start | bytes 552968 | tf_op jit(solution)/shard_map/ppermute | solution.py:363
  81.8 2.4 %collective-permute-done.12.refs_8_ = bf16[1,256,384]{2,1,0:T(8,128)(2,1)S(1)} collective-permute-done((bf16[1,256,384]{2,1,0:T(8,128)(2,1)S(1)}, bf16[1,256,384]{2,1,0:T(8,128)(2,1)S(1)}, u32[]{:S(2)}, u32[]{:S(2)}) %collective-permute-start.12) | collective-permute-done | bytes 196640 | tf_op jit(solution)/shard_map/ppermute | solution.py:363
  84.2 1.5 %collective-permute-done.9.refs_5_ = bf16[1,256,384]{2,1,0:T(8,128)(2,1)S(1)} collective-permute-done((bf16[1,256,384]{2,1,0:T(8,128)(2,1)S(1)}, bf16[1,256,384]{2,1,0:T(8,128)(2,1)S(1)}, u32[]{:S(2)}, u32[]{:S(2)}) %collective-permute-start.9) | collective-permute-done | bytes 196640 | tf_op jit(solution)/shard_map/ppermute | solution.py:363
  85.7 0.0 collective-permute-done.15.refs_11_
  85.7 1.7 %gather.1 = (bf16[784,384]{1,0:T(8,128)(2,1)S(1)}, bf16[784,384]{1,0:T(8,128)(2,1)S(1)}, f32[384,768]{1,0:T(8,128)S(1)}) custom-call(f32[4,256,384]{2,1,0:T(8,128)S(1)} %get-tuple-element.33.base_ref.refs_0_, f32[4,256,384]{2,1,0:T(8,128)S(1)} %get-tuple-element.34.base_ref.refs_1_, f32[4,272,384]{2,1,0:T(8,128)S(1)} %get-tuple-element.35.base_ref.refs_2_, ...), custom_call_target="tpu_custom_call" | custom-call | flops 462422016 | bytes 4816896 | tf_op jit(solution)/shard_map/gather/pallas_call | solution.py:293
  87.4 0.0 collective-permute-done.6.refs_2_
  87.4 11.7 %newton_schulz.1 = bf16[1024,384]{1,0:T(8,128)(2,1)S(1)} custom-call(f32[4,240,384]{2,1,0:T(8,128)S(1)} %get-tuple-element.32.base_ref.kept_ref, bf16[4,240,384]{2,1,0:T(8,128)(2,1)S(1)} %collective-permute-done.4.refs_0_, bf16[2,240,384]{2,1,0:T(8,128)(2,1)S(1)} %collective-permute-done.5.refs_1_, bf16[1,240,384]{2,1,0:T(8,128)(2,1)S(1)} %collective-permute-done.6.refs_2_, ...), custom_call_target="tpu_custom_call" | custom-call | flops 6681526272 | bytes 6291456 | tf_op jit(solution)/shard_map/newton_schulz/pallas_call | solution.py:345
  99.2 15.7 %all_to_all.5 = bf16[16,64,384]{2,1,0:T(8,128)(2,1)S(1)} all-to-all(bf16[16,64,384]{2,1,0:T(8,128)(2,1)S(1)} %bitcast.2), channel_id=1, replica_groups=mesh['rep'=16,'exp'=8] {'rep'}, dimensions={0} | all-to-all | bytes 1572864 | tf_op jit(solution)/shard_map/all_to_all | solution.py:377
  114.8 0.9 copy.4
Async XLA Ops:
  0.0 2.1 %copy-start = (bf16[16,64,384]{2,1,0:T(8,128)(2,1)S(1)}, bf16[16,64,384]{2,1,0:T(8,128)(2,1)}, u32[]{:S(2)}) copy-start(bf16[16,64,384]{2,1,0:T(8,128)(2,1)} %momentum_ref.9) | copy-start | bytes 2359300
  4.0 38.2 %collective-permute-start.3 = (bf16[8,272,384]{2,1,0:T(8,128)(2,1)S(1)}, bf16[8,272,384]{2,1,0:T(8,128)(2,1)S(1)}, u32[]{:S(2)}, u32[]{:S(2)}) collective-permute-start(bf16[8,272,384]{2,1,0:T(8,128)(2,1)S(1)} %get-tuple-element.27.refs_3_), channel_id=1, source_target_pairs={{0,8},{8,0},{16,24},{24,16},{32,40},{40,32},{48,56},{56,48},{64,72... | collective-permute-start | bytes 5013512 | tf_op jit(solution)/shard_map/ppermute | solution.py:363
  7.6 37.3 %collective-permute-start.2 = (bf16[8,256,384]{2,1,0:T(8,128)(2,1)S(1)}, bf16[8,256,384]{2,1,0:T(8,128)(2,1)S(1)}, u32[]{:S(2)}, u32[]{:S(2)}) collective-permute-start(bf16[8,256,384]{2,1,0:T(8,128)(2,1)S(1)} %get-tuple-element.26.refs_2_), channel_id=1, source_target_pairs={{0,32},{8,40},{16,48},{24,56},{32,0},{40,8},{48,16},{56,24},{64,96... | collective-permute-start | bytes 4718600 | tf_op jit(solution)/shard_map/ppermute | solution.py:363
  11.1 37.4 %collective-permute-start.1 = (bf16[8,256,384]{2,1,0:T(8,128)(2,1)S(1)}, bf16[8,256,384]{2,1,0:T(8,128)(2,1)S(1)}, u32[]{:S(2)}, u32[]{:S(2)}) collective-permute-start(bf16[8,256,384]{2,1,0:T(8,128)(2,1)S(1)} %get-tuple-element.25.refs_1_), channel_id=1, source_target_pairs={{0,24},{8,16},{16,8},{24,0},{32,56},{40,48},{48,40},{56,32},{64,88... | collective-permute-start | bytes 4718600 | tf_op jit(solution)/shard_map/ppermute | solution.py:363
  13.9 37.7 %collective-permute-start = (bf16[8,240,384]{2,1,0:T(8,128)(2,1)S(1)}, bf16[8,240,384]{2,1,0:T(8,128)(2,1)S(1)}, u32[]{:S(2)}, u32[]{:S(2)}) collective-permute-start(bf16[8,240,384]{2,1,0:T(8,128)(2,1)S(1)} %first_q0.1.refs_0_), channel_id=1, source_target_pairs={{0,96},{8,104},{16,112},{24,120},{32,64},{40,72},{48,80},{56,88},{... | collective-permute-start | bytes 4423688 | tf_op jit(solution)/shard_map/ppermute | solution.py:363
  43.0 19.6 %collective-permute-start.13 = (bf16[4,272,384]{2,1,0:T(8,128)(2,1)S(1)}, bf16[4,272,384]{2,1,0:T(8,128)(2,1)S(1)}, u32[]{:S(2)}, u32[]{:S(2)}) collective-permute-start(bf16[4,272,384]{2,1,0:T(8,128)(2,1)S(1)} %codes_q3_s1.1), channel_id=1, source_target_pairs={{0,32},{8,40},{16,48},{24,56},{32,0},{40,8},{48,16},{56,24},{64,96... | collective-permute-start | bytes 2506760 | tf_op jit(solution)/shard_map/ppermute | solution.py:363
  45.7 20.4 %collective-permute-start.10 = (bf16[4,256,384]{2,1,0:T(8,128)(2,1)S(1)}, bf16[4,256,384]{2,1,0:T(8,128)(2,1)S(1)}, u32[]{:S(2)}, u32[]{:S(2)}) collective-permute-start(bf16[4,256,384]{2,1,0:T(8,128)(2,1)S(1)} %codes_q2_s1.1), channel_id=1, source_target_pairs={{0,24},{8,16},{16,8},{24,0},{32,56},{40,48},{48,40},{56,32},{64,88... | collective-permute-start | bytes 2359304 | tf_op jit(solution)/shard_map/ppermute | solution.py:363
  49.3 20.2 %collective-permute-start.7 = (bf16[4,256,384]{2,1,0:T(8,128)(2,1)S(1)}, bf16[4,256,384]{2,1,0:T(8,128)(2,1)S(1)}, u32[]{:S(2)}, u32[]{:S(2)}) collective-permute-start(bf16[4,256,384]{2,1,0:T(8,128)(2,1)S(1)} %codes_q1_s1.1), channel_id=1, source_target_pairs={{0,96},{8,104},{16,112},{24,120},{32,64},{40,72},{48,80},{56,88},{... | collective-permute-start | bytes 2359304 | tf_op jit(solution)/shard_map/ppermute | solution.py:363
  52.3 18.0 %collective-permute-start.4 = (bf16[4,240,384]{2,1,0:T(8,128)(2,1)S(1)}, bf16[4,240,384]{2,1,0:T(8,128)(2,1)S(1)}, u32[]{:S(2)}, u32[]{:S(2)}) collective-permute-start(bf16[4,240,384]{2,1,0:T(8,128)(2,1)S(1)} %codes_q0_s1.1.refs_8_), channel_id=1, source_target_pairs={{0,8},{8,0},{16,24},{24,16},{32,40},{40,32},{48,56},{56,48},{64,72... | collective-permute-start | bytes 2211848 | tf_op jit(solution)/shard_map/ppermute | solution.py:363
  63.0 11.0 %collective-permute-start.14 = (bf16[2,272,384]{2,1,0:T(8,128)(2,1)S(1)}, bf16[2,272,384]{2,1,0:T(8,128)(2,1)S(1)}, u32[]{:S(2)}, u32[]{:S(2)}) collective-permute-start(bf16[2,272,384]{2,1,0:T(8,128)(2,1)S(1)} %codes_q3_s2.1), channel_id=1, source_target_pairs={{0,24},{8,16},{16,8},{24,0},{32,56},{40,48},{48,40},{56,32},{64,88... | collective-permute-start | bytes 1253384 | tf_op jit(solution)/shard_map/ppermute | solution.py:363
  66.4 11.7 %collective-permute-start.11 = (bf16[2,256,384]{2,1,0:T(8,128)(2,1)S(1)}, bf16[2,256,384]{2,1,0:T(8,128)(2,1)S(1)}, u32[]{:S(2)}, u32[]{:S(2)}) collective-permute-start(bf16[2,256,384]{2,1,0:T(8,128)(2,1)S(1)} %codes_q2_s2.1), channel_id=1, source_target_pairs={{0,96},{8,104},{16,112},{24,120},{32,64},{40,72},{48,80},{56,88},{... | collective-permute-start | bytes 1179656 | tf_op jit(solution)/shard_map/ppermute | solution.py:363
  69.9 9.7 %collective-permute-start.8 = (bf16[2,256,384]{2,1,0:T(8,128)(2,1)S(1)}, bf16[2,256,384]{2,1,0:T(8,128)(2,1)S(1)}, u32[]{:S(2)}, u32[]{:S(2)}) collective-permute-start(bf16[2,256,384]{2,1,0:T(8,128)(2,1)S(1)} %codes_q1_s2.1), channel_id=1, source_target_pairs={{0,8},{8,0},{16,24},{24,16},{32,40},{40,32},{48,56},{56,48},{64,72... | collective-permute-start | bytes 1179656 | tf_op jit(solution)/shard_map/ppermute | solution.py:363
  70.6 9.5 %collective-permute-start.5 = (bf16[2,240,384]{2,1,0:T(8,128)(2,1)S(1)}, bf16[2,240,384]{2,1,0:T(8,128)(2,1)S(1)}, u32[]{:S(2)}, u32[]{:S(2)}) collective-permute-start(bf16[2,240,384]{2,1,0:T(8,128)(2,1)S(1)} %codes_q0_s2.1), channel_id=1, source_target_pairs={{0,32},{8,40},{16,48},{24,56},{32,0},{40,8},{48,16},{56,24},{64,96... | collective-permute-start | bytes 1105928 | tf_op jit(solution)/shard_map/ppermute | solution.py:363
  74.4 11.3 %collective-permute-start.15 = (bf16[1,272,384]{2,1,0:T(8,128)(2,1)S(1)}, bf16[1,272,384]{2,1,0:T(8,128)(2,1)S(1)}, u32[]{:S(2)}, u32[]{:S(2)}) collective-permute-start(bf16[1,272,384]{2,1,0:T(8,128)(2,1)S(1)} %codes_q3_s3.1), channel_id=1, source_target_pairs={{0,96},{8,104},{16,112},{24,120},{32,64},{40,72},{48,80},{56,88},{... | collective-permute-start | bytes 626696 | tf_op jit(solution)/shard_map/ppermute | solution.py:363
  78.4 5.7 %collective-permute-start.12 = (bf16[1,256,384]{2,1,0:T(8,128)(2,1)S(1)}, bf16[1,256,384]{2,1,0:T(8,128)(2,1)S(1)}, u32[]{:S(2)}, u32[]{:S(2)}) collective-permute-start(bf16[1,256,384]{2,1,0:T(8,128)(2,1)S(1)} %codes_q2_s3.1), channel_id=1, source_target_pairs={{0,8},{8,0},{16,24},{24,16},{32,40},{40,32},{48,56},{56,48},{64,72... | collective-permute-start | bytes 589832 | tf_op jit(solution)/shard_map/ppermute | solution.py:363
  79.9 5.7 %collective-permute-start.9 = (bf16[1,256,384]{2,1,0:T(8,128)(2,1)S(1)}, bf16[1,256,384]{2,1,0:T(8,128)(2,1)S(1)}, u32[]{:S(2)}, u32[]{:S(2)}) collective-permute-start(bf16[1,256,384]{2,1,0:T(8,128)(2,1)S(1)} %codes_q1_s3.1), channel_id=1, source_target_pairs={{0,32},{8,40},{16,48},{24,56},{32,0},{40,8},{48,16},{56,24},{64,96... | collective-permute-start | bytes 589832 | tf_op jit(solution)/shard_map/ppermute | solution.py:363
  80.4 7.0 %collective-permute-start.6 = (bf16[1,240,384]{2,1,0:T(8,128)(2,1)S(1)}, bf16[1,240,384]{2,1,0:T(8,128)(2,1)S(1)}, u32[]{:S(2)}, u32[]{:S(2)}) collective-permute-start(bf16[1,240,384]{2,1,0:T(8,128)(2,1)S(1)} %codes_q0_s3.1), channel_id=1, source_target_pairs={{0,24},{8,16},{16,8},{24,0},{32,56},{40,48},{48,40},{56,32},{64,88... | collective-permute-start | bytes 552968 | tf_op jit(solution)/shard_map/ppermute | solution.py:363

commit v4 on v3

--- a/solution.py
+++ b/solution.py
@@ -27,13 +27,24 @@
 POWER = 9
 
 
-def partners(bit):
-    return [(rep, rep ^ FLIPS[bit]) for rep in range(16)]
+def flips_of(quarter, core):
+    return [FLIPS[bit] for bit in ORDERS[(quarter + 3 * core) % 4]]
+
+
+def partners(quarter, step):
+    pairs = []
+    for device in range(128):
+        rep, group = divmod(device, 8)
+        pairs.append((device, 8 * (rep ^ flips_of(quarter, group % 2)[step]) + group))
+    return pairs
 
 
 def expert_of(quarter, sent, index):
-    first, *others = [FLIPS[bit] for bit in ORDERS[quarter]]
-    expert = lax.axis_index("rep") ^ (first if sent else 0)
+    core = lax.axis_index("exp") & 1
+    first, *others = [zero + core * (one - zero) for zero, one in zip(flips_of(quarter, 0), flips_of(quarter, 1))]
+    expert = lax.axis_index("rep")
+    if sent:
+        expert = expert ^ first
     for place, flip in enumerate(others):
         expert = expert ^ (((index >> (2 - place)) & 1) * flip)
     return expert
@@ -323,13 +334,13 @@
         a_split = halves(a)
         b = -4.775 * a + 2.0315 * symmetric(a_split, a_split)
         b_split = halves(b)
+        if turn < NS_ITERS - 1:
+            once = 3.4445 * a + symmetric(a_split, b_split)
+            a = 3.4445 * once + symmetric(halves(once), b_split)
         if power is None:
             power = jnp.where(on_diagonal, 3.4445, 0.0) + b
         else:
             power = 3.4445 * power + symmetric(halves(power), b_split)
-        if turn < NS_ITERS - 1:
-            once = 3.4445 * a + symmetric(a_split, b_split)
-            a = 3.4445 * once + symmetric(halves(once), b_split)
     power_split = tall(halves(power * (scale * float(max(D, FF)) ** 0.5)))
     for start in range(0, D, BLOCK):
         rows = pl.ds(start, BLOCK)
@@ -360,7 +371,7 @@
     parts = grad_parts[0]
 
     def send(codes, step):
-        return [lax.ppermute(codes[quarter], "rep", partners(ORDERS[quarter][step])) for quarter in range(4)]
+        return [lax.ppermute(codes[quarter], ("rep", "exp"), partners(quarter, step)) for quarter in range(4)]
 
     codes = first_calls(parts, momentum)
     kept = keep_call(parts, momentum, codes)

time: 116 us -> 113 us (0.974)
  waiting for transfers between devices: 37.3 us -> 30.9 us
  starting transfers between devices: 27.1 us -> 28.9 us
  blocking collectives: 15.7 us -> 17.4 us
    ppermute x16, waiting for transfers between devices: 37.3 us -> 30.9 us  [send(): lax.ppermute(codes[quarter], ('rep', 'exp'), partners(quarter, step))]
    ppermute x16, starting transfers between devices: 27.1 us -> 28.9 us  [send(): lax.ppermute(codes[quarter], ('rep', 'exp'), partners(quarter, step))]
    all_to_all x1, blocking collectives: 15.7 us -> 17.4 us  [local(): lax.all_to_all(update.reshape(16, BAND, FF), 'rep', split_axis=0, concat_...]
  transfers between devices with their start and end apart: 16 -> 16, of which waited for: 7 -> 11; matrix products, arithmetic and copies ran while one was open for 0% -> 0% of each run, Pallas kernels for 16% -> 17%
where the time goes in v4:
time: 113 us; the launch traced here: 112 us
  Pallas kernels  34 us (30%)
  waiting for transfers between devices  30.9 us (27%)
  starting transfers between devices  28.9 us (26%)
  blocking collectives  17.4 us (15%)
    ppermute x16, waiting for transfers between devices, send(): lax.ppermute(codes[quarter], ('rep', 'exp'), partners(quarter, step))  30.9 us
    ppermute x16, starting transfers between devices, send(): lax.ppermute(codes[quarter], ('rep', 'exp'), partners(quarter, step))  28.9 us
    all_to_all x1, blocking collectives, local(): lax.all_to_all(update.reshape(16, BAND, FF), 'rep', split_axis=0, concat_...  17.4 us
    pallas_call x1, Pallas kernels, iterate_call(): pl.pallas_call(iterate_kernel, in_specs=[whole] * (1 + len(received) + le...  11.2 us
    pallas_call x4, Pallas kernels, first_calls(): pl.pallas_call(functools.partial(first_kernel, quarter), in_specs=[hbm, w...  6.29 us
    pallas_call x12, Pallas kernels, step_call(): pl.pallas_call(functools.partial(step_kernel, count), in_specs=[whole] *...  5.77 us
    pallas_call x1, Pallas kernels, keep_call(): pl.pallas_call(keep_kernel, in_specs=[pl.BlockSpec(memory_space=pltpu.HBM...  4.97 us
  transfers between devices with their start and end apart: 16, of which 11 were waited for; matrix products, arithmetic and copies ran while one was open for 0% of the time, Pallas kernels for 17%

profile of v4, /device:TPU:0, one launch (start us, length us, event | category | flops | bytes accessed | tf_op | source)
XLA Modules:
  0.0 112.4 jit_solution(2110371423534757793)
XLA Ops:
  0.0 0.0 copy-start
  0.0 2.0 %fetch.1.held_ref = f32[8,272,384]{2,1,0:T(8,128)S(1)} custom-call(f32[16,1024,384]{2,1,0:T(8,128)} %bitcast.3), custom_call_target="tpu_custom_call" | custom-call | bytes 6684672 | tf_op jit(solution)/shard_map/fetch/pallas_call | solution.py:129
  2.0 0.1 copy-done
  2.1 1.9 %first_q3.1 = (bf16[8,272,384]{2,1,0:T(8,128)(2,1)S(1)}, f32[8,256,384]{2,1,0:T(8,128)S(1)}) custom-call(f32[16,1024,384]{2,1,0:T(8,128)} %bitcast.4, bf16[16,64,384]{2,1,0:T(8,128)(2,1)S(1)} %copy-done, f32[8,272,384]{2,1,0:T(8,128)S(1)} %fetch.1.held_ref), custom_call_target="tpu_custom_call" | custom-call | flops 8355840 | bytes 5013504 | tf_op jit(solution)/shard_map/first_q3/pallas_call | solution.py:143
  4.0 1.7 %collective-permute-start.3 = (bf16[8,272,384]{2,1,0:T(8,128)(2,1)S(1)}, bf16[8,272,384]{2,1,0:T(8,128)(2,1)S(1)}, u32[]{:S(2)}, u32[]{:S(2)}) collective-permute-start(bf16[8,272,384]{2,1,0:T(8,128)(2,1)S(1)} %get-tuple-element.27.refs_3_), channel_id=1, source_target_pairs={{0,8},{1,33},{2,10},{3,35},{4,12},{5,37},{6,14},{7,39},{8,0},{9,41... | collective-permute-start | bytes 5013512 | tf_op jit(solution)/shard_map/ppermute | solution.py:374
  5.7 1.9 %first_q2.1 = (bf16[8,256,384]{2,1,0:T(8,128)(2,1)S(1)}, f32[8,256,384]{2,1,0:T(8,128)S(1)}) custom-call(f32[16,1024,384]{2,1,0:T(8,128)} %bitcast.5, bf16[16,64,384]{2,1,0:T(8,128)(2,1)S(1)} %copy-done, f32[8,256,384]{2,1,0:T(8,128)S(1)} %get-tuple-element.22.held_ref), custom_call_target="tpu_custom_call" | custom-call | flops 7864320 | bytes 4718592 | tf_op jit(solution)/shard_map/first_q2/pallas_call | solution.py:143
  7.6 1.7 %collective-permute-start.2 = (bf16[8,256,384]{2,1,0:T(8,128)(2,1)S(1)}, bf16[8,256,384]{2,1,0:T(8,128)(2,1)S(1)}, u32[]{:S(2)}, u32[]{:S(2)}) collective-permute-start(bf16[8,256,384]{2,1,0:T(8,128)(2,1)S(1)} %get-tuple-element.26.refs_2_), channel_id=1, source_target_pairs={{0,32},{1,25},{2,34},{3,27},{4,36},{5,29},{6,38},{7,31},{8,40},{9,... | collective-permute-start | bytes 4718600 | tf_op jit(solution)/shard_map/ppermute | solution.py:374
  9.3 1.8 %first_q1.1 = (bf16[8,256,384]{2,1,0:T(8,128)(2,1)S(1)}, f32[8,240,384]{2,1,0:T(8,128)S(1)}) custom-call(f32[16,1024,384]{2,1,0:T(8,128)} %bitcast.6, bf16[16,64,384]{2,1,0:T(8,128)(2,1)S(1)} %copy-done, f32[8,256,384]{2,1,0:T(8,128)S(1)} %get-tuple-element.23.held_ref), custom_call_target="tpu_custom_call" | custom-call | flops 7864320 | bytes 4718592 | tf_op jit(solution)/shard_map/first_q1/pallas_call | solution.py:143
  11.1 2.2 %collective-permute-start.1 = (bf16[8,256,384]{2,1,0:T(8,128)(2,1)S(1)}, bf16[8,256,384]{2,1,0:T(8,128)(2,1)S(1)}, u32[]{:S(2)}, u32[]{:S(2)}) collective-permute-start(bf16[8,256,384]{2,1,0:T(8,128)(2,1)S(1)} %get-tuple-element.25.refs_1_), channel_id=1, source_target_pairs={{0,24},{1,97},{2,26},{3,99},{4,28},{5,101},{6,30},{7,103},{8,16},{... | collective-permute-start | bytes 4718600 | tf_op jit(solution)/shard_map/ppermute | solution.py:374
  13.3 0.7 first_q0.1.refs_0_
  13.9 3.0 %collective-permute-start = (bf16[8,240,384]{2,1,0:T(8,128)(2,1)S(1)}, bf16[8,240,384]{2,1,0:T(8,128)(2,1)S(1)}, u32[]{:S(2)}, u32[]{:S(2)}) collective-permute-start(bf16[8,240,384]{2,1,0:T(8,128)(2,1)S(1)} %first_q0.1.refs_0_), channel_id=1, source_target_pairs={{0,96},{1,9},{2,98},{3,11},{4,100},{5,13},{6,102},{7,15},{8,104},{... | collective-permute-start | bytes 4423688 | tf_op jit(solution)/shard_map/ppermute | solution.py:374
  16.9 5.0 %keep.1 = (f32[8,240,384]{2,1,0:T(8,128)S(1)}, f32[8,256,384]{2,1,0:T(8,128)S(1)}, f32[8,256,384]{2,1,0:T(8,128)S(1)}, f32[8,272,384]{2,1,0:T(8,128)S(1)}) custom-call(f32[16,1024,384]{2,1,0:T(8,128)} %bitcast.8, bf16[16,64,384]{2,1,0:T(8,128)(2,1)S(1)} %copy-done, bf16[8,240,384]{2,1,0:T(8,128)(2,1)S(1)} %first_q0.1.refs_0_, ...), custom_call_target="tpu_custom_call" | custom-call | flops 3145728 | bytes 25165824 | tf_op jit(solution)/shard_map/keep/pallas_call | solution.py:184
  21.9 12.6 %collective-permute-done.3.refs_7_.refs_0_ = bf16[8,272,384]{2,1,0:T(8,128)(2,1)S(1)} collective-permute-done((bf16[8,272,384]{2,1,0:T(8,128)(2,1)S(1)}, bf16[8,272,384]{2,1,0:T(8,128)(2,1)S(1)}, u32[]{:S(2)}, u32[]{:S(2)}) %collective-permute-start.3) | collective-permute-done | bytes 1671200 | tf_op jit(solution)/shard_map/ppermute | solution.py:374
  34.5 0.8 codes_q3_s1.1
  35.3 2.6 %collective-permute-start.13 = (bf16[4,272,384]{2,1,0:T(8,128)(2,1)S(1)}, bf16[4,272,384]{2,1,0:T(8,128)(2,1)S(1)}, u32[]{:S(2)}, u32[]{:S(2)}) collective-permute-start(bf16[4,272,384]{2,1,0:T(8,128)(2,1)S(1)} %codes_q3_s1.1), channel_id=1, source_target_pairs={{0,32},{1,25},{2,34},{3,27},{4,36},{5,29},{6,38},{7,31},{8,40},{9,... | collective-permute-start | bytes 2506760 | tf_op jit(solution)/shard_map/ppermute | solution.py:374
  37.9 3.3 %collective-permute-done.2.refs_6_.refs_0_ = bf16[8,256,384]{2,1,0:T(8,128)(2,1)S(1)} collective-permute-done((bf16[8,256,384]{2,1,0:T(8,128)(2,1)S(1)}, bf16[8,256,384]{2,1,0:T(8,128)(2,1)S(1)}, u32[]{:S(2)}, u32[]{:S(2)}) %collective-permute-start.2) | collective-permute-done | bytes 1572896 | tf_op jit(solution)/shard_map/ppermute | solution.py:374
  41.2 0.8 codes_q2_s1.1
  42.0 3.0 %collective-permute-start.10 = (bf16[4,256,384]{2,1,0:T(8,128)(2,1)S(1)}, bf16[4,256,384]{2,1,0:T(8,128)(2,1)S(1)}, u32[]{:S(2)}, u32[]{:S(2)}) collective-permute-start(bf16[4,256,384]{2,1,0:T(8,128)(2,1)S(1)} %codes_q2_s1.1), channel_id=1, source_target_pairs={{0,24},{1,97},{2,26},{3,99},{4,28},{5,101},{6,30},{7,103},{8,16},{... | collective-permute-start | bytes 2359304 | tf_op jit(solution)/shard_map/ppermute | solution.py:374
  45.0 1.6 %collective-permute-done.1.refs_5_.refs_0_ = bf16[8,256,384]{2,1,0:T(8,128)(2,1)S(1)} collective-permute-done((bf16[8,256,384]{2,1,0:T(8,128)(2,1)S(1)}, bf16[8,256,384]{2,1,0:T(8,128)(2,1)S(1)}, u32[]{:S(2)}, u32[]{:S(2)}) %collective-permute-start.1) | collective-permute-done | bytes 1572896 | tf_op jit(solution)/shard_map/ppermute | solution.py:374
  46.6 0.8 codes_q1_s1.1
  47.4 1.5 %collective-permute-start.7 = (bf16[4,256,384]{2,1,0:T(8,128)(2,1)S(1)}, bf16[4,256,384]{2,1,0:T(8,128)(2,1)S(1)}, u32[]{:S(2)}, u32[]{:S(2)}) collective-permute-start(bf16[4,256,384]{2,1,0:T(8,128)(2,1)S(1)} %codes_q1_s1.1), channel_id=1, source_target_pairs={{0,96},{1,9},{2,98},{3,11},{4,100},{5,13},{6,102},{7,15},{8,104},{... | collective-permute-start | bytes 2359304 | tf_op jit(solution)/shard_map/ppermute | solution.py:374
  48.9 0.9 collective-permute-done.refs_0_.refs_4_
  49.7 0.7 codes_q0_s1.1.refs_8_
  50.4 0.7 collective-permute-start.4
  51.1 2.1 %fold.1 = (f32[4,240,384]{2,1,0:T(8,128)S(1)}, f32[4,256,384]{2,1,0:T(8,128)S(1)}, f32[4,256,384]{2,1,0:T(8,128)S(1)}, f32[4,272,384]{2,1,0:T(8,128)S(1)}) custom-call(f32[8,240,384]{2,1,0:T(8,128)S(1)} %get-tuple-element.28.base_ref.refs_0_, f32[8,256,384]{2,1,0:T(8,128)S(1)} %get-tuple-element.29.refs_1_.base_ref, ...), custom_call_target="tpu_custom_call" | custom-call | flops 12582912 | bytes 15728640 | tf_op jit(solution)/shard_map/fold/pallas_call | solution.py:209
  53.2 0.0 collective-permute-done.13.refs_0_.refs_9_
  53.2 0.4 codes_q3_s2.1
  53.6 3.0 %collective-permute-start.14 = (bf16[2,272,384]{2,1,0:T(8,128)(2,1)S(1)}, bf16[2,272,384]{2,1,0:T(8,128)(2,1)S(1)}, u32[]{:S(2)}, u32[]{:S(2)}) collective-permute-start(bf16[2,272,384]{2,1,0:T(8,128)(2,1)S(1)} %codes_q3_s2.1), channel_id=1, source_target_pairs={{0,24},{1,97},{2,26},{3,99},{4,28},{5,101},{6,30},{7,103},{8,16},{... | collective-permute-start | bytes 1253384 | tf_op jit(solution)/shard_map/ppermute | solution.py:374
  56.6 5.6 %collective-permute-done.10.refs_0_.refs_6_ = bf16[4,256,384]{2,1,0:T(8,128)(2,1)S(1)} collective-permute-done((bf16[4,256,384]{2,1,0:T(8,128)(2,1)S(1)}, bf16[4,256,384]{2,1,0:T(8,128)(2,1)S(1)}, u32[]{:S(2)}, u32[]{:S(2)}) %collective-permute-start.10) | collective-permute-done | bytes 786464 | tf_op jit(solution)/shard_map/ppermute | solution.py:374
  62.2 0.4 codes_q2_s2.1
  62.6 2.2 %collective-permute-start.11 = (bf16[2,256,384]{2,1,0:T(8,128)(2,1)S(1)}, bf16[2,256,384]{2,1,0:T(8,128)(2,1)S(1)}, u32[]{:S(2)}, u32[]{:S(2)}) collective-permute-start(bf16[2,256,384]{2,1,0:T(8,128)(2,1)S(1)} %codes_q2_s2.1), channel_id=1, source_target_pairs={{0,96},{1,9},{2,98},{3,11},{4,100},{5,13},{6,102},{7,15},{8,104},{... | collective-permute-start | bytes 1179656 | tf_op jit(solution)/shard_map/ppermute | solution.py:374
  64.9 0.2 collective-permute-done.7.refs_0_.refs_3_
  65.1 0.4 codes_q1_s2.1
  65.5 0.3 collective-permute-start.8
  65.8 0.7 collective-permute-done.4.refs_0_
  66.4 0.4 codes_q0_s2.1
  66.8 0.1 collective-permute-start.5
  66.9 0.0 collective-permute-done.14.refs_1_.refs_10_
  66.9 0.3 codes_q3_s3.1
  67.2 2.4 %collective-permute-start.15 = (bf16[1,272,384]{2,1,0:T(8,128)(2,1)S(1)}, bf16[1,272,384]{2,1,0:T(8,128)(2,1)S(1)}, u32[]{:S(2)}, u32[]{:S(2)}) collective-permute-start(bf16[1,272,384]{2,1,0:T(8,128)(2,1)S(1)} %codes_q3_s3.1), channel_id=1, source_target_pairs={{0,96},{1,9},{2,98},{3,11},{4,100},{5,13},{6,102},{7,15},{8,104},{... | collective-permute-start | bytes 626696 | tf_op jit(solution)/shard_map/ppermute | solution.py:374
  69.6 4.2 %collective-permute-done.11.refs_1_.refs_7_ = bf16[2,256,384]{2,1,0:T(8,128)(2,1)S(1)} collective-permute-done((bf16[2,256,384]{2,1,0:T(8,128)(2,1)S(1)}, bf16[2,256,384]{2,1,0:T(8,128)(2,1)S(1)}, u32[]{:S(2)}, u32[]{:S(2)}) %collective-permute-start.11) | collective-permute-done | bytes 393248 | tf_op jit(solution)/shard_map/ppermute | solution.py:374
  73.8 0.3 codes_q2_s3.1
  74.1 0.2 collective-permute-start.12
  74.4 0.0 collective-permute-done.8.refs_1_.refs_4_
  74.4 0.3 codes_q1_s3.1
  74.7 0.6 collective-permute-start.9
  75.2 0.0 collective-permute-done.5.refs_1_
  75.2 0.3 codes_q0_s3.1
  75.5 3.9 %collective-permute-start.6 = (bf16[1,240,384]{2,1,0:T(8,128)(2,1)S(1)}, bf16[1,240,384]{2,1,0:T(8,128)(2,1)S(1)}, u32[]{:S(2)}, u32[]{:S(2)}) collective-permute-start(bf16[1,240,384]{2,1,0:T(8,128)(2,1)S(1)} %codes_q0_s3.1), channel_id=1, source_target_pairs={{0,24},{1,97},{2,26},{3,99},{4,28},{5,101},{6,30},{7,103},{8,16},{... | collective-permute-start | bytes 552968 | tf_op jit(solution)/shard_map/ppermute | solution.py:374
  79.4 0.4 collective-permute-done.12.refs_8_
  79.9 0.6 collective-permute-done.9.refs_5_
  80.4 0.0 collective-permute-done.15.refs_11_
  80.4 1.7 %gather.1 = (bf16[784,384]{1,0:T(8,128)(2,1)S(1)}, bf16[784,384]{1,0:T(8,128)(2,1)S(1)}, f32[384,768]{1,0:T(8,128)S(1)}) custom-call(f32[4,256,384]{2,1,0:T(8,128)S(1)} %get-tuple-element.33.base_ref.refs_0_, f32[4,256,384]{2,1,0:T(8,128)S(1)} %get-tuple-element.34.base_ref.refs_1_, f32[4,272,384]{2,1,0:T(8,128)S(1)} %get-tuple-element.35.base_ref.refs_2_, ...), custom_call_target="tpu_custom_call" | custom-call | flops 462422016 | bytes 4816896 | tf_op jit(solution)/shard_map/gather/pallas_call | solution.py:304
  82.2 0.8 collective-permute-done.6.refs_2_
  82.9 11.2 %newton_schulz.1 = bf16[1024,384]{1,0:T(8,128)(2,1)S(1)} custom-call(f32[4,240,384]{2,1,0:T(8,128)S(1)} %get-tuple-element.32.base_ref.kept_ref, bf16[4,240,384]{2,1,0:T(8,128)(2,1)S(1)} %collective-permute-done.4.refs_0_, bf16[2,240,384]{2,1,0:T(8,128)(2,1)S(1)} %collective-permute-done.5.refs_1_, bf16[1,240,384]{2,1,0:T(8,128)(2,1)S(1)} %collective-permute-done.6.refs_2_, ...), custom_call_target="tpu_custom_call" | custom-call | flops 6681526272 | bytes 6291456 | tf_op jit(solution)/shard_map/newton_schulz/pallas_call | solution.py:356
  94.1 17.4 %all_to_all.5 = bf16[16,64,384]{2,1,0:T(8,128)(2,1)S(1)} all-to-all(bf16[16,64,384]{2,1,0:T(8,128)(2,1)S(1)} %bitcast.2), channel_id=1, replica_groups=mesh['rep'=16,'exp'=8] {'rep'}, dimensions={0} | all-to-all | bytes 1572864 | tf_op jit(solution)/shard_map/all_to_all | solution.py:388
  111.5 0.9 copy.4
Async XLA Ops:
  0.0 2.1 %copy-start = (bf16[16,64,384]{2,1,0:T(8,128)(2,1)S(1)}, bf16[16,64,384]{2,1,0:T(8,128)(2,1)}, u32[]{:S(2)}) copy-start(bf16[16,64,384]{2,1,0:T(8,128)(2,1)} %momentum_ref.9) | copy-start | bytes 2359300
  4.0 30.5 %collective-permute-start.3 = (bf16[8,272,384]{2,1,0:T(8,128)(2,1)S(1)}, bf16[8,272,384]{2,1,0:T(8,128)(2,1)S(1)}, u32[]{:S(2)}, u32[]{:S(2)}) collective-permute-start(bf16[8,272,384]{2,1,0:T(8,128)(2,1)S(1)} %get-tuple-element.27.refs_3_), channel_id=1, source_target_pairs={{0,8},{1,33},{2,10},{3,35},{4,12},{5,37},{6,14},{7,39},{8,0},{9,41... | collective-permute-start | bytes 5013512 | tf_op jit(solution)/shard_map/ppermute | solution.py:374
  7.6 33.6 %collective-permute-start.2 = (bf16[8,256,384]{2,1,0:T(8,128)(2,1)S(1)}, bf16[8,256,384]{2,1,0:T(8,128)(2,1)S(1)}, u32[]{:S(2)}, u32[]{:S(2)}) collective-permute-start(bf16[8,256,384]{2,1,0:T(8,128)(2,1)S(1)} %get-tuple-element.26.refs_2_), channel_id=1, source_target_pairs={{0,32},{1,25},{2,34},{3,27},{4,36},{5,29},{6,38},{7,31},{8,40},{9,... | collective-permute-start | bytes 4718600 | tf_op jit(solution)/shard_map/ppermute | solution.py:374
  11.1 35.5 %collective-permute-start.1 = (bf16[8,256,384]{2,1,0:T(8,128)(2,1)S(1)}, bf16[8,256,384]{2,1,0:T(8,128)(2,1)S(1)}, u32[]{:S(2)}, u32[]{:S(2)}) collective-permute-start(bf16[8,256,384]{2,1,0:T(8,128)(2,1)S(1)} %get-tuple-element.25.refs_1_), channel_id=1, source_target_pairs={{0,24},{1,97},{2,26},{3,99},{4,28},{5,101},{6,30},{7,103},{8,16},{... | collective-permute-start | bytes 4718600 | tf_op jit(solution)/shard_map/ppermute | solution.py:374
  13.9 35.8 %collective-permute-start = (bf16[8,240,384]{2,1,0:T(8,128)(2,1)S(1)}, bf16[8,240,384]{2,1,0:T(8,128)(2,1)S(1)}, u32[]{:S(2)}, u32[]{:S(2)}) collective-permute-start(bf16[8,240,384]{2,1,0:T(8,128)(2,1)S(1)} %first_q0.1.refs_0_), channel_id=1, source_target_pairs={{0,96},{1,9},{2,98},{3,11},{4,100},{5,13},{6,102},{7,15},{8,104},{... | collective-permute-start | bytes 4423688 | tf_op jit(solution)/shard_map/ppermute | solution.py:374
  35.3 17.8 %collective-permute-start.13 = (bf16[4,272,384]{2,1,0:T(8,128)(2,1)S(1)}, bf16[4,272,384]{2,1,0:T(8,128)(2,1)S(1)}, u32[]{:S(2)}, u32[]{:S(2)}) collective-permute-start(bf16[4,272,384]{2,1,0:T(8,128)(2,1)S(1)} %codes_q3_s1.1), channel_id=1, source_target_pairs={{0,32},{1,25},{2,34},{3,27},{4,36},{5,29},{6,38},{7,31},{8,40},{9,... | collective-permute-start | bytes 2506760 | tf_op jit(solution)/shard_map/ppermute | solution.py:374
  42.0 20.2 %collective-permute-start.10 = (bf16[4,256,384]{2,1,0:T(8,128)(2,1)S(1)}, bf16[4,256,384]{2,1,0:T(8,128)(2,1)S(1)}, u32[]{:S(2)}, u32[]{:S(2)}) collective-permute-start(bf16[4,256,384]{2,1,0:T(8,128)(2,1)S(1)} %codes_q2_s1.1), channel_id=1, source_target_pairs={{0,24},{1,97},{2,26},{3,99},{4,28},{5,101},{6,30},{7,103},{8,16},{... | collective-permute-start | bytes 2359304 | tf_op jit(solution)/shard_map/ppermute | solution.py:374
  47.4 17.7 %collective-permute-start.7 = (bf16[4,256,384]{2,1,0:T(8,128)(2,1)S(1)}, bf16[4,256,384]{2,1,0:T(8,128)(2,1)S(1)}, u32[]{:S(2)}, u32[]{:S(2)}) collective-permute-start(bf16[4,256,384]{2,1,0:T(8,128)(2,1)S(1)} %codes_q1_s1.1), channel_id=1, source_target_pairs={{0,96},{1,9},{2,98},{3,11},{4,100},{5,13},{6,102},{7,15},{8,104},{... | collective-permute-start | bytes 2359304 | tf_op jit(solution)/shard_map/ppermute | solution.py:374
  50.4 16.0 %collective-permute-start.4 = (bf16[4,240,384]{2,1,0:T(8,128)(2,1)S(1)}, bf16[4,240,384]{2,1,0:T(8,128)(2,1)S(1)}, u32[]{:S(2)}, u32[]{:S(2)}) collective-permute-start(bf16[4,240,384]{2,1,0:T(8,128)(2,1)S(1)} %codes_q0_s1.1.refs_8_), channel_id=1, source_target_pairs={{0,8},{1,33},{2,10},{3,35},{4,12},{5,37},{6,14},{7,39},{8,0},{9,41... | collective-permute-start | bytes 2211848 | tf_op jit(solution)/shard_map/ppermute | solution.py:374
  53.6 13.3 %collective-permute-start.14 = (bf16[2,272,384]{2,1,0:T(8,128)(2,1)S(1)}, bf16[2,272,384]{2,1,0:T(8,128)(2,1)S(1)}, u32[]{:S(2)}, u32[]{:S(2)}) collective-permute-start(bf16[2,272,384]{2,1,0:T(8,128)(2,1)S(1)} %codes_q3_s2.1), channel_id=1, source_target_pairs={{0,24},{1,97},{2,26},{3,99},{4,28},{5,101},{6,30},{7,103},{8,16},{... | collective-permute-start | bytes 1253384 | tf_op jit(solution)/shard_map/ppermute | solution.py:374
  62.6 11.2 %collective-permute-start.11 = (bf16[2,256,384]{2,1,0:T(8,128)(2,1)S(1)}, bf16[2,256,384]{2,1,0:T(8,128)(2,1)S(1)}, u32[]{:S(2)}, u32[]{:S(2)}) collective-permute-start(bf16[2,256,384]{2,1,0:T(8,128)(2,1)S(1)} %codes_q2_s2.1), channel_id=1, source_target_pairs={{0,96},{1,9},{2,98},{3,11},{4,100},{5,13},{6,102},{7,15},{8,104},{... | collective-permute-start | bytes 1179656 | tf_op jit(solution)/shard_map/ppermute | solution.py:374
  65.5 8.9 %collective-permute-start.8 = (bf16[2,256,384]{2,1,0:T(8,128)(2,1)S(1)}, bf16[2,256,384]{2,1,0:T(8,128)(2,1)S(1)}, u32[]{:S(2)}, u32[]{:S(2)}) collective-permute-start(bf16[2,256,384]{2,1,0:T(8,128)(2,1)S(1)} %codes_q1_s2.1), channel_id=1, source_target_pairs={{0,8},{1,33},{2,10},{3,35},{4,12},{5,37},{6,14},{7,39},{8,0},{9,41... | collective-permute-start | bytes 1179656 | tf_op jit(solution)/shard_map/ppermute | solution.py:374
  66.8 8.5 %collective-permute-start.5 = (bf16[2,240,384]{2,1,0:T(8,128)(2,1)S(1)}, bf16[2,240,384]{2,1,0:T(8,128)(2,1)S(1)}, u32[]{:S(2)}, u32[]{:S(2)}) collective-permute-start(bf16[2,240,384]{2,1,0:T(8,128)(2,1)S(1)} %codes_q0_s2.1), channel_id=1, source_target_pairs={{0,32},{1,25},{2,34},{3,27},{4,36},{5,29},{6,38},{7,31},{8,40},{9,... | collective-permute-start | bytes 1105928 | tf_op jit(solution)/shard_map/ppermute | solution.py:374
  67.2 13.2 %collective-permute-start.15 = (bf16[1,272,384]{2,1,0:T(8,128)(2,1)S(1)}, bf16[1,272,384]{2,1,0:T(8,128)(2,1)S(1)}, u32[]{:S(2)}, u32[]{:S(2)}) collective-permute-start(bf16[1,272,384]{2,1,0:T(8,128)(2,1)S(1)} %codes_q3_s3.1), channel_id=1, source_target_pairs={{0,96},{1,9},{2,98},{3,11},{4,100},{5,13},{6,102},{7,15},{8,104},{... | collective-permute-start | bytes 626696 | tf_op jit(solution)/shard_map/ppermute | solution.py:374
  74.1 5.7 %collective-permute-start.12 = (bf16[1,256,384]{2,1,0:T(8,128)(2,1)S(1)}, bf16[1,256,384]{2,1,0:T(8,128)(2,1)S(1)}, u32[]{:S(2)}, u32[]{:S(2)}) collective-permute-start(bf16[1,256,384]{2,1,0:T(8,128)(2,1)S(1)} %codes_q2_s3.1), channel_id=1, source_target_pairs={{0,8},{1,33},{2,10},{3,35},{4,12},{5,37},{6,14},{7,39},{8,0},{9,41... | collective-permute-start | bytes 589832 | tf_op jit(solution)/shard_map/ppermute | solution.py:374
  74.7 5.7 %collective-permute-start.9 = (bf16[1,256,384]{2,1,0:T(8,128)(2,1)S(1)}, bf16[1,256,384]{2,1,0:T(8,128)(2,1)S(1)}, u32[]{:S(2)}, u32[]{:S(2)}) collective-permute-start(bf16[1,256,384]{2,1,0:T(8,128)(2,1)S(1)} %codes_q1_s3.1), channel_id=1, source_target_pairs={{0,32},{1,25},{2,34},{3,27},{4,36},{5,29},{6,38},{7,31},{8,40},{9,... | collective-permute-start | bytes 589832 | tf_op jit(solution)/shard_map/ppermute | solution.py:374
  75.5 7.4 %collective-permute-start.6 = (bf16[1,240,384]{2,1,0:T(8,128)(2,1)S(1)}, bf16[1,240,384]{2,1,0:T(8,128)(2,1)S(1)}, u32[]{:S(2)}, u32[]{:S(2)}) collective-permute-start(bf16[1,240,384]{2,1,0:T(8,128)(2,1)S(1)} %codes_q0_s3.1), channel_id=1, source_target_pairs={{0,24},{1,97},{2,26},{3,99},{4,28},{5,101},{6,30},{7,103},{8,16},{... | collective-permute-start | bytes 552968 | tf_op jit(solution)/shard_map/ppermute | solution.py:374

commit v5 on v4

--- a/solution.py
+++ b/solution.py
@@ -13,7 +13,7 @@
 NS_ITERS = 5
 ROWS = (240, 256, 256, 272)
 FIRST = (784, 528, 272, 0)
-PIECE = 16
+PIECES = ((0, 16), (16, 48))
 STRIP = 64
 BAND = 64
 SPLIT = 256
@@ -74,12 +74,12 @@
 
     @pl.when((band_low < low + count) & (band_low + BAND > low))
     def _():
-        for start in range(0, BAND, PIECE):
+        for start, size in PIECES:
             row = band_low + start - low
 
             @pl.when((row >= 0) & (row < count))
-            def _(start=start, row=row):
-                body(pl.ds(pl.multiple_of(row, PIECE), PIECE), pl.ds(start, PIECE))
+            def _(start=start, size=size, row=row):
+                body(pl.ds(pl.multiple_of(row, 16), size), pl.ds(start, size))
 
 
 def strips(count):
@@ -287,7 +287,7 @@
         high = high_ref[rows]
         more = dot(high.T, jnp.concatenate([high, low_ref[rows]], axis=1))
         part = more if part is None else part + more
-    return part
+    return part[:, :FF] + (part[:, FF:] + part[:, FF:].T)
 
 
 def gather_kernel(*refs):
@@ -305,7 +305,7 @@
         gather_kernel,
         in_specs=[whole] * (len(kept) + len(received)),
         out_specs=[whole] * 3,
-        out_shape=[split, split, jax.ShapeDtypeStruct((FF, 2 * FF), jnp.float32)],
+        out_shape=[split, split, jax.ShapeDtypeStruct((FF, FF), jnp.float32)],
         compiler_params=pltpu.CompilerParams(vmem_limit_bytes=16 * 1024 * 1024),
         cost_estimate=pl.CostEstimate(
             flops=4 * rows * FF * FF, bytes_accessed=16 * rows * FF, transcendentals=8 * rows * FF
@@ -320,8 +320,7 @@
     high_ref[pl.ds(0, over)] = early_high[pl.ds(FIRST[0] - over, over)]
     low_ref[pl.ds(0, over)] = early_low[pl.ds(FIRST[0] - over, over)]
     split_sums(kept_ref, received, high_ref, low_ref, over)
-    part = part_ref[...] + gram_part(high_ref, low_ref)
-    gram = part[:, :FF] + (part[:, FF:] + part[:, FF:].T)
+    gram = part_ref[...] + gram_part(high_ref, low_ref)
 
     row = lax.broadcasted_iota(jnp.int32, (FF, FF), 0)
     column = lax.broadcasted_iota(jnp.int32, (FF, FF), 1)

time: 113 us -> 113 us (level)
  no operation moved by 1% of the time
where the time goes in v5:
time: 113 us; the launch traced here: 112 us
  Pallas kernels  34.1 us (30%)
  waiting for transfers between devices  31.2 us (28%)
  starting transfers between devices  28.5 us (25%)
  blocking collectives  17.4 us (15%)
    ppermute x16, waiting for transfers between devices, send(): lax.ppermute(codes[quarter], ('rep', 'exp'), partners(quarter, step))  31.2 us
    ppermute x16, starting transfers between devices, send(): lax.ppermute(codes[quarter], ('rep', 'exp'), partners(quarter, step))  28.5 us
    all_to_all x1, blocking collectives, local(): lax.all_to_all(update.reshape(16, BAND, FF), 'rep', split_axis=0, concat_...  17.4 us
    pallas_call x1, Pallas kernels, iterate_call(): pl.pallas_call(iterate_kernel, in_specs=[whole] * (1 + len(received) + le...  11.2 us
    pallas_call x4, Pallas kernels, first_calls(): pl.pallas_call(functools.partial(first_kernel, quarter), in_specs=[hbm, w...  6.26 us
    pallas_call x12, Pallas kernels, step_call(): pl.pallas_call(functools.partial(step_kernel, count), in_specs=[whole] *...  5.77 us
    pallas_call x1, Pallas kernels, keep_call(): pl.pallas_call(keep_kernel, in_specs=[pl.BlockSpec(memory_space=pltpu.HBM...  4.95 us
  transfers between devices with their start and end apart: 16, of which 11 were waited for; matrix products, arithmetic and copies ran while one was open for 0% of the time, Pallas kernels for 17%

profile of v5, /device:TPU:0, one launch (start us, length us, event | category | flops | bytes accessed | tf_op | source)
XLA Modules:
  0.0 112.4 jit_solution(10914764051973250618)
XLA Ops:
  0.0 0.0 copy-start
  0.0 2.0 %fetch.1.held_ref = f32[8,272,384]{2,1,0:T(8,128)S(1)} custom-call(f32[16,1024,384]{2,1,0:T(8,128)} %bitcast.3), custom_call_target="tpu_custom_call" | custom-call | bytes 6684672 | tf_op jit(solution)/shard_map/fetch/pallas_call | solution.py:129
  2.0 0.1 copy-done
  2.1 1.9 %first_q3.1 = (bf16[8,272,384]{2,1,0:T(8,128)(2,1)S(1)}, f32[8,256,384]{2,1,0:T(8,128)S(1)}) custom-call(f32[16,1024,384]{2,1,0:T(8,128)} %bitcast.4, bf16[16,64,384]{2,1,0:T(8,128)(2,1)S(1)} %copy-done, f32[8,272,384]{2,1,0:T(8,128)S(1)} %fetch.1.held_ref), custom_call_target="tpu_custom_call" | custom-call | flops 8355840 | bytes 5013504 | tf_op jit(solution)/shard_map/first_q3/pallas_call | solution.py:143
  4.0 1.7 %collective-permute-start.3 = (bf16[8,272,384]{2,1,0:T(8,128)(2,1)S(1)}, bf16[8,272,384]{2,1,0:T(8,128)(2,1)S(1)}, u32[]{:S(2)}, u32[]{:S(2)}) collective-permute-start(bf16[8,272,384]{2,1,0:T(8,128)(2,1)S(1)} %get-tuple-element.27.refs_3_), channel_id=1, source_target_pairs={{0,8},{1,33},{2,10},{3,35},{4,12},{5,37},{6,14},{7,39},{8,0},{9,41... | collective-permute-start | bytes 5013512 | tf_op jit(solution)/shard_map/ppermute | solution.py:373
  5.7 1.9 %first_q2.1 = (bf16[8,256,384]{2,1,0:T(8,128)(2,1)S(1)}, f32[8,256,384]{2,1,0:T(8,128)S(1)}) custom-call(f32[16,1024,384]{2,1,0:T(8,128)} %bitcast.5, bf16[16,64,384]{2,1,0:T(8,128)(2,1)S(1)} %copy-done, f32[8,256,384]{2,1,0:T(8,128)S(1)} %get-tuple-element.22.held_ref), custom_call_target="tpu_custom_call" | custom-call | flops 7864320 | bytes 4718592 | tf_op jit(solution)/shard_map/first_q2/pallas_call | solution.py:143
  7.6 1.7 %collective-permute-start.2 = (bf16[8,256,384]{2,1,0:T(8,128)(2,1)S(1)}, bf16[8,256,384]{2,1,0:T(8,128)(2,1)S(1)}, u32[]{:S(2)}, u32[]{:S(2)}) collective-permute-start(bf16[8,256,384]{2,1,0:T(8,128)(2,1)S(1)} %get-tuple-element.26.refs_2_), channel_id=1, source_target_pairs={{0,32},{1,25},{2,34},{3,27},{4,36},{5,29},{6,38},{7,31},{8,40},{9,... | collective-permute-start | bytes 4718600 | tf_op jit(solution)/shard_map/ppermute | solution.py:373
  9.3 1.8 %first_q1.1 = (bf16[8,256,384]{2,1,0:T(8,128)(2,1)S(1)}, f32[8,240,384]{2,1,0:T(8,128)S(1)}) custom-call(f32[16,1024,384]{2,1,0:T(8,128)} %bitcast.6, bf16[16,64,384]{2,1,0:T(8,128)(2,1)S(1)} %copy-done, f32[8,256,384]{2,1,0:T(8,128)S(1)} %get-tuple-element.23.held_ref), custom_call_target="tpu_custom_call" | custom-call | flops 7864320 | bytes 4718592 | tf_op jit(solution)/shard_map/first_q1/pallas_call | solution.py:143
  11.1 2.2 %collective-permute-start.1 = (bf16[8,256,384]{2,1,0:T(8,128)(2,1)S(1)}, bf16[8,256,384]{2,1,0:T(8,128)(2,1)S(1)}, u32[]{:S(2)}, u32[]{:S(2)}) collective-permute-start(bf16[8,256,384]{2,1,0:T(8,128)(2,1)S(1)} %get-tuple-element.25.refs_1_), channel_id=1, source_target_pairs={{0,24},{1,97},{2,26},{3,99},{4,28},{5,101},{6,30},{7,103},{8,16},{... | collective-permute-start | bytes 4718600 | tf_op jit(solution)/shard_map/ppermute | solution.py:373
  13.3 0.6 first_q0.1.refs_0_
  13.9 2.6 %collective-permute-start = (bf16[8,240,384]{2,1,0:T(8,128)(2,1)S(1)}, bf16[8,240,384]{2,1,0:T(8,128)(2,1)S(1)}, u32[]{:S(2)}, u32[]{:S(2)}) collective-permute-start(bf16[8,240,384]{2,1,0:T(8,128)(2,1)S(1)} %first_q0.1.refs_0_), channel_id=1, source_target_pairs={{0,96},{1,9},{2,98},{3,11},{4,100},{5,13},{6,102},{7,15},{8,104},{... | collective-permute-start | bytes 4423688 | tf_op jit(solution)/shard_map/ppermute | solution.py:373
  16.5 5.0 %keep.1 = (f32[8,240,384]{2,1,0:T(8,128)S(1)}, f32[8,256,384]{2,1,0:T(8,128)S(1)}, f32[8,256,384]{2,1,0:T(8,128)S(1)}, f32[8,272,384]{2,1,0:T(8,128)S(1)}) custom-call(f32[16,1024,384]{2,1,0:T(8,128)} %bitcast.8, bf16[16,64,384]{2,1,0:T(8,128)(2,1)S(1)} %copy-done, bf16[8,240,384]{2,1,0:T(8,128)(2,1)S(1)} %first_q0.1.refs_0_, ...), custom_call_target="tpu_custom_call" | custom-call | flops 3145728 | bytes 25165824 | tf_op jit(solution)/shard_map/keep/pallas_call | solution.py:184
  21.5 13.1 %collective-permute-done.3.refs_7_.refs_0_ = bf16[8,272,384]{2,1,0:T(8,128)(2,1)S(1)} collective-permute-done((bf16[8,272,384]{2,1,0:T(8,128)(2,1)S(1)}, bf16[8,272,384]{2,1,0:T(8,128)(2,1)S(1)}, u32[]{:S(2)}, u32[]{:S(2)}) %collective-permute-start.3) | collective-permute-done | bytes 1671200 | tf_op jit(solution)/shard_map/ppermute | solution.py:373
  34.6 0.8 codes_q3_s1.1
  35.4 2.5 %collective-permute-start.13 = (bf16[4,272,384]{2,1,0:T(8,128)(2,1)S(1)}, bf16[4,272,384]{2,1,0:T(8,128)(2,1)S(1)}, u32[]{:S(2)}, u32[]{:S(2)}) collective-permute-start(bf16[4,272,384]{2,1,0:T(8,128)(2,1)S(1)} %codes_q3_s1.1), channel_id=1, source_target_pairs={{0,32},{1,25},{2,34},{3,27},{4,36},{5,29},{6,38},{7,31},{8,40},{9,... | collective-permute-start | bytes 2506760 | tf_op jit(solution)/shard_map/ppermute | solution.py:373
  37.9 3.3 %collective-permute-done.2.refs_6_.refs_0_ = bf16[8,256,384]{2,1,0:T(8,128)(2,1)S(1)} collective-permute-done((bf16[8,256,384]{2,1,0:T(8,128)(2,1)S(1)}, bf16[8,256,384]{2,1,0:T(8,128)(2,1)S(1)}, u32[]{:S(2)}, u32[]{:S(2)}) %collective-permute-start.2) | collective-permute-done | bytes 1572896 | tf_op jit(solution)/shard_map/ppermute | solution.py:373
  41.2 0.8 codes_q2_s1.1
  42.0 3.0 %collective-permute-start.10 = (bf16[4,256,384]{2,1,0:T(8,128)(2,1)S(1)}, bf16[4,256,384]{2,1,0:T(8,128)(2,1)S(1)}, u32[]{:S(2)}, u32[]{:S(2)}) collective-permute-start(bf16[4,256,384]{2,1,0:T(8,128)(2,1)S(1)} %codes_q2_s1.1), channel_id=1, source_target_pairs={{0,24},{1,97},{2,26},{3,99},{4,28},{5,101},{6,30},{7,103},{8,16},{... | collective-permute-start | bytes 2359304 | tf_op jit(solution)/shard_map/ppermute | solution.py:373
  45.0 1.6 %collective-permute-done.1.refs_5_.refs_0_ = bf16[8,256,384]{2,1,0:T(8,128)(2,1)S(1)} collective-permute-done((bf16[8,256,384]{2,1,0:T(8,128)(2,1)S(1)}, bf16[8,256,384]{2,1,0:T(8,128)(2,1)S(1)}, u32[]{:S(2)}, u32[]{:S(2)}) %collective-permute-start.1) | collective-permute-done | bytes 1572896 | tf_op jit(solution)/shard_map/ppermute | solution.py:373
  46.6 0.8 codes_q1_s1.1
  47.4 1.5 %collective-permute-start.7 = (bf16[4,256,384]{2,1,0:T(8,128)(2,1)S(1)}, bf16[4,256,384]{2,1,0:T(8,128)(2,1)S(1)}, u32[]{:S(2)}, u32[]{:S(2)}) collective-permute-start(bf16[4,256,384]{2,1,0:T(8,128)(2,1)S(1)} %codes_q1_s1.1), channel_id=1, source_target_pairs={{0,96},{1,9},{2,98},{3,11},{4,100},{5,13},{6,102},{7,15},{8,104},{... | collective-permute-start | bytes 2359304 | tf_op jit(solution)/shard_map/ppermute | solution.py:373
  48.9 0.9 collective-permute-done.refs_0_.refs_4_
  49.7 0.7 codes_q0_s1.1.refs_8_
  50.4 0.7 collective-permute-start.4
  51.1 2.1 %fold.1 = (f32[4,240,384]{2,1,0:T(8,128)S(1)}, f32[4,256,384]{2,1,0:T(8,128)S(1)}, f32[4,256,384]{2,1,0:T(8,128)S(1)}, f32[4,272,384]{2,1,0:T(8,128)S(1)}) custom-call(f32[8,240,384]{2,1,0:T(8,128)S(1)} %get-tuple-element.28.base_ref.refs_0_, f32[8,256,384]{2,1,0:T(8,128)S(1)} %get-tuple-element.29.refs_1_.base_ref, ...), custom_call_target="tpu_custom_call" | custom-call | flops 12582912 | bytes 15728640 | tf_op jit(solution)/shard_map/fold/pallas_call | solution.py:209
  53.2 0.0 collective-permute-done.13.refs_0_.refs_9_
  53.2 0.4 codes_q3_s2.1
  53.6 3.0 %collective-permute-start.14 = (bf16[2,272,384]{2,1,0:T(8,128)(2,1)S(1)}, bf16[2,272,384]{2,1,0:T(8,128)(2,1)S(1)}, u32[]{:S(2)}, u32[]{:S(2)}) collective-permute-start(bf16[2,272,384]{2,1,0:T(8,128)(2,1)S(1)} %codes_q3_s2.1), channel_id=1, source_target_pairs={{0,24},{1,97},{2,26},{3,99},{4,28},{5,101},{6,30},{7,103},{8,16},{... | collective-permute-start | bytes 1253384 | tf_op jit(solution)/shard_map/ppermute | solution.py:373
  56.6 5.6 %collective-permute-done.10.refs_0_.refs_6_ = bf16[4,256,384]{2,1,0:T(8,128)(2,1)S(1)} collective-permute-done((bf16[4,256,384]{2,1,0:T(8,128)(2,1)S(1)}, bf16[4,256,384]{2,1,0:T(8,128)(2,1)S(1)}, u32[]{:S(2)}, u32[]{:S(2)}) %collective-permute-start.10) | collective-permute-done | bytes 786464 | tf_op jit(solution)/shard_map/ppermute | solution.py:373
  62.2 0.4 codes_q2_s2.1
  62.6 2.2 %collective-permute-start.11 = (bf16[2,256,384]{2,1,0:T(8,128)(2,1)S(1)}, bf16[2,256,384]{2,1,0:T(8,128)(2,1)S(1)}, u32[]{:S(2)}, u32[]{:S(2)}) collective-permute-start(bf16[2,256,384]{2,1,0:T(8,128)(2,1)S(1)} %codes_q2_s2.1), channel_id=1, source_target_pairs={{0,96},{1,9},{2,98},{3,11},{4,100},{5,13},{6,102},{7,15},{8,104},{... | collective-permute-start | bytes 1179656 | tf_op jit(solution)/shard_map/ppermute | solution.py:373
  64.9 0.2 collective-permute-done.7.refs_0_.refs_3_
  65.1 0.4 codes_q1_s2.1
  65.5 0.3 collective-permute-start.8
  65.8 0.7 collective-permute-done.4.refs_0_
  66.5 0.4 codes_q0_s2.1
  66.9 0.1 collective-permute-start.5
  66.9 0.0 collective-permute-done.14.refs_1_.refs_10_
  67.0 0.3 codes_q3_s3.1
  67.3 2.3 %collective-permute-start.15 = (bf16[1,272,384]{2,1,0:T(8,128)(2,1)S(1)}, bf16[1,272,384]{2,1,0:T(8,128)(2,1)S(1)}, u32[]{:S(2)}, u32[]{:S(2)}) collective-permute-start(bf16[1,272,384]{2,1,0:T(8,128)(2,1)S(1)} %codes_q3_s3.1), channel_id=1, source_target_pairs={{0,96},{1,9},{2,98},{3,11},{4,100},{5,13},{6,102},{7,15},{8,104},{... | collective-permute-start | bytes 626696 | tf_op jit(solution)/shard_map/ppermute | solution.py:373
  69.6 4.2 %collective-permute-done.11.refs_1_.refs_7_ = bf16[2,256,384]{2,1,0:T(8,128)(2,1)S(1)} collective-permute-done((bf16[2,256,384]{2,1,0:T(8,128)(2,1)S(1)}, bf16[2,256,384]{2,1,0:T(8,128)(2,1)S(1)}, u32[]{:S(2)}, u32[]{:S(2)}) %collective-permute-start.11) | collective-permute-done | bytes 393248 | tf_op jit(solution)/shard_map/ppermute | solution.py:373
  73.8 0.3 codes_q2_s3.1
  74.1 0.2 collective-permute-start.12
  74.4 0.0 collective-permute-done.8.refs_1_.refs_4_
  74.4 0.3 codes_q1_s3.1
  74.7 0.6 collective-permute-start.9
  75.2 0.0 collective-permute-done.5.refs_1_
  75.2 0.3 codes_q0_s3.1
  75.5 3.9 %collective-permute-start.6 = (bf16[1,240,384]{2,1,0:T(8,128)(2,1)S(1)}, bf16[1,240,384]{2,1,0:T(8,128)(2,1)S(1)}, u32[]{:S(2)}, u32[]{:S(2)}) collective-permute-start(bf16[1,240,384]{2,1,0:T(8,128)(2,1)S(1)} %codes_q0_s3.1), channel_id=1, source_target_pairs={{0,24},{1,97},{2,26},{3,99},{4,28},{5,101},{6,30},{7,103},{8,16},{... | collective-permute-start | bytes 552968 | tf_op jit(solution)/shard_map/ppermute | solution.py:373
  79.4 0.4 collective-permute-done.12.refs_8_
  79.9 0.6 collective-permute-done.9.refs_5_
  80.4 0.0 collective-permute-done.15.refs_11_
  80.4 1.9 %gather.1 = (bf16[784,384]{1,0:T(8,128)(2,1)S(1)}, bf16[784,384]{1,0:T(8,128)(2,1)S(1)}, f32[384,384]{1,0:T(8,128)S(1)}) custom-call(f32[4,256,384]{2,1,0:T(8,128)S(1)} %get-tuple-element.33.base_ref.refs_0_, f32[4,256,384]{2,1,0:T(8,128)S(1)} %get-tuple-element.34.base_ref.refs_1_, f32[4,272,384]{2,1,0:T(8,128)S(1)} %get-tuple-element.35.base_ref.refs_2_, ...), custom_call_target="tpu_custom_call" | custom-call | flops 462422016 | bytes 4816896 | tf_op jit(solution)/shard_map/gather/pallas_call | solution.py:304
  82.3 0.6 collective-permute-done.6.refs_2_
  82.9 11.2 %newton_schulz.1 = bf16[1024,384]{1,0:T(8,128)(2,1)S(1)} custom-call(f32[4,240,384]{2,1,0:T(8,128)S(1)} %get-tuple-element.32.base_ref.kept_ref, bf16[4,240,384]{2,1,0:T(8,128)(2,1)S(1)} %collective-permute-done.4.refs_0_, bf16[2,240,384]{2,1,0:T(8,128)(2,1)S(1)} %collective-permute-done.5.refs_1_, bf16[1,240,384]{2,1,0:T(8,128)(2,1)S(1)} %collective-permute-done.6.refs_2_, ...), custom_call_target="tpu_custom_call" | custom-call | flops 6681526272 | bytes 6291456 | tf_op jit(solution)/shard_map/newton_schulz/pallas_call | solution.py:355
  94.1 17.4 %all_to_all.5 = bf16[16,64,384]{2,1,0:T(8,128)(2,1)S(1)} all-to-all(bf16[16,64,384]{2,1,0:T(8,128)(2,1)S(1)} %bitcast.2), channel_id=1, replica_groups=mesh['rep'=16,'exp'=8] {'rep'}, dimensions={0} | all-to-all | bytes 1572864 | tf_op jit(solution)/shard_map/all_to_all | solution.py:387
  111.5 0.9 copy.4
Async XLA Ops:
  0.0 2.1 %copy-start = (bf16[16,64,384]{2,1,0:T(8,128)(2,1)S(1)}, bf16[16,64,384]{2,1,0:T(8,128)(2,1)}, u32[]{:S(2)}) copy-start(bf16[16,64,384]{2,1,0:T(8,128)(2,1)} %momentum_ref.9) | copy-start | bytes 2359300
  4.0 30.5 %collective-permute-start.3 = (bf16[8,272,384]{2,1,0:T(8,128)(2,1)S(1)}, bf16[8,272,384]{2,1,0:T(8,128)(2,1)S(1)}, u32[]{:S(2)}, u32[]{:S(2)}) collective-permute-start(bf16[8,272,384]{2,1,0:T(8,128)(2,1)S(1)} %get-tuple-element.27.refs_3_), channel_id=1, source_target_pairs={{0,8},{1,33},{2,10},{3,35},{4,12},{5,37},{6,14},{7,39},{8,0},{9,41... | collective-permute-start | bytes 5013512 | tf_op jit(solution)/shard_map/ppermute | solution.py:373
  7.6 33.6 %collective-permute-start.2 = (bf16[8,256,384]{2,1,0:T(8,128)(2,1)S(1)}, bf16[8,256,384]{2,1,0:T(8,128)(2,1)S(1)}, u32[]{:S(2)}, u32[]{:S(2)}) collective-permute-start(bf16[8,256,384]{2,1,0:T(8,128)(2,1)S(1)} %get-tuple-element.26.refs_2_), channel_id=1, source_target_pairs={{0,32},{1,25},{2,34},{3,27},{4,36},{5,29},{6,38},{7,31},{8,40},{9,... | collective-permute-start | bytes 4718600 | tf_op jit(solution)/shard_map/ppermute | solution.py:373
  11.1 35.5 %collective-permute-start.1 = (bf16[8,256,384]{2,1,0:T(8,128)(2,1)S(1)}, bf16[8,256,384]{2,1,0:T(8,128)(2,1)S(1)}, u32[]{:S(2)}, u32[]{:S(2)}) collective-permute-start(bf16[8,256,384]{2,1,0:T(8,128)(2,1)S(1)} %get-tuple-element.25.refs_1_), channel_id=1, source_target_pairs={{0,24},{1,97},{2,26},{3,99},{4,28},{5,101},{6,30},{7,103},{8,16},{... | collective-permute-start | bytes 4718600 | tf_op jit(solution)/shard_map/ppermute | solution.py:373
  13.9 35.8 %collective-permute-start = (bf16[8,240,384]{2,1,0:T(8,128)(2,1)S(1)}, bf16[8,240,384]{2,1,0:T(8,128)(2,1)S(1)}, u32[]{:S(2)}, u32[]{:S(2)}) collective-permute-start(bf16[8,240,384]{2,1,0:T(8,128)(2,1)S(1)} %first_q0.1.refs_0_), channel_id=1, source_target_pairs={{0,96},{1,9},{2,98},{3,11},{4,100},{5,13},{6,102},{7,15},{8,104},{... | collective-permute-start | bytes 4423688 | tf_op jit(solution)/shard_map/ppermute | solution.py:373
  35.4 17.8 %collective-permute-start.13 = (bf16[4,272,384]{2,1,0:T(8,128)(2,1)S(1)}, bf16[4,272,384]{2,1,0:T(8,128)(2,1)S(1)}, u32[]{:S(2)}, u32[]{:S(2)}) collective-permute-start(bf16[4,272,384]{2,1,0:T(8,128)(2,1)S(1)} %codes_q3_s1.1), channel_id=1, source_target_pairs={{0,32},{1,25},{2,34},{3,27},{4,36},{5,29},{6,38},{7,31},{8,40},{9,... | collective-permute-start | bytes 2506760 | tf_op jit(solution)/shard_map/ppermute | solution.py:373
  42.0 20.2 %collective-permute-start.10 = (bf16[4,256,384]{2,1,0:T(8,128)(2,1)S(1)}, bf16[4,256,384]{2,1,0:T(8,128)(2,1)S(1)}, u32[]{:S(2)}, u32[]{:S(2)}) collective-permute-start(bf16[4,256,384]{2,1,0:T(8,128)(2,1)S(1)} %codes_q2_s1.1), channel_id=1, source_target_pairs={{0,24},{1,97},{2,26},{3,99},{4,28},{5,101},{6,30},{7,103},{8,16},{... | collective-permute-start | bytes 2359304 | tf_op jit(solution)/shard_map/ppermute | solution.py:373
  47.4 17.7 %collective-permute-start.7 = (bf16[4,256,384]{2,1,0:T(8,128)(2,1)S(1)}, bf16[4,256,384]{2,1,0:T(8,128)(2,1)S(1)}, u32[]{:S(2)}, u32[]{:S(2)}) collective-permute-start(bf16[4,256,384]{2,1,0:T(8,128)(2,1)S(1)} %codes_q1_s1.1), channel_id=1, source_target_pairs={{0,96},{1,9},{2,98},{3,11},{4,100},{5,13},{6,102},{7,15},{8,104},{... | collective-permute-start | bytes 2359304 | tf_op jit(solution)/shard_map/ppermute | solution.py:373
  50.4 16.1 %collective-permute-start.4 = (bf16[4,240,384]{2,1,0:T(8,128)(2,1)S(1)}, bf16[4,240,384]{2,1,0:T(8,128)(2,1)S(1)}, u32[]{:S(2)}, u32[]{:S(2)}) collective-permute-start(bf16[4,240,384]{2,1,0:T(8,128)(2,1)S(1)} %codes_q0_s1.1.refs_8_), channel_id=1, source_target_pairs={{0,8},{1,33},{2,10},{3,35},{4,12},{5,37},{6,14},{7,39},{8,0},{9,41... | collective-permute-start | bytes 2211848 | tf_op jit(solution)/shard_map/ppermute | solution.py:373
  53.6 13.4 %collective-permute-start.14 = (bf16[2,272,384]{2,1,0:T(8,128)(2,1)S(1)}, bf16[2,272,384]{2,1,0:T(8,128)(2,1)S(1)}, u32[]{:S(2)}, u32[]{:S(2)}) collective-permute-start(bf16[2,272,384]{2,1,0:T(8,128)(2,1)S(1)} %codes_q3_s2.1), channel_id=1, source_target_pairs={{0,24},{1,97},{2,26},{3,99},{4,28},{5,101},{6,30},{7,103},{8,16},{... | collective-permute-start | bytes 1253384 | tf_op jit(solution)/shard_map/ppermute | solution.py:373
  62.6 11.2 %collective-permute-start.11 = (bf16[2,256,384]{2,1,0:T(8,128)(2,1)S(1)}, bf16[2,256,384]{2,1,0:T(8,128)(2,1)S(1)}, u32[]{:S(2)}, u32[]{:S(2)}) collective-permute-start(bf16[2,256,384]{2,1,0:T(8,128)(2,1)S(1)} %codes_q2_s2.1), channel_id=1, source_target_pairs={{0,96},{1,9},{2,98},{3,11},{4,100},{5,13},{6,102},{7,15},{8,104},{... | collective-permute-start | bytes 1179656 | tf_op jit(solution)/shard_map/ppermute | solution.py:373
  65.5 8.9 %collective-permute-start.8 = (bf16[2,256,384]{2,1,0:T(8,128)(2,1)S(1)}, bf16[2,256,384]{2,1,0:T(8,128)(2,1)S(1)}, u32[]{:S(2)}, u32[]{:S(2)}) collective-permute-start(bf16[2,256,384]{2,1,0:T(8,128)(2,1)S(1)} %codes_q1_s2.1), channel_id=1, source_target_pairs={{0,8},{1,33},{2,10},{3,35},{4,12},{5,37},{6,14},{7,39},{8,0},{9,41... | collective-permute-start | bytes 1179656 | tf_op jit(solution)/shard_map/ppermute | solution.py:373
  66.9 8.4 %collective-permute-start.5 = (bf16[2,240,384]{2,1,0:T(8,128)(2,1)S(1)}, bf16[2,240,384]{2,1,0:T(8,128)(2,1)S(1)}, u32[]{:S(2)}, u32[]{:S(2)}) collective-permute-start(bf16[2,240,384]{2,1,0:T(8,128)(2,1)S(1)} %codes_q0_s2.1), channel_id=1, source_target_pairs={{0,32},{1,25},{2,34},{3,27},{4,36},{5,29},{6,38},{7,31},{8,40},{9,... | collective-permute-start | bytes 1105928 | tf_op jit(solution)/shard_map/ppermute | solution.py:373
  67.3 13.1 %collective-permute-start.15 = (bf16[1,272,384]{2,1,0:T(8,128)(2,1)S(1)}, bf16[1,272,384]{2,1,0:T(8,128)(2,1)S(1)}, u32[]{:S(2)}, u32[]{:S(2)}) collective-permute-start(bf16[1,272,384]{2,1,0:T(8,128)(2,1)S(1)} %codes_q3_s3.1), channel_id=1, source_target_pairs={{0,96},{1,9},{2,98},{3,11},{4,100},{5,13},{6,102},{7,15},{8,104},{... | collective-permute-start | bytes 626696 | tf_op jit(solution)/shard_map/ppermute | solution.py:373
  74.1 5.7 %collective-permute-start.12 = (bf16[1,256,384]{2,1,0:T(8,128)(2,1)S(1)}, bf16[1,256,384]{2,1,0:T(8,128)(2,1)S(1)}, u32[]{:S(2)}, u32[]{:S(2)}) collective-permute-start(bf16[1,256,384]{2,1,0:T(8,128)(2,1)S(1)} %codes_q2_s3.1), channel_id=1, source_target_pairs={{0,8},{1,33},{2,10},{3,35},{4,12},{5,37},{6,14},{7,39},{8,0},{9,41... | collective-permute-start | bytes 589832 | tf_op jit(solution)/shard_map/ppermute | solution.py:373
  74.7 5.7 %collective-permute-start.9 = (bf16[1,256,384]{2,1,0:T(8,128)(2,1)S(1)}, bf16[1,256,384]{2,1,0:T(8,128)(2,1)S(1)}, u32[]{:S(2)}, u32[]{:S(2)}) collective-permute-start(bf16[1,256,384]{2,1,0:T(8,128)(2,1)S(1)} %codes_q1_s3.1), channel_id=1, source_target_pairs={{0,32},{1,25},{2,34},{3,27},{4,36},{5,29},{6,38},{7,31},{8,40},{9,... | collective-permute-start | bytes 589832 | tf_op jit(solution)/shard_map/ppermute | solution.py:373
  75.5 7.4 %collective-permute-start.6 = (bf16[1,240,384]{2,1,0:T(8,128)(2,1)S(1)}, bf16[1,240,384]{2,1,0:T(8,128)(2,1)S(1)}, u32[]{:S(2)}, u32[]{:S(2)}) collective-permute-start(bf16[1,240,384]{2,1,0:T(8,128)(2,1)S(1)} %codes_q0_s3.1), channel_id=1, source_target_pairs={{0,24},{1,97},{2,26},{3,99},{4,28},{5,101},{6,30},{7,103},{8,16},{... | collective-permute-start | bytes 552968 | tf_op jit(solution)/shard_map/ppermute | solution.py:373
